TPU v7x, 512 devices: a whole 4x8x8 slice. The times are simulated.
512 devices in a mesh: branch: 2 (over core), dp: 128 (over z_hi, x, y), seq: 2 (over z_lo).
Axes of the slice: x: 4, y: 8, z: 8 (z_hi: 4, z_lo: 2; z = z_hi * 2 + z_lo), core: 2. Of those that a mesh axis runs over, the one named last changes fastest.
Arguments:
- attn: bfloat16 [2, 32768, 2432], P('branch', ('dp', 'seq')), may hold values from -24 to 24
- hidden: bfloat16 [2, 32768, 2432], P('branch', ('dp', 'seq')), may hold values from -6 to 6
- noisy: bfloat16 [32768, 2432], P(('dp', 'seq')), may hold values from -6 to 6
- target: bfloat16 [32768, 2432], P(('dp', 'seq')), may hold values from -6 to 6
- quantized_weight_codes: bfloat16 [2432, 2432], P('dp'), may hold values from -0.0625 to 0.0625
- weight_exponents: int32 [2432, 19], P('dp'), may hold values from -1 to 2
- adapter_down_map: bfloat16 [2432, 128], replicated, may hold values from -0.125 to 0.125
- adapter_up_transposed: bfloat16 [2432, 128], replicated, may hold values from -0.5 to 0.5
- gates: float32 [2, 8, 2432], P('branch'), may hold values from 0.25 to 1.5
- group_prompt: int32 [128], P('dp'), may hold values from 0 to 7
- step_index: int32 [1], replicated, may hold values from 14 to 28
Outputs:
- grad_attn: bfloat16 [2, 32768, 2432], P('branch', ('dp', 'seq'))
- grad_down: float32 [2432, 128], P('dp')
- grad_up_t: float32 [2432, 128], P('dp')
All inputs are finite; a program needn't handle non-finite values.
Results may differ from a plain program's by a relative error of at most 0.01.
Values may be sent and summed in bfloat16 or wider, within the bound.
No kernel may reach another device: no remote copies, remote signals or barrier semaphores. Data moves between devices by JAX's collectives and lax.ppermute only.
A program may use at most 128 MiB of HBM per device.

v0:
```python
import jax
import jax.numpy as jnp
from jax import lax
from jax.sharding import PartitionSpec as P

MODEL_WIDTH = 2432
QBLOCK = 128
STEPS = 28


GUIDE = 4.5
REWARD = 0.08
ADAPTER_STRENGTH = 0.5
SHIFT = 3.0


def from_partner(value, axis, apart):
    mask = 2**apart
    pairs = [(source, source ^ mask) for source in range(lax.axis_size(axis))]
    return lax.ppermute(value, axis, pairs)


def noise_level(step_index):
    frac = step_index[0].astype(jnp.float32) / STEPS
    return SHIFT * frac / (1.0 + (SHIFT - 1.0) * frac)


def dequantize(codes, exps):
    count = codes.shape[0]
    block_scale = jnp.exp2(exps.astype(jnp.float32))
    grouped = (
        codes.astype(jnp.float32).reshape(count, MODEL_WIDTH // QBLOCK, QBLOCK)
        * block_scale[:, :, None]
    )
    return grouped.reshape(count, MODEL_WIDTH).astype(jnp.bfloat16)


def contract_trailing(left, right):
    return lax.dot_general(
        left, right, (((1,), (1,)), ((), ())), preferred_element_type=jnp.float32
    )


def contract_first(left, right):
    return lax.dot_general(
        left, right, (((0,), (0,)), ((), ())), preferred_element_type=jnp.float32
    )


def per_device(
    attn,
    hidden,
    noisy,
    target,
    quantized_weight_codes,
    weight_exponents,
    adapter_down_map,
    adapter_up_transposed,
    gates,
    group_prompt,
    step_index,
):
    local_weight = dequantize(quantized_weight_codes, weight_exponents)
    merged_weight = lax.all_gather(local_weight, "dp", axis=0, tiled=True)
    level = noise_level(step_index)
    attention_rows = attn[0]
    selector = (jnp.arange(gates.shape[1], dtype=jnp.int32) == group_prompt[0]).astype(jnp.float32)
    gate_row = jnp.sum(selector[:, None] * gates[0], axis=0)
    adapter_product = jnp.dot(
        attention_rows, adapter_down_map, preferred_element_type=jnp.float32
    ).astype(jnp.bfloat16)
    projection_output = jnp.dot(
        attention_rows, merged_weight, preferred_element_type=jnp.float32
    ) + ADAPTER_STRENGTH * contract_trailing(adapter_product, adapter_up_transposed)
    velocity = hidden[0].astype(jnp.float32) + gate_row * projection_output
    is_conditional = lax.axis_index("branch") == 0
    branch_coef = jnp.where(is_conditional, jnp.float32(GUIDE), jnp.float32(1.0 - GUIDE))
    partner = from_partner(velocity, "branch", 0)
    conditional = jnp.where(is_conditional, velocity, partner)
    unconditional = jnp.where(is_conditional, partner, velocity)
    guided = unconditional + GUIDE * (conditional - unconditional)
    denoised = noisy.astype(jnp.float32) - level * guided
    reward_grad = REWARD * (target.astype(jnp.float32) - denoised)
    gradient_before = (-level * branch_coef * gate_row * reward_grad).astype(jnp.bfloat16)
    adapter_gradient = jnp.dot(
        gradient_before, adapter_up_transposed, preferred_element_type=jnp.float32
    ).astype(jnp.bfloat16)
    grad_rows = (
        contract_trailing(gradient_before, merged_weight)
        + ADAPTER_STRENGTH * contract_trailing(adapter_gradient, adapter_down_map)
    ).astype(jnp.bfloat16)
    term_down = ADAPTER_STRENGTH * contract_first(attention_rows, adapter_gradient)
    term_up = ADAPTER_STRENGTH * contract_first(gradient_before, adapter_product)
    summed = (
        lax.psum(term_down.astype(jnp.bfloat16), ("branch", "seq")).astype(jnp.float32),
        lax.psum(term_up.astype(jnp.bfloat16), ("branch", "seq")).astype(jnp.float32),
    )
    down_grad, up_grad = (
        lax.psum_scatter(summed[0], "dp", scatter_dimension=0, tiled=True),
        lax.psum_scatter(summed[1], "dp", scatter_dimension=0, tiled=True),
    )
    return (grad_rows[None], down_grad, up_grad)


def solution(mesh):
    return jax.shard_map(
        per_device,
        mesh=mesh,
        in_specs=(
            P("branch", ("dp", "seq"), None),
            P("branch", ("dp", "seq"), None),
            P(("dp", "seq"), None),
            P(("dp", "seq"), None),
            P("dp", None),
            P("dp", None),
            P(),
            P(),
            P("branch", None, None),
            P("dp"),
            P(),
        ),
        out_specs=(P("branch", ("dp", "seq"), None), P("dp", None), P("dp", None)),
        check_vma=False,
    )
```

profile of v0, /device:TPU:64, one launch (start us, length us, event | category | flops | bytes accessed | tf_op | source)
XLA Modules:
  0.0 1112.7 jit_solution(2909447742008898161)
XLA Ops:
  7.2 0.0 copy-start
  7.2 0.0 copy-start.6
  7.2 0.0 copy-start.4
  7.2 0.0 all-gather.3.cloned.1.call-start
  7.2 0.8 multiply_exponential_fusion
  8.1 0.1 mul.83
  8.2 0.0 copy-start.7
  8.2 0.0 copy-start.1
  8.3 0.0 copy-done.6
  8.3 0.7 fusion.12
  9.0 0.0 all-gather.3.cloned.1.call-update
  9.0 0.0 all-reduce.7.cloned.1.call-start
  9.0 0.0 copy-done.4
  9.1 0.3 copy.32
  10.1 0.0 copy-done.7
  10.1 0.1 fusion.13
  10.2 0.0 copy-done
  10.2 0.0 copy-done.1
  10.2 0.3 convolution_convert_fusion.1
  10.5 204.4 %all-gather.3.cloned.1.call-done = bf16[128,19,2432]{2,1,0:T(8,128)(2,1)} async-done(((bf16[1,19,2432]{2,1,0:T(8,128)(2,1)}), bf16[128,19,2432]{2,1,0:T(8,128)(2,1)}) %all-gather.3.cloned.1.call-update) | async-done | bytes 11829264 | tf_op jit(solution)/shard_map/all_gather | solution.py:64
  214.9 16.8 %reshape.31 = bf16[2432,2432]{1,0:T(8,128)(2,1)} reshape(bf16[128,19,2432]{2,1,0:T(8,128)(2,1)} %all-gather.3.cloned.1.call-done) | data formatting | bytes 23658496
  231.7 0.0 copy-start.2
  231.7 6.6 convolution_bitcast_fusion
  238.3 0.0 copy-done.2
  238.3 1.2 fusion.3
  239.5 0.0 copy-start.5
  239.5 2.1 collective-permute-start
  241.6 2.1 copy.31
  243.7 0.0 copy-done.5
  243.7 1.1 copy.30
  245.5 1.3 dynamic-slice
  247.4 0.0 copy-start.3
  247.5 0.0 collective-permute-done
  247.5 2.2 multiply_convert_fusion
  249.7 0.0 copy-done.3
  249.7 0.4 convolution_convert_fusion
  250.1 1.1 fusion.6
  251.2 1.2 fusion.7
  252.4 0.0 all-reduce.7.cloned.1.call-update
  252.4 6.1 fusion.14
  258.6 0.3 fusion.8
  258.9 1.1 copy.37
  260.0 62.7 %all-reduce.7.cloned.1.call-done = (bf16[2432,128]{1,0:T(8,128)(2,1)}, bf16[2432,128]{1,0:T(8,128)(2,1)}) async-done(((bf16[2432,128]{1,0:T(8,128)(2,1)}, bf16[2432,128]{1,0:T(8,128)(2,1)}), (bf16[2432,128]{1,0:T(8,128)(2,1)}, bf16[2432,128]{1,0:T(8,128)(2,1)})) %all-reduce.7.cloned.1.call-update) | async-done | bytes 1245200 | tf_op jit(solution)/shard_map/psum | solution.py:95
  322.6 781.9 %all-reduce.8 = (f32[2432,128]{1,0:T(8,128)S(1)}, f32[2432,128]{1,0:T(8,128)}) all-reduce(bf16[2432,128]{1,0:T(8,128)(2,1)} %get-tuple-element.14, bf16[2432,128]{1,0:T(8,128)(2,1)} %get-tuple-element.15), channel_id=2, replica_groups=mesh['branch'=2,'dp'=128,'seq'=2] {'dp'}, use_global_device_ids=true, to_apply=%region_2.3.clone | all-reduce | flops 622592 | bytes 3735552
  1104.6 1.3 constant_dynamic-slice_fusion
  (4 shorter events, 0.1 us)
Async XLA Ops:
  7.2 3.0 copy-start
  7.2 1.1 copy-start.6
  7.2 1.9 copy-start.4
  7.2 207.7 %all-gather.3.cloned.1.call-start = ((), (), s32[]{:S(2)}) async-start(), calls=%async_computation | async-start | bytes 15058944 | tf_op jit(solution)/shard_map/all_gather | solution.py:64
  8.2 1.8 copy-start.7
  8.2 1.9 copy-start.1
  9.0 313.6 %all-reduce.7.cloned.1.call-start = ((), (), s32[]{:S(2)}) async-start(), calls=%async_computation.1 | async-start | bytes 2490368 | tf_op jit(solution)/shard_map/psum | solution.py:95
  231.7 6.6 copy-start.2
  239.5 4.2 copy-start.5
  239.5 8.0 collective-permute-start
  247.4 2.2 copy-start.3
Sparse Core Ops, SparseCore 0:
  12.9 201.9 all-gather.2
  252.5 70.0 all-reduce.6
where the time goes:
time: 1110 us
  blocking collectives  782 us (70%)
  waiting for transfers between devices  267 us (24%)
  local copies, waits for them, and re-layouts  24.2 us (2%)
  matrix products  17.3 us (2%)
  between operations  16.3 us (1%)
    unnamed x1, blocking collectives  782 us
    all_gather x1, waiting for transfers between devices, per_device(): merged_weight = lax.all_gather(local_weight, 'dp', axis=0, tiled=True)  204 us
    psum x1, waiting for transfers between devices, per_device(): lax.psum(term_down.astype(jnp.bfloat16), ('branch', 'seq'))  62.7 us
    unnamed x25, local copies, waits for them, and re-layouts  24.1 us
  transfers between devices with their start and end apart: 3, of which 2 were waited for; matrix products, arithmetic and copies ran while one was open for 1% of the time, Pallas kernels for 0%

commit v1 on v0

v1 whole, which is shorter than its diff:
```python
import jax
import jax.numpy as jnp
from jax import lax
from jax.sharding import PartitionSpec as P

MODEL_WIDTH = 2432
QBLOCK = 128
RANK = 128
STEPS = 28
ZH, XN, YN = 4, 4, 8
PLANE = XN * YN
SLICE = MODEL_WIDTH // 4
ROWS = 19
TOK = 128

GUIDE = 4.5
REWARD = 0.08
ADAPTER_STRENGTH = 0.5
SHIFT = 3.0
F32 = jnp.float32
BF16 = jnp.bfloat16
EVERY = ("branch", "dp", "seq")


def swap(value, axis):
    return lax.ppermute(value, axis, [(0, 1), (1, 0)])


def noise_level(step_index):
    frac = step_index[0].astype(F32) / STEPS
    return SHIFT * frac / (1.0 + (SHIFT - 1.0) * frac)


def dequantize(codes, exps):
    count = codes.shape[0]
    block_scale = jnp.exp2(exps.astype(F32))
    grouped = (
        codes.astype(F32).reshape(count, MODEL_WIDTH // QBLOCK, QBLOCK)
        * block_scale[:, :, None]
    )
    return grouped.reshape(count, MODEL_WIDTH).astype(BF16)


def dot_nn(left, right):
    return lax.dot_general(left, right, (((1,), (0,)), ((), ())), preferred_element_type=F32)


def dot_nt(left, right):
    return lax.dot_general(left, right, (((1,), (1,)), ((), ())), preferred_element_type=F32)


def dot_tn(left, right):
    return lax.dot_general(left, right, (((0,), (0,)), ((), ())), preferred_element_type=F32)


def dp_index(z, x, y):
    return z * PLANE + x * YN + y


Y_GROUPS = [[dp_index(z, x, y) for y in range(YN)] for z in range(ZH) for x in range(XN)]
X_GROUPS = [[dp_index(z, x, y) for x in range(XN)] for z in range(ZH) for y in range(YN)]
XY_GROUPS = [[z * PLANE + i for i in range(PLANE)] for z in range(ZH)]


def along_z(value, by):
    pairs = [(d, (d + by * PLANE) % (ZH * PLANE)) for d in range(ZH * PLANE)]
    return lax.ppermute(value, "dp", pairs)


def place(branch, dp, seq):
    return (branch * ZH * PLANE + dp) * 2 + seq


def z_transposed(value, flip):
    pairs = []
    for z in range(ZH):
        for i in range(PLANE):
            for q in range(4):
                r = z ^ flip
                pairs.append((place(q // 2, z * PLANE + i, q % 2), place(r // 2, q * PLANE + i, r % 2)))
    return lax.ppermute(value, EVERY, pairs)


def gathered_weight(codes, exps, q, z):
    local = dequantize(codes, exps).reshape(ROWS, 4, SLICE)
    mine = lax.dynamic_index_in_dim(local, q, 1, keepdims=False)
    parts = [along_z(mine, 3), along_z(mine, 2), along_z(mine, 1), mine]
    ring = jnp.stack(parts + parts[:3])
    ordered = lax.dynamic_slice_in_dim(ring, 3 - z, 4, 0)
    lined = lax.all_gather(ordered, "dp", axis=0, axis_index_groups=Y_GROUPS)
    square = lined.transpose(1, 0, 2, 3).reshape(SLICE, SLICE)
    whole = lax.all_gather(square, "dp", axis=0, axis_index_groups=X_GROUPS)
    return whole.reshape(MODEL_WIDTH, SLICE)


def per_device(
    attn,
    hidden,
    noisy,
    target,
    quantized_weight_codes,
    weight_exponents,
    adapter_down_map,
    adapter_up_transposed,
    gates,
    group_prompt,
    step_index,
):
    b = lax.axis_index("branch")
    s = lax.axis_index("seq")
    z = lax.axis_index("dp") // PLANE
    q = 2 * b + s
    weight = gathered_weight(quantized_weight_codes, weight_exponents, q, z)

    level = noise_level(step_index)
    own = attn[0].reshape(TOK, ZH, XN, YN * ROWS).transpose(0, 2, 1, 3).reshape(TOK, MODEL_WIDTH)
    from_seq = swap(own, "seq")
    from_branch = swap(own, "branch")
    from_both = swap(from_seq, "branch")
    rows = jnp.concatenate([own, from_seq, from_branch, from_both], 0)

    is_first = b == 0
    shared = jnp.where(is_first, noisy, target)
    outgoing = jnp.stack([hidden[0], shared]).reshape(2, TOK, 4, SLICE).transpose(2, 0, 1, 3)
    incoming = lax.all_to_all(outgoing, ("branch", "seq"), 0, 0)
    pick = lambda i, j: lax.dynamic_index_in_dim(incoming[:, j], i, 0, keepdims=False).astype(F32)
    hid = [pick(q ^ k, 0) for k in range(4)]
    lift = [pick(2 + t, 1) - pick(t, 1) for t in (s, 1 - s)]

    selector = (jnp.arange(gates.shape[1], dtype=jnp.int32) == group_prompt[0]).astype(F32)
    gate_row = jnp.sum(selector[:, None] * gates[0], axis=0)
    gate_other = swap(gate_row, "branch")
    cut = lambda v: lax.dynamic_slice_in_dim(v, q * SLICE, SLICE, 0)
    g_own, g_other = cut(gate_row), cut(gate_other)
    c_own = jnp.where(is_first, F32(GUIDE), F32(1.0 - GUIDE))
    c_other = jnp.where(is_first, F32(1.0 - GUIDE), F32(GUIDE))

    up_slice = cut(adapter_up_transposed)
    down_turned = (
        adapter_down_map.reshape(ZH, XN, YN * ROWS, RANK).transpose(1, 0, 2, 3).reshape(MODEL_WIDTH, RANK)
    )
    low_rank = dot_nn(rows, down_turned).astype(BF16)
    projected = dot_nn(rows, weight) + ADAPTER_STRENGTH * dot_nt(low_rank, up_slice)
    projected = projected.reshape(4, TOK, SLICE)
    gradients = []
    for t in range(2):
        v_own = hid[t] + g_own * projected[t]
        v_other = hid[2 + t] + g_other * projected[2 + t]
        guided = c_own * v_own + c_other * v_other
        reward_grad = REWARD * (lift[t] + level * guided)
        gradients.append((
            (-level * c_own * g_own * reward_grad).astype(BF16),
            (-level * c_other * g_other * reward_grad).astype(BF16),
        ))
    before = jnp.concatenate([gradients[0][0], gradients[1][0], gradients[0][1], gradients[1][1]], 0)

    low_part = dot_nn(before, up_slice)
    low_part16 = low_part.astype(BF16)
    pair = low_part + jnp.roll(swap(low_part16, "branch").astype(F32), 2 * TOK, axis=0)
    far = swap(pair.astype(BF16), "seq").astype(F32).reshape(2, 2, TOK, RANK)[:, ::-1].reshape(4 * TOK, RANK)
    low_grad = (pair + far).astype(BF16)
    columns = lax.dynamic_index_in_dim(rows.reshape(4 * TOK, XN, ZH, YN * ROWS), q, 2, keepdims=False)
    term_down = ADAPTER_STRENGTH * dot_tn(columns.reshape(4 * TOK, SLICE), low_grad)
    term_up = ADAPTER_STRENGTH * dot_tn(before, low_rank)
    terms = jnp.stack([term_down.astype(BF16), term_up.astype(BF16)]).reshape(2, PLANE, ROWS, RANK)
    terms = terms.transpose(1, 0, 2, 3).reshape(PLANE, 2 * ROWS, RANK)
    spread = lax.all_to_all(terms, "dp", 0, 0, axis_index_groups=XY_GROUPS)
    plane_sum = jnp.sum(spread.astype(F32), axis=0)
    got = [z_transposed(plane_sum, k) for k in range(4)]
    total = (got[0] + got[1]) + (got[2] + got[3])

    part = (
        dot_nt(before, weight) + ADAPTER_STRENGTH * dot_nt(low_part16, down_turned)
    ).reshape(4, TOK, MODEL_WIDTH)
    near_far = swap(part[3].astype(BF16), "branch").astype(F32)
    near = swap(part[2].astype(BF16), "branch").astype(F32)
    across = swap((part[1] + near_far).astype(BF16), "seq").astype(F32)
    grad = (part[0] + near + across).astype(BF16)
    grad = grad.reshape(TOK, XN, ZH, YN * ROWS).transpose(0, 2, 1, 3).reshape(TOK, MODEL_WIDTH)
    return (grad[None], total[:ROWS], total[ROWS:])


def solution(mesh):
    return jax.shard_map(
        per_device,
        mesh=mesh,
        in_specs=(
            P("branch", ("dp", "seq"), None),
            P("branch", ("dp", "seq"), None),
            P(("dp", "seq"), None),
            P(("dp", "seq"), None),
            P("dp", None),
            P("dp", None),
            P(),
            P(),
            P("branch", None, None),
            P("dp"),
            P(),
        ),
        out_specs=(P("branch", ("dp", "seq"), None), P("dp", None), P("dp", None)),
        check_vma=False,
    )
```

time: 1110 us -> 188 us (0.17)
  the two profiles are of different devices: /device:TPU:64 before, /device:TPU:1 now
where the time goes in v1:
time: 188 us; the launch traced here: 187 us
  starting transfers between devices  84.7 us (45%)
  waiting for transfers between devices  26 us (14%)
  blocking collectives  22.8 us (12%)
  between operations  16 us (9%)
  matrix products  15.1 us (8%)
  local copies, waits for them, and re-layouts  13.5 us (7%)
  other arithmetic  9.08 us (5%)
    ppermute x9, starting transfers between devices, swap(): return lax.ppermute(value, axis, [(0, 1), (1, 0)])  23.8 us
    ppermute x4, starting transfers between devices, z_transposed(): return lax.ppermute(value, EVERY, pairs)  23.7 us
    all_gather x1, blocking collectives, gathered_weight(): lined = lax.all_gather(ordered, 'dp', axis=0, axis_index_groups=Y_GROUPS)  22.8 us
    ppermute x3, starting transfers between devices, along_z(): return lax.ppermute(value, 'dp', pairs)  17.6 us
    all_gather x1, waiting for transfers between devices, gathered_weight(): whole = lax.all_gather(square, 'dp', axis=0, axis_index_groups=X_GROUPS)  14 us
    all_to_all x1, starting transfers between devices, per_device(): incoming = lax.all_to_all(outgoing, ('branch', 'seq'), 0, 0)  11.4 us
    all_to_all x1, starting transfers between devices, per_device(): spread = lax.all_to_all(terms, 'dp', 0, 0, axis_index_groups=XY_GROUPS)  8.19 us
    dot_general x3, matrix products, dot_nn(): lax.dot_general(left, right, (((1,), (0,)), ((), ())), preferred_element_...  7.71 us
  transfers between devices with their start and end apart: 19, of which 6 were waited for; matrix products, arithmetic and copies ran while one was open for 11% of the time, Pallas kernels for 0%

profile of v1, /device:TPU:1, one launch (start us, length us, event | category | flops | bytes accessed | tf_op | source)
XLA Modules:
  0.0 187.2 jit_solution(15348147083613214156)
XLA Ops:
  7.2 0.8 multiply_exponential_fusion
  8.5 11.5 %collective-permute-start.3 = (bf16[19,608]{1,0:T(8,128)(2,1)S(1)}, bf16[19,608]{1,0:T(8,128)(2,1)S(1)}, u32[]{:S(2)}, u32[]{:S(2)}) collective-permute-start(bf16[19,608]{1,0:T(8,128)(2,1)S(1)} %bitcast.105), channel_id=1, source_target_pairs={{0,192},{2,194},{4,196},{6,198},{8,200},{10,202},{12,204},{14,206}... | collective-permute-start | bytes 69320 | tf_op jit(solution)/shard_map/ppermute | solution.py:67
  20.0 1.9 %collective-permute-start.5 = (bf16[19,608]{1,0:T(8,128)(2,1)S(1)}, bf16[19,608]{1,0:T(8,128)(2,1)S(1)}, u32[]{:S(2)}, u32[]{:S(2)}) collective-permute-start(bf16[19,608]{1,0:T(8,128)(2,1)S(1)} %bitcast.106), channel_id=1, source_target_pairs={{0,64},{2,66},{4,68},{6,70},{8,72},{10,74},{12,76},{14,78},{16,80}... | collective-permute-start | bytes 69320 | tf_op jit(solution)/shard_map/ppermute | solution.py:67
  22.0 4.2 %collective-permute-start.4 = (bf16[19,608]{1,0:T(8,128)(2,1)S(1)}, bf16[19,608]{1,0:T(8,128)(2,1)S(1)}, u32[]{:S(2)}, u32[]{:S(2)}) collective-permute-start(bf16[19,608]{1,0:T(8,128)(2,1)S(1)} %bitcast.107), channel_id=1, source_target_pairs={{0,128},{2,130},{4,132},{6,134},{8,136},{10,138},{12,140},{14,142}... | collective-permute-start | bytes 69320 | tf_op jit(solution)/shard_map/ppermute | solution.py:67
  26.2 4.3 %collective-permute-done.4 = bf16[19,608]{1,0:T(8,128)(2,1)S(1)} collective-permute-done((bf16[19,608]{1,0:T(8,128)(2,1)S(1)}, bf16[19,608]{1,0:T(8,128)(2,1)S(1)}, u32[]{:S(2)}, u32[]{:S(2)}) %collective-permute-start.4) | collective-permute-done | bytes 23136 | tf_op jit(solution)/shard_map/ppermute | solution.py:67
  30.6 22.8 %all-gather = bf16[32,19,608]{2,1,0:T(8,128)(2,1)S(1)} all-gather(bf16[4,19,608]{2,1,0:T(8,128)(2,1)S(1)} %constant_dynamic-slice_fusion), channel_id=2, replica_groups={{0,2,4,6,8,10,12,14},{16,18,20,22,24,26,28,30},{32,34,36,38,40,42,44,46..., dimensions={0}, use_global_device_ids=true | all-gather | bytes 831744 | tf_op jit(solution)/shard_map/all_gather | solution.py:90
  53.6 1.3 all_gather_reshape.3
  55.3 0.9 copy.45
  56.1 3.6 %collective-permute-start = (bf16[128,2432]{0,1:T(8,128)(2,1)}, bf16[128,2432]{0,1:T(8,128)(2,1)}, u32[]{:S(2)}, u32[]{:S(2)}) collective-permute-start(bf16[128,2432]{0,1:T(8,128)(2,1)} %bitcast.10), channel_id=1, source_target_pairs={{0,1},{1,0},{2,3},{3,2},{4,5},{5,4},{6,7},{7,6},{8,9},{9,8},{10,11... | collective-permute-start | bytes 1867784 | tf_op jit(solution)/shard_map/ppermute | solution.py:26
  60.2 0.7 copy-done.6
  61.3 1.2 maximum_bitcast_fusion
  62.5 11.4 %all-to-all-start = ((bf16[4,2,128,608]{2,3,1,0:T(8,128)(2,1)}), bf16[4,2,128,608]{2,3,1,0:T(8,128)(2,1)S(1)}, u32[]{:S(2)}, u32[]{:S(2)}) async-start(bf16[4,2,128,608]{2,3,1,0:T(8,128)(2,1)} %maximum_bitcast_fusion), calls=%async_computation | async-start | bytes 2490368 | tf_op jit(solution)/shard_map/all_to_all | solution.py:125
  73.9 1.9 %collective-permute-start.1 = (bf16[128,2432]{0,1:T(8,128)(2,1)}, bf16[128,2432]{0,1:T(8,128)(2,1)}, u32[]{:S(2)}, u32[]{:S(2)}) collective-permute-start(bf16[128,2432]{0,1:T(8,128)(2,1)} %bitcast.10), channel_id=1, source_target_pairs={{0,256},{256,0},{1,257},{257,1},{2,258},{258,2},{3,259},{259,3},{4... | collective-permute-start | bytes 1867784 | tf_op jit(solution)/shard_map/ppermute | solution.py:26
  75.9 2.4 %collective-permute-start.2 = (bf16[128,2432]{0,1:T(8,128)(2,1)}, bf16[128,2432]{0,1:T(8,128)(2,1)}, u32[]{:S(2)}, u32[]{:S(2)}) collective-permute-start(bf16[128,2432]{0,1:T(8,128)(2,1)} %collective-permute-done), channel_id=1, source_target_pairs={{0,256},{256,0},{1,257},{257,1},{2,258},{258,2},{3,259},{259,3},{4... | collective-permute-start | bytes 1867784 | tf_op jit(solution)/shard_map/ppermute | solution.py:26
  79.0 2.0 %collective-permute-start.6 = (f32[2432]{0:T(1024)S(1)}, f32[2432]{0:T(1024)S(1)}, u32[]{:S(2)}, u32[]{:S(2)}) collective-permute-start(f32[2432]{0:T(1024)S(1)} %fusion.27), channel_id=1, source_target_pairs={{0,256},{256,0},{1,257},{257,1},{2,258},{258,2},{3,259},{259,3},{4... | collective-permute-start | bytes 29192 | tf_op jit(solution)/shard_map/ppermute | solution.py:26
  81.8 1.1 copy.47
  83.0 2.0 %fusion.8 = bf16[512,4,1,152]{0,3,1,2:T(8,128)(2,1)} fusion(s32[]{:T(128)S(6)} %select_n.62, bf16[128,4,4,152]{0,3,1,2:T(8,128)(2,1)S(1)} %bitcast.90, bf16[128,4,4,152]{0,3,2,1:T(8,128)(2,1)} %bitcast.30, bf16[128,4,4,152]{0,3,2,1:T(8,128)(2,1)} %bitcast.29, bf16[128,4,4,152]{0,3,2,1:T(8,128)(2,1)} %bitcast.28), kind=kLoop, calls=%fused_computation.24 | loop fusion | flops 2490368 | bytes 3112964 | tf_op jit(solution)/shard_map/concatenate | solution.py:120
  85.0 2.5 %convolution_convert_fusion = bf16[512,128]{1,0:T(8,128)(2,1)S(1)} fusion(bf16[2432,128]{1,0:T(8,128)(2,1)S(1)} %bitcast.93, bf16[128,2432]{0,1:T(8,128)(2,1)} %collective-permute-done.2, bf16[128,2432]{0,1:T(8,128)(2,1)} %collective-permute-done.1, bf16[128,2432]{0,1:T(8,128)(2,1)} %collective-permute-done, bf16[128,2432]{0,1:T(8,128)(2,1)} %bitcast.10), kind=kOutput, calls=%fused_computation.19 | convolution fusion | flops 328794112 | bytes 3244032 | tf_op jit(solution)/shard_map/dot_general | solution.py:45
  87.5 1.4 convolution_multiply_fusion.1
  88.8 0.8 all-to-all-done
  89.7 0.9 fusion.37
  90.6 14.0 %all-gather.3.cloned.1.call-done = bf16[4,608,608]{2,1,0:T(8,128)(2,1)} async-done(((bf16[1,608,608]{2,1,0:T(8,128)(2,1)}), bf16[4,608,608]{2,1,0:T(8,128)(2,1)}) %all-gather.3.cloned.1.call-update) | async-done | bytes 2957328 | tf_op jit(solution)/shard_map/all_gather | solution.py:92
  104.6 4.8 %convolution_add_fusion = f32[512,608]{0,1:T(8,128)S(1)} fusion(f32[512,608]{0,1:T(8,128)} %convolution_multiply_fusion.1, bf16[2432,608]{1,0:T(8,128)(2,1)} %bitcast.108, bf16[128,2432]{0,1:T(8,128)(2,1)} %collective-permute-done.2, bf16[128,2432]{0,1:T(8,128)(2,1)} %collective-permute-done.1, bf16[128,2432]{0,1:T(8,128)(2,1)} %collective-permute-done, ...), kind=kOutput, calls=%fused_computation.8 | convolution fusion | flops 1524416512 | bytes 7938048 | tf_op jit(solution)/shard_map/dot_general | solution.py:45
  110.3 0.4 fusion.40
  110.7 1.3 copy-done.10
  112.0 2.3 %fusion.33 = f32[512,2432]{1,0:T(8,128)S(1)} fusion(bf16[2432,608]{1,0:T(8,128)(2,1)S(1)} %bitcast.109, bf16[128,608]{0,1:T(8,128)(2,1)S(1)} %get-tuple-element.29, bf16[128,608]{0,1:T(8,128)(2,1)S(1)} %get-tuple-element.28, bf16[128,608]{0,1:T(8,128)(2,1)S(1)} %get-tuple-element.14, bf16[128,608]{0,1:T(8,128)(2,1)S(1)} %get-tuple-element.12), kind=kOutput, calls=%fused_computation.79 | convolution fusion | flops 1516634112 | bytes 8560640 | tf_op jit(solution)/shard_map/dot_general | solution.py:49
  114.3 2.6 %collective-permute-start.10 = (bf16[512,128]{1,0:T(8,128)(2,1)S(1)}, bf16[512,128]{1,0:T(8,128)(2,1)S(1)}, u32[]{:S(2)}, u32[]{:S(2)}) collective-permute-start(bf16[512,128]{1,0:T(8,128)(2,1)S(1)} %get-tuple-element.30), channel_id=1, source_target_pairs={{0,256},{256,0},{1,257},{257,1},{2,258},{258,2},{3,259},{259,3},{4... | collective-permute-start | bytes 393224 | tf_op jit(solution)/shard_map/ppermute | solution.py:26
  116.8 3.1 %fusion.41 = (bf16[512,2432]{1,0:T(8,128)(2,1)S(1)}, f32[512,2432]{1,0:T(8,128)}) fusion(f32[512,2432]{1,0:T(8,128)S(1)} %fusion.33, bf16[512,128]{1,0:T(8,128)(2,1)S(1)} %get-tuple-element.30, bf16[2432,128]{1,0:T(8,128)(2,1)S(1)} %bitcast.94), kind=kOutput, calls=%fused_computation.85 | convolution fusion | flops 322502656 | bytes 13205504 | tf_op jit(solution)/shard_map/dot_general | solution.py:49
  119.9 0.9 fusion.36
  120.8 1.9 %collective-permute-start.8 = (bf16[128,2432]{1,0:T(8,128)(2,1)}, bf16[128,2432]{1,0:T(8,128)(2,1)}, u32[]{:S(2)}, u32[]{:S(2)}) collective-permute-start(bf16[128,2432]{1,0:T(8,128)(2,1)} %get-tuple-element.21), channel_id=1, source_target_pairs={{0,256},{256,0},{1,257},{257,1},{2,258},{258,2},{3,259},{259,3},{4... | collective-permute-start | bytes 1867784 | tf_op jit(solution)/shard_map/ppermute | solution.py:26
  122.8 0.7 fusion.28
  123.5 3.3 %collective-permute-start.11 = (bf16[512,128]{1,0:T(8,128)(2,1)}, bf16[512,128]{1,0:T(8,128)(2,1)S(1)}, u32[]{:S(2)}, u32[]{:S(2)}) collective-permute-start(bf16[512,128]{1,0:T(8,128)(2,1)} %fusion.28), channel_id=1, source_target_pairs={{0,1},{1,0},{2,3},{3,2},{4,5},{5,4},{6,7},{7,6},{8,9},{9,8},{10,11... | collective-permute-start | bytes 393224 | tf_op jit(solution)/shard_map/ppermute | solution.py:26
  127.1 2.8 %collective-permute-start.7 = (bf16[128,2432]{1,0:T(8,128)(2,1)S(1)}, bf16[128,2432]{1,0:T(8,128)(2,1)S(1)}, u32[]{:S(2)}, u32[]{:S(2)}) collective-permute-start(bf16[128,2432]{1,0:T(8,128)(2,1)S(1)} %get-tuple-element.20), channel_id=1, source_target_pairs={{0,256},{256,0},{1,257},{257,1},{2,258},{258,2},{3,259},{259,3},{4... | collective-permute-start | bytes 1867784 | tf_op jit(solution)/shard_map/ppermute | solution.py:26
  130.1 0.6 copy-done.7
  130.8 0.9 rev.3
  132.2 0.9 copy.54
  133.1 8.2 %all-to-all-start.1 = ((bf16[32,38,128]{2,1,0:T(8,128)(2,1)}), bf16[32,38,128]{2,1,0:T(8,128)(2,1)S(1)}, u32[]{:S(2)}, u32[]{:S(2)}) async-start(bf16[32,38,128]{2,1,0:T(8,128)(2,1)} %copy.54), calls=%async_computation.1 | async-start | bytes 655360 | tf_op jit(solution)/shard_map/all_to_all | solution.py:167
  141.3 1.6 fusion.1
  142.9 3.3 %collective-permute-start.9 = (bf16[128,2432]{1,0:T(8,128)(2,1)S(1)}, bf16[128,2432]{1,0:T(8,128)(2,1)}, u32[]{:S(2)}, u32[]{:S(2)}) collective-permute-start(bf16[128,2432]{1,0:T(8,128)(2,1)S(1)} %fusion.1), channel_id=1, source_target_pairs={{0,1},{1,0},{2,3},{3,2},{4,5},{5,4},{6,7},{7,6},{8,9},{9,8},{10,11... | collective-permute-start | bytes 1867784 | tf_op jit(solution)/shard_map/ppermute | solution.py:26
  146.2 5.1 %all-to-all-done.1 = bf16[32,38,128]{2,1,0:T(8,128)(2,1)S(1)} async-done(((bf16[32,38,128]{2,1,0:T(8,128)(2,1)}), bf16[32,38,128]{2,1,0:T(8,128)(2,1)S(1)}, u32[]{:S(2)}, u32[]{:S(2)}) %all-to-all-start.1) | async-done | bytes 311328 | tf_op jit(solution)/shard_map/all_to_all | solution.py:167
  151.3 7.0 %collective-permute-start.15 = (f32[38,128]{1,0:T(8,128)S(1)}, f32[38,128]{1,0:T(8,128)S(1)}, u32[]{:S(2)}, u32[]{:S(2)}) collective-permute-start(f32[38,128]{1,0:T(8,128)S(1)} %convert_reduce_fusion), channel_id=1, source_target_pairs={{0,257},{1,321},{256,385},{257,449},{2,259},{3,323},{258,387},{259... | collective-permute-start | bytes 58376 | tf_op jit(solution)/shard_map/ppermute | solution.py:81
  158.3 7.4 %collective-permute-start.14 = (f32[38,128]{1,0:T(8,128)S(1)}, f32[38,128]{1,0:T(8,128)S(1)}, u32[]{:S(2)}, u32[]{:S(2)}) collective-permute-start(f32[38,128]{1,0:T(8,128)S(1)} %convert_reduce_fusion), channel_id=1, source_target_pairs={{0,256},{1,320},{256,384},{257,448},{2,258},{3,322},{258,386},{259... | collective-permute-start | bytes 58376 | tf_op jit(solution)/shard_map/ppermute | solution.py:81
  165.7 1.9 %collective-permute-start.13 = (f32[38,128]{1,0:T(8,128)S(1)}, f32[38,128]{1,0:T(8,128)S(1)}, u32[]{:S(2)}, u32[]{:S(2)}) collective-permute-start(f32[38,128]{1,0:T(8,128)S(1)} %convert_reduce_fusion), channel_id=1, source_target_pairs={{0,1},{1,65},{256,129},{257,193},{2,3},{3,67},{258,131},{259,195},... | collective-permute-start | bytes 58376 | tf_op jit(solution)/shard_map/ppermute | solution.py:81
  167.6 7.4 %collective-permute-start.12 = (f32[38,128]{1,0:T(8,128)S(1)}, f32[38,128]{1,0:T(8,128)S(1)}, u32[]{:S(2)}, u32[]{:S(2)}) collective-permute-start(f32[38,128]{1,0:T(8,128)S(1)} %convert_reduce_fusion), channel_id=1, source_target_pairs={{0,0},{1,64},{256,128},{257,192},{2,2},{3,66},{258,130},{259,194},... | collective-permute-start | bytes 58376 | tf_op jit(solution)/shard_map/ppermute | solution.py:81
  175.0 1.6 collective-permute-done.12
  176.7 0.6 fusion.39
  177.3 1.6 fusion.3
  179.3 1.1 copy.55
  (74 shorter events, 4.4 us)
Async XLA Ops:
  7.2 80.3 %copy-start = (bf16[2432,128]{1,0:T(8,128)(2,1)S(1)}, bf16[2432,128]{1,0:T(8,128)(2,1)}, u32[]{:S(2)}) copy-start(bf16[2432,128]{1,0:T(8,128)(2,1)} %param.18) | copy-start | bytes 1867780
  7.2 1.0 copy-start.8
  7.2 97.4 %all-gather.3.cloned.1.call-start = ((), (), s32[]{:S(2)}) async-start(), calls=%async_computation.2 | async-start | bytes 3891200 | tf_op jit(solution)/shard_map/all_gather | solution.py:92
  8.5 17.7 %collective-permute-start.3 = (bf16[19,608]{1,0:T(8,128)(2,1)S(1)}, bf16[19,608]{1,0:T(8,128)(2,1)S(1)}, u32[]{:S(2)}, u32[]{:S(2)}) collective-permute-start(bf16[19,608]{1,0:T(8,128)(2,1)S(1)} %bitcast.105), channel_id=1, source_target_pairs={{0,192},{2,194},{4,196},{6,198},{8,200},{10,202},{12,204},{14,206}... | collective-permute-start | bytes 69320 | tf_op jit(solution)/shard_map/ppermute | solution.py:67
  20.0 10.5 %collective-permute-start.5 = (bf16[19,608]{1,0:T(8,128)(2,1)S(1)}, bf16[19,608]{1,0:T(8,128)(2,1)S(1)}, u32[]{:S(2)}, u32[]{:S(2)}) collective-permute-start(bf16[19,608]{1,0:T(8,128)(2,1)S(1)} %bitcast.106), channel_id=1, source_target_pairs={{0,64},{2,66},{4,68},{6,70},{8,72},{10,74},{12,76},{14,78},{16,80}... | collective-permute-start | bytes 69320 | tf_op jit(solution)/shard_map/ppermute | solution.py:67
  22.0 8.5 %collective-permute-start.4 = (bf16[19,608]{1,0:T(8,128)(2,1)S(1)}, bf16[19,608]{1,0:T(8,128)(2,1)S(1)}, u32[]{:S(2)}, u32[]{:S(2)}) collective-permute-start(bf16[19,608]{1,0:T(8,128)(2,1)S(1)} %bitcast.107), channel_id=1, source_target_pairs={{0,128},{2,130},{4,132},{6,134},{8,136},{10,138},{12,140},{14,142}... | collective-permute-start | bytes 69320 | tf_op jit(solution)/shard_map/ppermute | solution.py:67
  53.6 1.3 copy-start.3
  54.9 4.9 %copy-start.4 = (bf16[128,2432]{1,0:T(8,128)(2,1)S(1)}, bf16[128,2432]{1,0:T(8,128)(2,1)}, u32[]{:S(2)}) copy-start(bf16[128,2432]{1,0:T(8,128)(2,1)} %param.13) | copy-start | bytes 1867780
  55.2 4.5 %copy-start.5 = (bf16[128,2432]{1,0:T(8,128)(2,1)S(1)}, bf16[128,2432]{1,0:T(8,128)(2,1)}, u32[]{:S(2)}) copy-start(bf16[128,2432]{1,0:T(8,128)(2,1)} %param.14) | copy-start | bytes 1867780
  56.1 19.7 %collective-permute-start = (bf16[128,2432]{0,1:T(8,128)(2,1)}, bf16[128,2432]{0,1:T(8,128)(2,1)}, u32[]{:S(2)}, u32[]{:S(2)}) collective-permute-start(bf16[128,2432]{0,1:T(8,128)(2,1)} %bitcast.10), channel_id=1, source_target_pairs={{0,1},{1,0},{2,3},{3,2},{4,5},{5,4},{6,7},{7,6},{8,9},{9,8},{10,11... | collective-permute-start | bytes 1867784 | tf_op jit(solution)/shard_map/ppermute | solution.py:26
  59.9 1.1 copy-start.6
  62.5 16.4 %copy-start.9 = (f32[1,8,2432]{2,1,0:T(8,128)S(1)}, f32[1,8,2432]{2,1,0:T(8,128)}, u32[]{:S(2)}) copy-start(f32[1,8,2432]{2,1,0:T(8,128)} %param.19) | copy-start | bytes 233476
  62.5 27.2 %all-to-all-start = ((bf16[4,2,128,608]{2,3,1,0:T(8,128)(2,1)}), bf16[4,2,128,608]{2,3,1,0:T(8,128)(2,1)S(1)}, u32[]{:S(2)}, u32[]{:S(2)}) async-start(bf16[4,2,128,608]{2,3,1,0:T(8,128)(2,1)} %maximum_bitcast_fusion), calls=%async_computation | async-start | bytes 2490368 | tf_op jit(solution)/shard_map/all_to_all | solution.py:125
  73.9 9.1 %collective-permute-start.1 = (bf16[128,2432]{0,1:T(8,128)(2,1)}, bf16[128,2432]{0,1:T(8,128)(2,1)}, u32[]{:S(2)}, u32[]{:S(2)}) collective-permute-start(bf16[128,2432]{0,1:T(8,128)(2,1)} %bitcast.10), channel_id=1, source_target_pairs={{0,256},{256,0},{1,257},{257,1},{2,258},{258,2},{3,259},{259,3},{4... | collective-permute-start | bytes 1867784 | tf_op jit(solution)/shard_map/ppermute | solution.py:26
  75.9 7.2 %collective-permute-start.2 = (bf16[128,2432]{0,1:T(8,128)(2,1)}, bf16[128,2432]{0,1:T(8,128)(2,1)}, u32[]{:S(2)}, u32[]{:S(2)}) collective-permute-start(bf16[128,2432]{0,1:T(8,128)(2,1)} %collective-permute-done), channel_id=1, source_target_pairs={{0,256},{256,0},{1,257},{257,1},{2,258},{258,2},{3,259},{259,3},{4... | collective-permute-start | bytes 1867784 | tf_op jit(solution)/shard_map/ppermute | solution.py:26
  79.0 3.9 %collective-permute-start.6 = (f32[2432]{0:T(1024)S(1)}, f32[2432]{0:T(1024)S(1)}, u32[]{:S(2)}, u32[]{:S(2)}) collective-permute-start(f32[2432]{0:T(1024)S(1)} %fusion.27), channel_id=1, source_target_pairs={{0,256},{256,0},{1,257},{257,1},{2,258},{258,2},{3,259},{259,3},{4... | collective-permute-start | bytes 29192 | tf_op jit(solution)/shard_map/ppermute | solution.py:26
  104.6 4.8 %copy-start.2 = (bf16[4,1,128,608]{2,3,1,0:T(8,128)(2,1)S(1)}, bf16[4,1,128,608]{2,3,1,0:T(8,128)(2,1)}, u32[]{:S(2)}) copy-start(bf16[4,1,128,608]{2,3,1,0:T(8,128)(2,1)} %get-tuple-element.23) | copy-start | bytes 1867780
  110.1 1.9 %copy-start.10 = (bf16[4,608,608]{2,1,0:T(8,128)(2,1)S(1)}, bf16[4,608,608]{2,1,0:T(8,128)(2,1)}, u32[]{:S(2)}) copy-start(bf16[4,608,608]{2,1,0:T(8,128)(2,1)} %all-gather.3.cloned.1.call-done) | copy-start | bytes 8871940
  114.3 8.5 %collective-permute-start.10 = (bf16[512,128]{1,0:T(8,128)(2,1)S(1)}, bf16[512,128]{1,0:T(8,128)(2,1)S(1)}, u32[]{:S(2)}, u32[]{:S(2)}) collective-permute-start(bf16[512,128]{1,0:T(8,128)(2,1)S(1)} %get-tuple-element.30), channel_id=1, source_target_pairs={{0,256},{256,0},{1,257},{257,1},{2,258},{258,2},{3,259},{259,3},{4... | collective-permute-start | bytes 393224 | tf_op jit(solution)/shard_map/ppermute | solution.py:26
  120.8 20.5 %collective-permute-start.8 = (bf16[128,2432]{1,0:T(8,128)(2,1)}, bf16[128,2432]{1,0:T(8,128)(2,1)}, u32[]{:S(2)}, u32[]{:S(2)}) collective-permute-start(bf16[128,2432]{1,0:T(8,128)(2,1)} %get-tuple-element.21), channel_id=1, source_target_pairs={{0,256},{256,0},{1,257},{257,1},{2,258},{258,2},{3,259},{259,3},{4... | collective-permute-start | bytes 1867784 | tf_op jit(solution)/shard_map/ppermute | solution.py:26
  123.5 6.7 %collective-permute-start.11 = (bf16[512,128]{1,0:T(8,128)(2,1)}, bf16[512,128]{1,0:T(8,128)(2,1)S(1)}, u32[]{:S(2)}, u32[]{:S(2)}) collective-permute-start(bf16[512,128]{1,0:T(8,128)(2,1)} %fusion.28), channel_id=1, source_target_pairs={{0,1},{1,0},{2,3},{3,2},{4,5},{5,4},{6,7},{7,6},{8,9},{9,8},{10,11... | collective-permute-start | bytes 393224 | tf_op jit(solution)/shard_map/ppermute | solution.py:26
  127.1 4.7 %copy-start.1 = (bf16[512,4,1,152]{0,3,1,2:T(8,128)(2,1)S(1)}, bf16[512,4,1,152]{0,3,1,2:T(8,128)(2,1)}, u32[]{:S(2)}) copy-start(bf16[512,4,1,152]{0,3,1,2:T(8,128)(2,1)} %fusion.8) | copy-start | bytes 1867780
  127.1 50.1 %collective-permute-start.7 = (bf16[128,2432]{1,0:T(8,128)(2,1)S(1)}, bf16[128,2432]{1,0:T(8,128)(2,1)S(1)}, u32[]{:S(2)}, u32[]{:S(2)}) collective-permute-start(bf16[128,2432]{1,0:T(8,128)(2,1)S(1)} %get-tuple-element.20), channel_id=1, source_target_pairs={{0,256},{256,0},{1,257},{257,1},{2,258},{258,2},{3,259},{259,3},{4... | collective-permute-start | bytes 1867784 | tf_op jit(solution)/shard_map/ppermute | solution.py:26
  130.1 0.6 copy-start.7
  133.1 18.1 %all-to-all-start.1 = ((bf16[32,38,128]{2,1,0:T(8,128)(2,1)}), bf16[32,38,128]{2,1,0:T(8,128)(2,1)S(1)}, u32[]{:S(2)}, u32[]{:S(2)}) async-start(bf16[32,38,128]{2,1,0:T(8,128)(2,1)} %copy.54), calls=%async_computation.1 | async-start | bytes 655360 | tf_op jit(solution)/shard_map/all_to_all | solution.py:167
  142.9 34.4 %collective-permute-start.9 = (bf16[128,2432]{1,0:T(8,128)(2,1)S(1)}, bf16[128,2432]{1,0:T(8,128)(2,1)}, u32[]{:S(2)}, u32[]{:S(2)}) collective-permute-start(bf16[128,2432]{1,0:T(8,128)(2,1)S(1)} %fusion.1), channel_id=1, source_target_pairs={{0,1},{1,0},{2,3},{3,2},{4,5},{5,4},{6,7},{7,6},{8,9},{9,8},{10,11... | collective-permute-start | bytes 1867784 | tf_op jit(solution)/shard_map/ppermute | solution.py:26
  151.3 16.3 %collective-permute-start.15 = (f32[38,128]{1,0:T(8,128)S(1)}, f32[38,128]{1,0:T(8,128)S(1)}, u32[]{:S(2)}, u32[]{:S(2)}) collective-permute-start(f32[38,128]{1,0:T(8,128)S(1)} %convert_reduce_fusion), channel_id=1, source_target_pairs={{0,257},{1,321},{256,385},{257,449},{2,259},{3,323},{258,387},{259... | collective-permute-start | bytes 58376 | tf_op jit(solution)/shard_map/ppermute | solution.py:81
  158.3 16.7 %collective-permute-start.14 = (f32[38,128]{1,0:T(8,128)S(1)}, f32[38,128]{1,0:T(8,128)S(1)}, u32[]{:S(2)}, u32[]{:S(2)}) collective-permute-start(f32[38,128]{1,0:T(8,128)S(1)} %convert_reduce_fusion), channel_id=1, source_target_pairs={{0,256},{1,320},{256,384},{257,448},{2,258},{3,322},{258,386},{259... | collective-permute-start | bytes 58376 | tf_op jit(solution)/shard_map/ppermute | solution.py:81
  165.7 9.3 %collective-permute-start.13 = (f32[38,128]{1,0:T(8,128)S(1)}, f32[38,128]{1,0:T(8,128)S(1)}, u32[]{:S(2)}, u32[]{:S(2)}) collective-permute-start(f32[38,128]{1,0:T(8,128)S(1)} %convert_reduce_fusion), channel_id=1, source_target_pairs={{0,1},{1,65},{256,129},{257,193},{2,3},{3,67},{258,131},{259,195},... | collective-permute-start | bytes 58376 | tf_op jit(solution)/shard_map/ppermute | solution.py:81
  167.6 9.0 %collective-permute-start.12 = (f32[38,128]{1,0:T(8,128)S(1)}, f32[38,128]{1,0:T(8,128)S(1)}, u32[]{:S(2)}, u32[]{:S(2)}) collective-permute-start(f32[38,128]{1,0:T(8,128)S(1)} %convert_reduce_fusion), channel_id=1, source_target_pairs={{0,0},{1,64},{256,128},{257,192},{2,2},{3,66},{258,130},{259,194},... | collective-permute-start | bytes 58376 | tf_op jit(solution)/shard_map/ppermute | solution.py:81
Sparse Core Ops, SparseCore 0:
  55.0 49.5 all-gather.2

commit v2 on v1

v2 whole, which is shorter than its diff:
```python
import jax
import jax.numpy as jnp
from jax import lax
from jax.experimental import pallas as pl
from jax.experimental.pallas import tpu as pltpu
from jax.sharding import PartitionSpec as P

MODEL_WIDTH = 2432
QBLOCK = 128
RANK = 128
STEPS = 28
ZH, XN, YN = 4, 4, 8
PLANE = XN * YN
SLICE = MODEL_WIDTH // 4
ROWS = 19
TOK = 128

GUIDE = 4.5
REWARD = 0.08
ADAPTER_STRENGTH = 0.5
SHIFT = 3.0
F32 = jnp.float32
BF16 = jnp.bfloat16
EVERY = ("branch", "dp", "seq")


def swap(value, axis):
    return lax.ppermute(value, axis, [(0, 1), (1, 0)])


def noise_level(step_index):
    frac = step_index[0].astype(F32) / STEPS
    return SHIFT * frac / (1.0 + (SHIFT - 1.0) * frac)


def dequantize(codes, exps):
    count = codes.shape[0]
    block_scale = jnp.exp2(exps.astype(F32))
    grouped = (
        codes.astype(F32).reshape(count, MODEL_WIDTH // QBLOCK, QBLOCK)
        * block_scale[:, :, None]
    )
    return grouped.reshape(count, MODEL_WIDTH).astype(BF16)


def dot_nn(left, right):
    return lax.dot_general(left, right, (((1,), (0,)), ((), ())), preferred_element_type=F32)


def dot_nt(left, right):
    return lax.dot_general(left, right, (((1,), (1,)), ((), ())), preferred_element_type=F32)


def dot_tn(left, right):
    return lax.dot_general(left, right, (((0,), (0,)), ((), ())), preferred_element_type=F32)


def dp_index(z, x, y):
    return z * PLANE + x * YN + y


Z_GROUPS = [[dp_index(z, x, y) for z in range(ZH)] for x in range(XN) for y in range(YN)]
Y_GROUPS = [[dp_index(z, x, y) for y in range(YN)] for z in range(ZH) for x in range(XN)]
X_GROUPS = [[dp_index(z, x, y) for x in range(XN)] for z in range(ZH) for y in range(YN)]
XY_GROUPS = [[z * PLANE + i for i in range(PLANE)] for z in range(ZH)]


def to_all(value, groups):
    copies = jnp.broadcast_to(value, (len(groups[0]),) + value.shape)
    return lax.all_to_all(copies, "dp", 0, 0, axis_index_groups=groups)


def place(branch, dp, seq):
    return (branch * ZH * PLANE + dp) * 2 + seq


def z_transposed(value, flip):
    pairs = []
    for z in range(ZH):
        for i in range(PLANE):
            for q in range(4):
                r = z ^ flip
                pairs.append((place(q // 2, z * PLANE + i, q % 2), place(r // 2, q * PLANE + i, r % 2)))
    return lax.ppermute(value, EVERY, pairs)


def own_columns(codes, exps, q):
    local = dequantize(codes, exps).reshape(ROWS, 4, SLICE)
    return lax.dynamic_index_in_dim(local, q, 1, keepdims=False)


def lanes(refs):
    return jnp.concatenate([ref[...] for ref in refs], 1)


def call(kernel, outs, flops, *args, **more):
    return pl.pallas_call(
        kernel,
        out_shape=[jax.ShapeDtypeStruct(shape, kind) for shape, kind in outs],
        compiler_params=pltpu.CompilerParams(vmem_limit_bytes=24 * 2**20),
        cost_estimate=pl.CostEstimate(flops=flops, bytes_accessed=8 * 10**6, transcendentals=0),
        **more,
    )(*args)


def adapter_kernel(own, seq, branch, both, down, up, lift, lift_far, a_own, a_other, low_rank, base):
    rows = lanes((own, seq, branch, both))
    low = dot_tn(down[...], rows).astype(BF16)
    low_rank[...] = low
    adapted = ADAPTER_STRENGTH * dot_nn(up[...], low)
    base[...] = lanes((lift, lift_far)) - a_own[...] * adapted[:, :2 * TOK] - a_other[...] * adapted[:, 2 * TOK:]


def forward_kernel(own, seq, branch, both, weight, base, a_own, a_other, up, before, low, product):
    step = pl.program_id(0)
    part = dot_tn(weight[...], lanes((own, seq, branch, both)))

    @pl.when(step == 0)
    def _():
        product[...] = part

    @pl.when((step > 0) & (step < XN - 1))
    def _():
        product[...] += part

    @pl.when(step == XN - 1)
    def _():
        whole = product[...] + part
        first, second = a_own[...], a_other[...]
        reward_grad = REWARD * (base[...] - first * whole[:, :2 * TOK] - second * whole[:, 2 * TOK:])
        grad = jnp.concatenate([first * reward_grad, second * reward_grad], 1).astype(BF16)
        before[...] = grad
        low[...] = dot_tn(up[...], grad)


def backward_kernel(before, weight, low, down, home, cross, near, far):
    part = dot_nn(weight[...], before[...]) + ADAPTER_STRENGTH * dot_nn(down[...], low[...].astype(BF16))
    for block, out in enumerate((home, cross, near, far)):
        out[...] = part[:, block * TOK:(block + 1) * TOK].astype(out.dtype)


def fixed(*shape):
    return pl.BlockSpec(shape, lambda n: (0, 0))


def rows_of(width):
    return pl.BlockSpec((SLICE, width), lambda n: (n, 0))


def forward(tokens, weight, base, a_own, a_other, up):
    return call(
        forward_kernel,
        [((SLICE, 4 * TOK), BF16), ((RANK, 4 * TOK), F32)],
        2 * 512 * 2432 * 608,
        *tokens, weight, base, a_own, a_other, up,
        grid=(XN,),
        in_specs=[rows_of(TOK)] * 4 + [rows_of(SLICE), fixed(SLICE, 2 * TOK), fixed(SLICE, 1), fixed(SLICE, 1), fixed(SLICE, RANK)],
        out_specs=[fixed(SLICE, 4 * TOK), fixed(RANK, 4 * TOK)],
        scratch_shapes=[pltpu.VMEM((SLICE, 4 * TOK), F32)],
    )


def backward(before, weight, low, down):
    shape = (MODEL_WIDTH, TOK)
    return call(
        backward_kernel,
        [(shape, F32), (shape, F32), (shape, BF16), (shape, BF16)],
        2 * 512 * 2432 * 736,
        before, weight, low, down,
        grid=(XN,),
        in_specs=[fixed(SLICE, 4 * TOK), rows_of(SLICE), fixed(RANK, 4 * TOK), rows_of(RANK)],
        out_specs=[rows_of(TOK)] * 4,
    )


def per_device(
    attn,
    hidden,
    noisy,
    target,
    quantized_weight_codes,
    weight_exponents,
    adapter_down_map,
    adapter_up_transposed,
    gates,
    group_prompt,
    step_index,
):
    b = lax.axis_index("branch")
    s = lax.axis_index("seq")
    q = 2 * b + s
    level = noise_level(step_index)
    is_first = b == 0
    mine = own_columns(quantized_weight_codes, weight_exponents, q)
    plane = to_all(mine, Z_GROUPS).reshape(ZH * ROWS, SLICE)
    plane, hidden = lax.optimization_barrier((plane, hidden))
    lined = to_all(plane, Y_GROUPS)

    own = attn[0].T.reshape(ZH, XN, YN * ROWS, TOK).transpose(1, 0, 2, 3).reshape(MODEL_WIDTH, TOK)
    from_seq = swap(own, "seq")
    from_branch = swap(own, "branch")

    c_own = jnp.where(is_first, F32(GUIDE), F32(1.0 - GUIDE))
    c_other = jnp.where(is_first, F32(1.0 - GUIDE), F32(GUIDE))
    half = lambda v, i: lax.dynamic_slice_in_dim(v, i * 2 * SLICE, 2 * SLICE, 1).astype(F32)
    hid_other = swap(lax.dynamic_slice_in_dim(hidden[0], (1 - b) * 2 * SLICE, 2 * SLICE, 1), "branch").astype(F32)
    lift = half(target, b) - half(noisy, b) + level * (c_own * half(hidden[0], b) + c_other * hid_other)
    lift = jnp.stack([lift[:, :SLICE].T, lift[:, SLICE:].T])
    take = lambda i: lax.dynamic_index_in_dim(lift, i, 0, keepdims=False)
    lift_near = take(s)
    lift_far = swap(take(1 - s), "seq")

    lined, from_seq, from_branch = lax.optimization_barrier((lined, from_seq, from_branch))
    square = lined.reshape(YN, ZH, ROWS, SLICE).transpose(1, 0, 2, 3).reshape(SLICE, SLICE)
    weight = to_all(square, X_GROUPS).reshape(MODEL_WIDTH, SLICE)
    from_both = swap(from_seq, "branch")
    tokens = (own, from_seq, from_branch, from_both)

    selector = (jnp.arange(gates.shape[1], dtype=jnp.int32) == group_prompt[0]).astype(F32)
    gate_row = jnp.sum(selector[:, None] * gates[0], axis=0)
    gate_other = swap(gate_row, "branch")
    cut = lambda v: lax.dynamic_slice_in_dim(v, q * SLICE, SLICE, 0)
    a_own = (-level * c_own * cut(gate_row))[:, None]
    a_other = (-level * c_other * cut(gate_other))[:, None]
    up_slice = cut(adapter_up_transposed)
    down_turned = (
        adapter_down_map.reshape(ZH, XN, YN * ROWS, RANK).transpose(1, 0, 2, 3).reshape(MODEL_WIDTH, RANK)
    )
    low_rank, base = call(
        adapter_kernel,
        [((RANK, 4 * TOK), BF16), ((SLICE, 2 * TOK), F32)],
        2 * 512 * 128 * 3040,
        *tokens, down_turned, up_slice, lift_near, lift_far, a_own, a_other,
    )
    before, low_part = forward(tokens, weight, base, a_own, a_other, up_slice)

    blocks = lambda v, *which: jnp.concatenate([v[:, i * TOK:(i + 1) * TOK] for i in which], 1)
    from_core = swap(low_part.astype(BF16), "branch").astype(F32)
    pair = low_part + blocks(from_core, 2, 3, 0, 1)
    pair16 = pair.astype(BF16)
    pair16, before_late = lax.optimization_barrier((pair16, before))
    from_chip = swap(pair16, "seq").astype(F32)
    low_grad = (pair + blocks(from_chip, 1, 0, 3, 2)).astype(BF16)
    mine_of = lambda v: lax.dynamic_index_in_dim(v.reshape(XN, ZH, YN * ROWS, TOK), q, 1, keepdims=False)
    columns = jnp.concatenate([mine_of(v).reshape(SLICE, TOK) for v in tokens], 1)
    term_down = ADAPTER_STRENGTH * dot_nt(columns, low_grad)
    term_up = ADAPTER_STRENGTH * dot_nt(before_late, low_rank)
    terms = jnp.stack([term_down.astype(BF16), term_up.astype(BF16)]).reshape(2, PLANE, ROWS, RANK)
    terms = terms.transpose(1, 0, 2, 3).reshape(PLANE, 2 * ROWS, RANK)
    spread = lax.all_to_all(terms, "dp", 0, 0, axis_index_groups=XY_GROUPS)
    plane_sum = jnp.sum(spread.astype(F32), axis=0)
    got = [z_transposed(plane_sum, k) for k in range(4)]
    total = (got[0] + got[1]) + (got[2] + got[3])

    home, cross, near, far = backward(before_late, weight, low_part, down_turned)
    cross = (cross + swap(far, "branch").astype(F32)).astype(BF16)
    grad = (home + swap(near, "branch").astype(F32) + swap(cross, "seq").astype(F32)).astype(BF16)
    grad = grad.reshape(XN, ZH, YN * ROWS, TOK).transpose(1, 0, 2, 3).reshape(MODEL_WIDTH, TOK).T
    return (grad[None], total[:ROWS], total[ROWS:])


def solution(mesh):
    return jax.shard_map(
        per_device,
        mesh=mesh,
        in_specs=(
            P("branch", ("dp", "seq"), None),
            P("branch", ("dp", "seq"), None),
            P(("dp", "seq"), None),
            P(("dp", "seq"), None),
            P("dp", None),
            P("dp", None),
            P(),
            P(),
            P("branch", None, None),
            P("dp"),
            P(),
        ),
        out_specs=(P("branch", ("dp", "seq"), None), P("dp", None), P("dp", None)),
        check_vma=False,
    )
```

time: 188 us -> 176 us (0.936)
  local copies, waits for them, and re-layouts: 13.5 us -> 30.9 us
  starting transfers between devices: 84.7 us -> 70.6 us
  between operations: 16 us -> 2.49 us
  Pallas kernels: 0 us -> 12.5 us
  matrix products: 15.1 us -> 3.24 us
  blocking collectives: 22.8 us -> 18.1 us
    all_gather x1 -> x0, blocking collectives: 22.8 us -> none  [gathered_weight(): lined = lax.all_gather(ordered, 'dp', axis=0, axis_index_groups=Y_GROUPS)]
    all_to_all x0 -> x1, blocking collectives: none -> 18.1 us  [to_all(): return lax.all_to_all(copies, 'dp', 0, 0, axis_index_groups=groups)]
    ppermute x3 -> x0, starting transfers between devices: 17.6 us -> none  [along_z(): return lax.ppermute(value, 'dp', pairs)]
    all_gather x1 -> x0, waiting for transfers between devices: 14 us -> none  [gathered_weight(): whole = lax.all_gather(square, 'dp', axis=0, axis_index_groups=X_GROUPS)]
    ppermute x9 -> x11, starting transfers between devices: 23.8 us -> 37.1 us  [swap(): return lax.ppermute(value, axis, [(0, 1), (1, 0)])]
    pallas_call x0 -> x3, Pallas kernels: none -> 12.5 us  [call(): pl.pallas_call(kernel, out_shape=[jax.ShapeDtypeStruct(shape, kind) for s...]
    ppermute x9 -> x11, waiting for transfers between devices: 0.17 us -> 9.78 us  [swap(): return lax.ppermute(value, axis, [(0, 1), (1, 0)])]
    dot_general x5 -> x0, matrix products: 8.36 us -> none  [the longest x3 7.71 us: dot_nn(): lax.dot_general(left, right, (((1,), (0,)), ((), ())), preferred_element_...]
  transfers between devices with their start and end apart: 19 -> 18, of which waited for: 6 -> 7; matrix products, arithmetic and copies ran while one was open for 11% -> 15% of each run, Pallas kernels for 0% -> 1%
where the time goes in v2:
time: 176 us; the launch traced here: 174 us
  starting transfers between devices  70.6 us (40%)
  local copies, waits for them, and re-layouts  30.9 us (18%)
  waiting for transfers between devices  25.5 us (14%)
  blocking collectives  18.1 us (10%)
  Pallas kernels  12.5 us (7%)
  other arithmetic  10.7 us (6%)
  matrix products  3.24 us (2%)
  between operations  2.49 us (1%)
    ppermute x11, starting transfers between devices, swap(): return lax.ppermute(value, axis, [(0, 1), (1, 0)])  37.1 us
    all_to_all x1, blocking collectives, to_all(): return lax.all_to_all(copies, 'dp', 0, 0, axis_index_groups=groups)  18.1 us
    ppermute x4, starting transfers between devices, z_transposed(): return lax.ppermute(value, EVERY, pairs)  18 us
    pallas_call x3, Pallas kernels, call(): pl.pallas_call(kernel, out_shape=[jax.ShapeDtypeStruct(shape, kind) for s...  12.5 us
    all_to_all x2, starting transfers between devices, to_all(): return lax.all_to_all(copies, 'dp', 0, 0, axis_index_groups=groups)  11.6 us
    unnamed x43, local copies, waits for them, and re-layouts  9.99 us
    ppermute x11, waiting for transfers between devices, swap(): return lax.ppermute(value, axis, [(0, 1), (1, 0)])  9.78 us
    all_to_all x2, waiting for transfers between devices, to_all(): return lax.all_to_all(copies, 'dp', 0, 0, axis_index_groups=groups)  5.9 us
  transfers between devices with their start and end apart: 18, of which 7 were waited for; matrix products, arithmetic and copies ran while one was open for 15% of the time, Pallas kernels for 1%

profile of v2, /device:TPU:1, one launch (start us, length us, event | category | flops | bytes accessed | tf_op | source)
XLA Modules:
  0.0 174.1 jit_solution(15395329686239938751)
XLA Ops:
  2.0 18.1 %all_to_all.20 = bf16[4,19,608]{2,1,0:T(8,128)(2,1)S(1)} all-to-all(bf16[4,19,608]{2,1,0:T(8,128)(2,1)S(1)} %broadcast_in_dim.20), channel_id=1, replica_groups={{0,64,128,192},{2,66,130,194},{4,68,132,196},{6,70,134,198},{8,72,136,2..., dimensions={0} | all-to-all | bytes 184832 | tf_op jit(solution)/shard_map/all_to_all | solution.py:70
  20.2 1.0 broadcast_in_dim.21
  21.2 6.8 %all-to-all-start.1 = ((bf16[8,76,608]{2,1,0:T(8,128)(2,1)}), bf16[8,76,608]{2,1,0:T(8,128)(2,1)S(1)}, u32[]{:S(2)}, u32[]{:S(2)}) async-start(bf16[8,76,608]{2,1,0:T(8,128)(2,1)} %broadcast_in_dim.21), calls=%async_computation.1 | async-start | bytes 1638400 | tf_op jit(solution)/shard_map/all_to_all | solution.py:70
  29.2 3.1 %collective-permute-start = (bf16[2432,128]{1,0:T(8,128)(2,1)S(1)}, bf16[2432,128]{1,0:T(8,128)(2,1)S(1)}, u32[]{:S(2)}, u32[]{:S(2)}) collective-permute-start(bf16[2432,128]{1,0:T(8,128)(2,1)S(1)} %bitcast.67), channel_id=1, source_target_pairs={{0,1},{1,0},{2,3},{3,2},{4,5},{5,4},{6,7},{7,6},{8,9},{9,8},{10,11... | collective-permute-start | bytes 1867784 | tf_op jit(solution)/shard_map/ppermute | solution.py:28
  32.2 4.3 %collective-permute-start.1 = (bf16[2432,128]{1,0:T(8,128)(2,1)S(1)}, bf16[2432,128]{1,0:T(8,128)(2,1)S(1)}, u32[]{:S(2)}, u32[]{:S(2)}) collective-permute-start(bf16[2432,128]{1,0:T(8,128)(2,1)S(1)} %bitcast.68), channel_id=1, source_target_pairs={{0,256},{256,0},{1,257},{257,1},{2,258},{258,2},{3,259},{259,3},{4... | collective-permute-start | bytes 1867784 | tf_op jit(solution)/shard_map/ppermute | solution.py:28
  36.5 7.2 %collective-permute-done.seq = bf16[2432,128]{1,0:T(8,128)(2,1)S(1)} collective-permute-done((bf16[2432,128]{1,0:T(8,128)(2,1)S(1)}, bf16[2432,128]{1,0:T(8,128)(2,1)S(1)}, u32[]{:S(2)}, u32[]{:S(2)}) %collective-permute-start) | collective-permute-done | bytes 622624 | tf_op jit(solution)/shard_map/ppermute | solution.py:28
  43.7 5.9 %all-to-all-done.1 = bf16[8,76,608]{2,1,0:T(8,128)(2,1)S(1)} async-done(((bf16[8,76,608]{2,1,0:T(8,128)(2,1)}), bf16[8,76,608]{2,1,0:T(8,128)(2,1)S(1)}, u32[]{:S(2)}, u32[]{:S(2)}) %all-to-all-start.1) | async-done | bytes 739360 | tf_op jit(solution)/shard_map/all_to_all | solution.py:70
  49.9 1.3 reshape.101
  51.2 3.1 %broadcast_in_dim.22 = bf16[4,608,608]{2,1,0:T(8,128)(2,1)} broadcast(bf16[608,608]{1,0:T(8,128)(2,1)} %reshape.101), dimensions={1,2} | broadcast | bytes 3696640 | tf_op jit(solution)/shard_map/broadcast_in_dim | solution.py:69
  54.3 4.8 %all-to-all-start.2 = ((bf16[4,608,608]{2,1,0:T(8,128)(2,1)}), bf16[4,608,608]{2,1,0:T(8,128)(2,1)}, u32[]{:S(2)}, u32[]{:S(2)}) async-start(bf16[4,608,608]{2,1,0:T(8,128)(2,1)} %broadcast_in_dim.22), calls=%async_computation.2 | async-start | bytes 6225920 | tf_op jit(solution)/shard_map/all_to_all | solution.py:70
  59.9 5.1 %collective-permute-start.3 = (bf16[128,1216]{1,0:T(8,128)(2,1)S(1)}, bf16[128,1216]{1,0:T(8,128)(2,1)}, u32[]{:S(2)}, u32[]{:S(2)}) collective-permute-start(bf16[128,1216]{1,0:T(8,128)(2,1)S(1)} %dynamic-slice_bitcast_fusion), channel_id=1, source_target_pairs={{0,256},{256,0},{1,257},{257,1},{2,258},{258,2},{3,259},{259,3},{4... | collective-permute-start | bytes 933896 | tf_op jit(solution)/shard_map/ppermute | solution.py:28
  65.7 1.9 %collective-permute-start.5 = (f32[2432]{0:T(1024)}, f32[2432]{0:T(1024)}, u32[]{:S(2)}, u32[]{:S(2)}) collective-permute-start(f32[2432]{0:T(1024)} %fusion.15), channel_id=1, source_target_pairs={{0,256},{256,0},{1,257},{257,1},{2,258},{258,2},{3,259},{259,3},{4... | collective-permute-start | bytes 29192 | tf_op jit(solution)/shard_map/ppermute | solution.py:28
  68.4 1.6 constant_dynamic-slice_fusion.1
  70.0 1.7 fusion.3
  71.7 2.4 %collective-permute-start.2 = (bf16[2432,128]{1,0:T(8,128)(2,1)S(1)}, bf16[2432,128]{1,0:T(8,128)(2,1)S(1)}, u32[]{:S(2)}, u32[]{:S(2)}) collective-permute-start(bf16[2432,128]{1,0:T(8,128)(2,1)S(1)} %collective-permute-done.seq), channel_id=1, source_target_pairs={{0,256},{256,0},{1,257},{257,1},{2,258},{258,2},{3,259},{259,3},{4... | collective-permute-start | bytes 1867784 | tf_op jit(solution)/shard_map/ppermute | solution.py:28
  76.0 3.0 %collective-permute-start.4 = (f32[608,128]{1,0:T(8,128)}, f32[608,128]{1,0:T(8,128)}, u32[]{:S(2)}, u32[]{:S(2)}) collective-permute-start(f32[608,128]{1,0:T(8,128)} %bitcast.86), channel_id=1, source_target_pairs={{0,1},{1,0},{2,3},{3,2},{4,5},{5,4},{6,7},{7,6},{8,9},{9,8},{10,11... | collective-permute-start | bytes 933896 | tf_op jit(solution)/shard_map/ppermute | solution.py:28
  80.5 1.9 %copy.50 = bf16[4,4,152,128]{3,2,0,1:T(8,128)(2,1)} copy(bf16[4,4,152,128]{3,2,1,0:T(8,128)(2,1)} %bitcast.85) | data formatting | bytes 1245184 | tf_op jit(solution)/shard_map/reshape | solution.py:227
  84.2 1.9 %copy.51 = f32[1,608,128]{2,1,0:T(8,128)} copy(f32[1,608,128]{1,2,0:T(8,128)} %get-tuple-element.43) | data formatting | bytes 622592 | tf_op jit(solution)/shard_map/jit(dynamic_index_in_dim)/dynamic_slice | solution.py:209
  86.1 1.1 collective-permute-done.4.lift_far
  87.2 1.0 copy-done.1
  88.2 1.1 copy-done.3
  91.1 1.8 %shard_map.130 = (bf16[128,512]{1,0:T(8,128)(2,1)S(1)}, f32[608,256]{1,0:T(8,128)S(1)}) custom-call(bf16[2432,128]{1,0:T(8,128)(2,1)S(1)} %bitcast.69, bf16[2432,128]{1,0:T(8,128)(2,1)S(1)} %collective-permute-done.seq, bf16[2432,128]{1,0:T(8,128)(2,1)S(1)} %collective-permute-done.1.branch, bf16[2432,128]{1,0:T(8,128)(2,1)S(1)} %collective-permute-done.2.both, ...), custom_call_target="tpu_custom_call" | custom-call | flops 398458880 | bytes 8000000 | tf_op jit(solution)/shard_map/pallas_call | solution.py:97
  93.8 1.0 copy-done.2
  95.6 1.1 copy-done.11
  96.7 5.2 %shard_map.131 = (bf16[608,512]{1,0:T(8,128)(2,1)S(1)}, f32[128,512]{1,0:T(8,128)S(1)}) custom-call(bf16[2432,128]{1,0:T(8,128)(2,1)S(1)} %bitcast.70, bf16[2432,128]{1,0:T(8,128)(2,1)S(1)} %collective-permute-done.seq, bf16[2432,128]{1,0:T(8,128)(2,1)S(1)} %collective-permute-done.1.branch, bf16[2432,128]{1,0:T(8,128)(2,1)S(1)} %collective-permute-done.2.both, ...), custom_call_target="tpu_custom_call" | custom-call | flops 1514143744 | bytes 8000000 | tf_op jit(solution)/shard_map/pallas_call | solution.py:97
  101.9 5.6 %collective-permute-start.6 = (bf16[128,512]{1,0:T(8,128)(2,1)S(1)}, bf16[128,512]{1,0:T(8,128)(2,1)S(1)}, u32[]{:S(2)}, u32[]{:S(2)}) collective-permute-start(bf16[128,512]{1,0:T(8,128)(2,1)S(1)} %convert_element_type.81), channel_id=1, source_target_pairs={{0,256},{256,0},{1,257},{257,1},{2,258},{258,2},{3,259},{259,3},{4... | collective-permute-start | bytes 393224 | tf_op jit(solution)/shard_map/ppermute | solution.py:28
  109.8 5.6 %shard_map.132 = (f32[2432,128]{1,0:T(8,128)S(1)}, f32[2432,128]{1,0:T(8,128)S(1)}, bf16[2432,128]{1,0:T(8,128)(2,1)}, bf16[2432,128]{1,0:T(8,128)(2,1)}) custom-call(bf16[608,512]{1,0:T(8,128)(2,1)S(1)} %get-tuple-element.26.before, bf16[2432,608]{1,0:T(8,128)(2,1)} %bitcast.7.weight, f32[128,512]{1,0:T(8,128)S(1)} %get-tuple-element.24.low, ...), custom_call_target="tpu_custom_call" | custom-call | flops 1832910848 | bytes 8000000 | tf_op jit(solution)/shard_map/pallas_call | solution.py:97
  115.4 2.0 %collective-permute-start.8 = (bf16[2432,128]{1,0:T(8,128)(2,1)}, bf16[2432,128]{1,0:T(8,128)(2,1)}, u32[]{:S(2)}, u32[]{:S(2)}) collective-permute-start(bf16[2432,128]{1,0:T(8,128)(2,1)} %get-tuple-element.30), channel_id=1, source_target_pairs={{0,256},{256,0},{1,257},{257,1},{2,258},{258,2},{3,259},{259,3},{4... | collective-permute-start | bytes 1867784 | tf_op jit(solution)/shard_map/ppermute | solution.py:28
  117.4 2.4 %collective-permute-start.7 = (bf16[2432,128]{1,0:T(8,128)(2,1)}, bf16[2432,128]{1,0:T(8,128)(2,1)}, u32[]{:S(2)}, u32[]{:S(2)}) collective-permute-start(bf16[2432,128]{1,0:T(8,128)(2,1)} %get-tuple-element.28), channel_id=1, source_target_pairs={{0,256},{256,0},{1,257},{257,1},{2,258},{258,2},{3,259},{259,3},{4... | collective-permute-start | bytes 1867784 | tf_op jit(solution)/shard_map/ppermute | solution.py:28
  119.8 4.1 %collective-permute-start.10 = (bf16[128,512]{1,0:T(8,128)(2,1)}, bf16[128,512]{1,0:T(8,128)(2,1)}, u32[]{:S(2)}, u32[]{:S(2)}) collective-permute-start(bf16[128,512]{1,0:T(8,128)(2,1)} %fusion.16), channel_id=1, source_target_pairs={{0,1},{1,0},{2,3},{3,2},{4,5},{5,4},{6,7},{7,6},{8,9},{9,8},{10,11... | collective-permute-start | bytes 393224 | tf_op jit(solution)/shard_map/ppermute | solution.py:28
  124.0 1.0 fusion.1
  125.0 1.6 stack.22
  126.6 1.5 collective-permute-done.10
  129.0 2.3 %fusion = bf16[608,128]{1,0:T(8,128)(2,1)} fusion(bf16[608,128]{1,0:T(8,128)(2,1)} %bitcast.90, bf16[608,128]{1,0:T(8,128)(2,1)} %bitcast.89, bf16[608,128]{1,0:T(8,128)(2,1)} %bitcast.88, bf16[608,128]{1,0:T(8,128)(2,1)} %bitcast.87, f32[128,128]{1,0:T(8,128)S(1)} %get-tuple-element.49, f32[128,128]{1,0:T(8,128)S(1)} %get-tuple-element.48, ...), kind=kOutput, calls=%fused_computation.4 | convolution fusion | flops 82796544 | bytes 1564672 | tf_op jit(solution)/shard_map/dot_general | solution.py:51
  131.2 1.0 stack.21
  132.2 1.0 maximum_bitcast_fusion
  134.1 3.9 %all-to-all-start.3 = ((bf16[32,38,128]{2,1,0:T(8,128)(2,1)}), bf16[32,38,128]{2,1,0:T(8,128)(2,1)S(1)}, u32[]{:S(2)}, u32[]{:S(2)}) async-start(bf16[32,38,128]{2,1,0:T(8,128)(2,1)} %copy.59), calls=%async_computation.3 | async-start | bytes 655360 | tf_op jit(solution)/shard_map/all_to_all | solution.py:250
  138.0 2.0 %add_convert_fusion.1 = bf16[2432,128]{1,0:T(8,128)(2,1)} fusion(f32[2432,128]{1,0:T(8,128)S(1)} %get-tuple-element.29, bf16[2432,128]{1,0:T(8,128)(2,1)} %collective-permute-done.8), kind=kLoop, calls=%fused_computation.1 | loop fusion | flops 933888 | bytes 2490368 | tf_op jit(solution)/shard_map/convert_element_type | solution.py:256
  140.0 3.1 %collective-permute-start.9 = (bf16[2432,128]{1,0:T(8,128)(2,1)}, bf16[2432,128]{1,0:T(8,128)(2,1)S(1)}, u32[]{:S(2)}, u32[]{:S(2)}) collective-permute-start(bf16[2432,128]{1,0:T(8,128)(2,1)} %add_convert_fusion.1), channel_id=1, source_target_pairs={{0,1},{1,0},{2,3},{3,2},{4,5},{5,4},{6,7},{7,6},{8,9},{9,8},{10,11... | collective-permute-start | bytes 1867784 | tf_op jit(solution)/shard_map/ppermute | solution.py:28
  143.2 5.4 %all-to-all-done.3 = bf16[32,38,128]{2,1,0:T(8,128)(2,1)S(1)} async-done(((bf16[32,38,128]{2,1,0:T(8,128)(2,1)}), bf16[32,38,128]{2,1,0:T(8,128)(2,1)S(1)}, u32[]{:S(2)}, u32[]{:S(2)}) %all-to-all-start.3) | async-done | bytes 311328 | tf_op jit(solution)/shard_map/all_to_all | solution.py:250
  148.6 4.7 %collective-permute-start.13 = (f32[38,128]{1,0:T(8,128)S(1)}, f32[38,128]{1,0:T(8,128)S(1)}, u32[]{:S(2)}, u32[]{:S(2)}) collective-permute-start(f32[38,128]{1,0:T(8,128)S(1)} %convert_reduce_fusion), channel_id=1, source_target_pairs={{0,256},{1,320},{256,384},{257,448},{2,258},{3,322},{258,386},{259... | collective-permute-start | bytes 58376 | tf_op jit(solution)/shard_map/ppermute | solution.py:84
  153.3 7.1 %collective-permute-start.14 = (f32[38,128]{1,0:T(8,128)S(1)}, f32[38,128]{1,0:T(8,128)S(1)}, u32[]{:S(2)}, u32[]{:S(2)}) collective-permute-start(f32[38,128]{1,0:T(8,128)S(1)} %convert_reduce_fusion), channel_id=1, source_target_pairs={{0,257},{1,321},{256,385},{257,449},{2,259},{3,323},{258,387},{259... | collective-permute-start | bytes 58376 | tf_op jit(solution)/shard_map/ppermute | solution.py:84
  160.5 3.4 %collective-permute-start.11 = (f32[38,128]{1,0:T(8,128)S(1)}, f32[38,128]{1,0:T(8,128)S(1)}, u32[]{:S(2)}, u32[]{:S(2)}) collective-permute-start(f32[38,128]{1,0:T(8,128)S(1)} %convert_reduce_fusion), channel_id=1, source_target_pairs={{0,0},{1,64},{256,128},{257,192},{2,2},{3,66},{258,130},{259,194},... | collective-permute-start | bytes 58376 | tf_op jit(solution)/shard_map/ppermute | solution.py:84
  163.9 2.7 %collective-permute-start.12 = (f32[38,128]{1,0:T(8,128)S(1)}, f32[38,128]{1,0:T(8,128)S(1)}, u32[]{:S(2)}, u32[]{:S(2)}) collective-permute-start(f32[38,128]{1,0:T(8,128)S(1)} %convert_reduce_fusion), channel_id=1, source_target_pairs={{0,1},{1,65},{256,129},{257,193},{2,3},{3,67},{258,131},{259,195},... | collective-permute-start | bytes 58376 | tf_op jit(solution)/shard_map/ppermute | solution.py:84
  166.6 2.9 %collective-permute-done.11 = f32[38,128]{1,0:T(8,128)S(1)} collective-permute-done((f32[38,128]{1,0:T(8,128)S(1)}, f32[38,128]{1,0:T(8,128)S(1)}, u32[]{:S(2)}, u32[]{:S(2)}) %collective-permute-start.11) | collective-permute-done | bytes 19488 | tf_op jit(solution)/shard_map/ppermute | solution.py:84
  169.5 1.6 collective-permute-done.12
  171.7 1.3 add_convert_fusion
  173.1 1.1 copy.60
  (82 shorter events, 17.1 us)
Async XLA Ops:
  0.6 78.4 %copy-start = (bf16[2432,128]{1,0:T(8,128)(2,1)S(1)}, bf16[2432,128]{1,0:T(8,128)(2,1)}, u32[]{:S(2)}) copy-start(bf16[2432,128]{1,0:T(8,128)(2,1)} %param.18) | copy-start | bytes 1867780
  0.6 1.0 copy-start.17
  20.2 7.8 %copy-start.14 = (bf16[1,128,2432]{2,1,0:T(8,128)(2,1)S(1)}, bf16[1,128,2432]{2,1,0:T(8,128)(2,1)}, u32[]{:S(2)}) copy-start(bf16[1,128,2432]{2,1,0:T(8,128)(2,1)} %param.11) | copy-start | bytes 1867780
  21.2 28.4 %all-to-all-start.1 = ((bf16[8,76,608]{2,1,0:T(8,128)(2,1)}), bf16[8,76,608]{2,1,0:T(8,128)(2,1)S(1)}, u32[]{:S(2)}, u32[]{:S(2)}) async-start(bf16[8,76,608]{2,1,0:T(8,128)(2,1)} %broadcast_in_dim.21), calls=%async_computation.1 | async-start | bytes 1638400 | tf_op jit(solution)/shard_map/all_to_all | solution.py:70
  28.3 0.8 copy-start.12
  29.2 14.5 %collective-permute-start = (bf16[2432,128]{1,0:T(8,128)(2,1)S(1)}, bf16[2432,128]{1,0:T(8,128)(2,1)S(1)}, u32[]{:S(2)}, u32[]{:S(2)}) collective-permute-start(bf16[2432,128]{1,0:T(8,128)(2,1)S(1)} %bitcast.67), channel_id=1, source_target_pairs={{0,1},{1,0},{2,3},{3,2},{4,5},{5,4},{6,7},{7,6},{8,9},{9,8},{10,11... | collective-permute-start | bytes 1867784 | tf_op jit(solution)/shard_map/ppermute | solution.py:28
  32.2 11.5 %collective-permute-start.1 = (bf16[2432,128]{1,0:T(8,128)(2,1)S(1)}, bf16[2432,128]{1,0:T(8,128)(2,1)S(1)}, u32[]{:S(2)}, u32[]{:S(2)}) collective-permute-start(bf16[2432,128]{1,0:T(8,128)(2,1)S(1)} %bitcast.68), channel_id=1, source_target_pairs={{0,256},{256,0},{1,257},{257,1},{2,258},{258,2},{3,259},{259,3},{4... | collective-permute-start | bytes 1867784 | tf_op jit(solution)/shard_map/ppermute | solution.py:28
  54.3 5.5 %copy-start.13 = (bf16[1,128,2432]{2,1,0:T(8,128)(2,1)S(1)}, bf16[1,128,2432]{2,1,0:T(8,128)(2,1)}, u32[]{:S(2)}) copy-start(bf16[1,128,2432]{2,1,0:T(8,128)(2,1)} %param.12) | copy-start | bytes 1867780
  54.3 10.8 %copy-start.18 = (f32[1,8,2432]{2,1,0:T(8,128)S(1)}, f32[1,8,2432]{2,1,0:T(8,128)}, u32[]{:S(2)}) copy-start(f32[1,8,2432]{2,1,0:T(8,128)} %param.19) | copy-start | bytes 233476
  54.3 39.5 %all-to-all-start.2 = ((bf16[4,608,608]{2,1,0:T(8,128)(2,1)}), bf16[4,608,608]{2,1,0:T(8,128)(2,1)}, u32[]{:S(2)}, u32[]{:S(2)}) async-start(bf16[4,608,608]{2,1,0:T(8,128)(2,1)} %broadcast_in_dim.22), calls=%async_computation.2 | async-start | bytes 6225920 | tf_op jit(solution)/shard_map/all_to_all | solution.py:70
  59.9 10.1 %collective-permute-start.3 = (bf16[128,1216]{1,0:T(8,128)(2,1)S(1)}, bf16[128,1216]{1,0:T(8,128)(2,1)}, u32[]{:S(2)}, u32[]{:S(2)}) collective-permute-start(bf16[128,1216]{1,0:T(8,128)(2,1)S(1)} %dynamic-slice_bitcast_fusion), channel_id=1, source_target_pairs={{0,256},{256,0},{1,257},{257,1},{2,258},{258,2},{3,259},{259,3},{4... | collective-permute-start | bytes 933896 | tf_op jit(solution)/shard_map/ppermute | solution.py:28
  65.7 16.8 %collective-permute-start.5 = (f32[2432]{0:T(1024)}, f32[2432]{0:T(1024)}, u32[]{:S(2)}, u32[]{:S(2)}) collective-permute-start(f32[2432]{0:T(1024)} %fusion.15), channel_id=1, source_target_pairs={{0,256},{256,0},{1,257},{257,1},{2,258},{258,2},{3,259},{259,3},{4... | collective-permute-start | bytes 29192 | tf_op jit(solution)/shard_map/ppermute | solution.py:28
  71.7 15.5 %collective-permute-start.2 = (bf16[2432,128]{1,0:T(8,128)(2,1)S(1)}, bf16[2432,128]{1,0:T(8,128)(2,1)S(1)}, u32[]{:S(2)}, u32[]{:S(2)}) collective-permute-start(bf16[2432,128]{1,0:T(8,128)(2,1)S(1)} %collective-permute-done.seq), channel_id=1, source_target_pairs={{0,256},{256,0},{1,257},{257,1},{2,258},{258,2},{3,259},{259,3},{4... | collective-permute-start | bytes 1867784 | tf_op jit(solution)/shard_map/ppermute | solution.py:28
  76.0 11.2 %collective-permute-start.4 = (f32[608,128]{1,0:T(8,128)}, f32[608,128]{1,0:T(8,128)}, u32[]{:S(2)}, u32[]{:S(2)}) collective-permute-start(f32[608,128]{1,0:T(8,128)} %bitcast.86), channel_id=1, source_target_pairs={{0,1},{1,0},{2,3},{3,2},{4,5},{5,4},{6,7},{7,6},{8,9},{9,8},{10,11... | collective-permute-start | bytes 933896 | tf_op jit(solution)/shard_map/ppermute | solution.py:28
  87.2 1.0 copy-start.1
  88.2 1.1 copy-start.3
  89.2 0.9 copy-start.5
  90.1 1.0 copy-start.7
  92.9 0.8 copy-start.10
  93.8 1.0 copy-start.2
  94.7 0.9 copy-start.6
  95.6 1.1 copy-start.11
  101.9 7.9 %copy-start.8 = (f32[128,512]{1,0:T(8,128)}, f32[128,512]{1,0:T(8,128)S(1)}, u32[]{:S(2)}) copy-start(f32[128,512]{1,0:T(8,128)S(1)} %get-tuple-element.24.low) | copy-start | bytes 786436
  101.9 7.9 %copy-start.4 = (bf16[4,4,152,128]{3,2,0,1:T(8,128)(2,1)S(1)}, bf16[4,4,152,128]{3,2,0,1:T(8,128)(2,1)}, u32[]{:S(2)}) copy-start(bf16[4,4,152,128]{3,2,0,1:T(8,128)(2,1)} %copy.50) | copy-start | bytes 1867780
  101.9 7.1 %collective-permute-start.6 = (bf16[128,512]{1,0:T(8,128)(2,1)S(1)}, bf16[128,512]{1,0:T(8,128)(2,1)S(1)}, u32[]{:S(2)}, u32[]{:S(2)}) collective-permute-start(bf16[128,512]{1,0:T(8,128)(2,1)S(1)} %convert_element_type.81), channel_id=1, source_target_pairs={{0,256},{256,0},{1,257},{257,1},{2,258},{258,2},{3,259},{259,3},{4... | collective-permute-start | bytes 393224 | tf_op jit(solution)/shard_map/ppermute | solution.py:28
  109.0 0.8 copy-start.15
  109.0 0.8 copy-start.16
  115.4 13.6 %copy-start.9 = (f32[128,512]{1,0:T(8,128)S(1)}, f32[128,512]{1,0:T(8,128)}, u32[]{:S(2)}) copy-start(f32[128,512]{1,0:T(8,128)} %copy-done.8) | copy-start | bytes 786436
  115.4 22.6 %collective-permute-start.8 = (bf16[2432,128]{1,0:T(8,128)(2,1)}, bf16[2432,128]{1,0:T(8,128)(2,1)}, u32[]{:S(2)}, u32[]{:S(2)}) collective-permute-start(bf16[2432,128]{1,0:T(8,128)(2,1)} %get-tuple-element.30), channel_id=1, source_target_pairs={{0,256},{256,0},{1,257},{257,1},{2,258},{258,2},{3,259},{259,3},{4... | collective-permute-start | bytes 1867784 | tf_op jit(solution)/shard_map/ppermute | solution.py:28
  117.4 54.3 %collective-permute-start.7 = (bf16[2432,128]{1,0:T(8,128)(2,1)}, bf16[2432,128]{1,0:T(8,128)(2,1)}, u32[]{:S(2)}, u32[]{:S(2)}) collective-permute-start(bf16[2432,128]{1,0:T(8,128)(2,1)} %get-tuple-element.28), channel_id=1, source_target_pairs={{0,256},{256,0},{1,257},{257,1},{2,258},{258,2},{3,259},{259,3},{4... | collective-permute-start | bytes 1867784 | tf_op jit(solution)/shard_map/ppermute | solution.py:28
  119.8 8.3 %collective-permute-start.10 = (bf16[128,512]{1,0:T(8,128)(2,1)}, bf16[128,512]{1,0:T(8,128)(2,1)}, u32[]{:S(2)}, u32[]{:S(2)}) collective-permute-start(bf16[128,512]{1,0:T(8,128)(2,1)} %fusion.16), channel_id=1, source_target_pairs={{0,1},{1,0},{2,3},{3,2},{4,5},{5,4},{6,7},{7,6},{8,9},{9,8},{10,11... | collective-permute-start | bytes 393224 | tf_op jit(solution)/shard_map/ppermute | solution.py:28
  134.1 14.4 %all-to-all-start.3 = ((bf16[32,38,128]{2,1,0:T(8,128)(2,1)}), bf16[32,38,128]{2,1,0:T(8,128)(2,1)S(1)}, u32[]{:S(2)}, u32[]{:S(2)}) async-start(bf16[32,38,128]{2,1,0:T(8,128)(2,1)} %copy.59), calls=%async_computation.3 | async-start | bytes 655360 | tf_op jit(solution)/shard_map/all_to_all | solution.py:250
  140.0 31.7 %collective-permute-start.9 = (bf16[2432,128]{1,0:T(8,128)(2,1)}, bf16[2432,128]{1,0:T(8,128)(2,1)S(1)}, u32[]{:S(2)}, u32[]{:S(2)}) collective-permute-start(bf16[2432,128]{1,0:T(8,128)(2,1)} %add_convert_fusion.1), channel_id=1, source_target_pairs={{0,1},{1,0},{2,3},{3,2},{4,5},{5,4},{6,7},{7,6},{8,9},{9,8},{10,11... | collective-permute-start | bytes 1867784 | tf_op jit(solution)/shard_map/ppermute | solution.py:28
  148.6 15.3 %collective-permute-start.13 = (f32[38,128]{1,0:T(8,128)S(1)}, f32[38,128]{1,0:T(8,128)S(1)}, u32[]{:S(2)}, u32[]{:S(2)}) collective-permute-start(f32[38,128]{1,0:T(8,128)S(1)} %convert_reduce_fusion), channel_id=1, source_target_pairs={{0,256},{1,320},{256,384},{257,448},{2,258},{3,322},{258,386},{259... | collective-permute-start | bytes 58376 | tf_op jit(solution)/shard_map/ppermute | solution.py:84
  153.3 13.3 %collective-permute-start.14 = (f32[38,128]{1,0:T(8,128)S(1)}, f32[38,128]{1,0:T(8,128)S(1)}, u32[]{:S(2)}, u32[]{:S(2)}) collective-permute-start(f32[38,128]{1,0:T(8,128)S(1)} %convert_reduce_fusion), channel_id=1, source_target_pairs={{0,257},{1,321},{256,385},{257,449},{2,259},{3,323},{258,387},{259... | collective-permute-start | bytes 58376 | tf_op jit(solution)/shard_map/ppermute | solution.py:84
  160.5 9.0 %collective-permute-start.11 = (f32[38,128]{1,0:T(8,128)S(1)}, f32[38,128]{1,0:T(8,128)S(1)}, u32[]{:S(2)}, u32[]{:S(2)}) collective-permute-start(f32[38,128]{1,0:T(8,128)S(1)} %convert_reduce_fusion), channel_id=1, source_target_pairs={{0,0},{1,64},{256,128},{257,192},{2,2},{3,66},{258,130},{259,194},... | collective-permute-start | bytes 58376 | tf_op jit(solution)/shard_map/ppermute | solution.py:84
  163.9 7.2 %collective-permute-start.12 = (f32[38,128]{1,0:T(8,128)S(1)}, f32[38,128]{1,0:T(8,128)S(1)}, u32[]{:S(2)}, u32[]{:S(2)}) collective-permute-start(f32[38,128]{1,0:T(8,128)S(1)} %convert_reduce_fusion), channel_id=1, source_target_pairs={{0,1},{1,65},{256,129},{257,193},{2,3},{3,67},{258,131},{259,195},... | collective-permute-start | bytes 58376 | tf_op jit(solution)/shard_map/ppermute | solution.py:84

commit v3 on v1

v3 whole, which is shorter than its diff:
```python
import math

import jax
import jax.numpy as jnp
import numpy as np
from jax import lax
from jax.experimental import pallas as pl
from jax.experimental.pallas import tpu as pltpu
from jax.sharding import PartitionSpec as P

MODEL_WIDTH = 2432
QBLOCK = 128
RANK = 128
STEPS = 28
ZH, XN, YN = 4, 4, 8
PLANE = XN * YN
SLICE = MODEL_WIDTH // 4
ROWS = 19
PADDED = 24
TOK = 128

GUIDE = 4.5
REWARD = 0.08
ADAPTER_STRENGTH = 0.5
SHIFT = 3.0
F32 = jnp.float32
BF16 = jnp.bfloat16
EVERY = ("branch", "dp", "seq")


def swap(value, axis):
    return lax.ppermute(value, axis, [(0, 1), (1, 0)])


def noise_level(step_index):
    frac = step_index[0].astype(F32) / STEPS
    return SHIFT * frac / (1.0 + (SHIFT - 1.0) * frac)


def dequantize(codes, exps):
    count = codes.shape[0]
    block_scale = jnp.exp2(exps.astype(F32))
    grouped = (
        codes.astype(F32).reshape(count, MODEL_WIDTH // QBLOCK, QBLOCK)
        * block_scale[:, :, None]
    )
    return grouped.reshape(count, MODEL_WIDTH).astype(BF16)


def dot_nn(left, right):
    return lax.dot_general(left, right, (((1,), (0,)), ((), ())), preferred_element_type=F32)


def dot_nt(left, right):
    return lax.dot_general(left, right, (((1,), (1,)), ((), ())), preferred_element_type=F32)


def dot_tn(left, right):
    return lax.dot_general(left, right, (((0,), (0,)), ((), ())), preferred_element_type=F32)


def dp_index(z, x, y):
    return z * PLANE + x * YN + y


Z_GROUPS = [[dp_index(z, x, y) for z in range(ZH)] for x in range(XN) for y in range(YN)]
Y_GROUPS = [[dp_index(z, x, y) for y in range(YN)] for z in range(ZH) for x in range(XN)]
XY_GROUPS = [[z * PLANE + i for i in range(PLANE)] for z in range(ZH)]


def to_all(value, groups):
    copies = jnp.broadcast_to(value, (len(groups[0]),) + value.shape)
    return lax.all_to_all(copies, "dp", 0, 0, axis_index_groups=groups)


def along_x(value, by):
    pairs = []
    for z in range(ZH):
        for x in range(XN):
            for y in range(YN):
                pairs.append((dp_index(z, x, y), dp_index(z, (x + by) % XN, y)))
    return lax.ppermute(value, "dp", pairs)


def place(branch, dp, seq):
    return (branch * ZH * PLANE + dp) * 2 + seq


def z_transposed(value, flip):
    pairs = []
    for z in range(ZH):
        for i in range(PLANE):
            for q in range(4):
                r = z ^ flip
                pairs.append((place(q // 2, z * PLANE + i, q % 2), place(r // 2, q * PLANE + i, r % 2)))
    return lax.ppermute(value, EVERY, pairs)


def own_columns(codes, exps, q):
    local = dequantize(codes, exps).reshape(ROWS, 4, SLICE)
    return lax.dynamic_index_in_dim(local, q, 1, keepdims=False)


SPREAD = np.zeros((PLANE * PADDED, SLICE), np.float32)
for _i in range(PLANE):
    for _j in range(ROWS):
        SPREAD[PADDED * _i + _j, ROWS * _i + _j] = 1.0


def x_block(ref, x):
    return ref[:, x].astype(F32).reshape(SLICE, ref.shape[-1]).astype(BF16)


def call(kernel, outs, flops, *args, places=None, **more):
    specs = [pl.BlockSpec(memory_space=pltpu.VMEM)] * len(args)
    if places is not None:
        args, specs = (places,) + args, [pl.BlockSpec(memory_space=pltpu.SMEM)] + specs
    more = more or dict(in_specs=specs)
    moved = sum(a.size * a.dtype.itemsize for a in args)
    moved += sum(math.prod(shape) * jnp.dtype(kind).itemsize for shape, kind in outs)
    return pl.pallas_call(
        kernel,
        out_shape=[jax.ShapeDtypeStruct(shape, kind) for shape, kind in outs],
        compiler_params=pltpu.CompilerParams(vmem_limit_bytes=24 * 2**20),
        cost_estimate=pl.CostEstimate(flops=flops, bytes_accessed=moved, transcendentals=0),
        **more,
    )(*args)


def features(places, own, other, down, rows, low_rank):
    low = jnp.zeros((2 * TOK, RANK), F32)
    for c in range(XN):
        part = jnp.concatenate([x_block(ref, places[c]).T for ref in (own, other)], 0)
        rows[c] = part
        low = low + dot_nn(part, x_block(down, places[c]))
    low_rank[...] = low.astype(BF16)


def far_kernel(places, own, other, down, near_rank, up, lift, far_lift, a_own, a_other, rows, low_rank, base, far_base):
    features(places, own, other, down, rows, low_rank)
    for rank, source, out in ((near_rank, lift, base), (low_rank, far_lift, far_base)):
        adapted = ADAPTER_STRENGTH * dot_nt(rank[...], up[...])
        out[...] = source[...] - a_own[...] * adapted[:TOK] - a_other[...] * adapted[TOK:]


def piece(upper, lower):
    return jnp.concatenate([upper[...], lower[...]], 0)


def near_kernel(rows, far_rows, *refs):
    weights, product = refs[:-1], refs[-1]
    for i, ref in enumerate((rows, far_rows)):
        total = dot_nn(ref[0], piece(*weights[:2]))
        for c in range(1, XN - 1):
            total = total + dot_nn(ref[c], piece(*weights[2 * c:2 * c + 2]))
        product[2 * TOK * i:2 * TOK * (i + 1)] = total


def forward_kernel(product, rows, far_rows, upper, lower, base, far_base, a_own, a_other, up, before, low):
    weight = piece(upper, lower)
    first, second = a_own[...], a_other[...]
    for i, (ref, lift) in enumerate(((rows, base), (far_rows, far_base))):
        part = slice(2 * TOK * i, 2 * TOK * (i + 1))
        whole = product[part] + dot_nn(ref[XN - 1], weight)
        reward_grad = REWARD * (lift[...] - first * whole[:TOK] - second * whole[TOK:])
        grad = jnp.concatenate([first * reward_grad, second * reward_grad], 0).astype(BF16)
        before[part] = grad
        low[part] = dot_nn(grad, up[...])


def backward_kernel(places, before, low, down, *refs):
    weights, (keep, send) = refs[:-2], refs[-2:]
    before_t = before[...].T
    low_t = low[...].astype(BF16).T
    for c in range(XN):
        part = dot_nn(piece(*weights[2 * c:2 * c + 2]), before_t)
        part = part + ADAPTER_STRENGTH * dot_nn(x_block(down, places[c]), low_t)
        for out, start in ((keep, 0), (send, TOK)):
            both = jnp.concatenate([part[:, start:start + TOK], part[:, start + 2 * TOK:start + 3 * TOK]], 1)
            out[:, places[c]] = both.reshape(ZH, YN * ROWS, 2 * TOK).astype(BF16)


def join_kernel(keep, got, home, cross):
    both = keep[...].astype(F32) + got[...].astype(F32)
    home[...] = both[..., :TOK]
    cross[...] = both[..., TOK:].astype(BF16)


def finish_kernel(home, across, grad):
    grad[...] = (home[...].reshape(MODEL_WIDTH, TOK) + across[...].astype(F32).reshape(MODEL_WIDTH, TOK)).T.astype(BF16)


def terms_kernel(quarter, pair, far, up, spread, *refs):
    tokens, terms = refs[:-1], refs[-1]
    far = far[...].astype(F32)
    low = (pair[...] + jnp.concatenate([far[2 * TOK:], far[:2 * TOK]], 0)).astype(BF16)
    columns = jnp.concatenate([ref[0] for ref in tokens], 1)
    down = (ADAPTER_STRENGTH * dot_nn(columns, low)).astype(BF16)
    both = dot_nn(spread[...], jnp.concatenate([down, up[...]], 1))
    first = both[:, :RANK].reshape(PLANE, PADDED, RANK)
    second = pltpu.roll(both[:, RANK:], ROWS - 16, 0).reshape(PLANE, PADDED, RANK)
    middle = first[:, 16:] + second[:, :8]
    terms[...] = jnp.concatenate([first[:, :16], middle, second[:, 8:]], 1).astype(BF16)


def by_x(value):
    return value.reshape(ZH, XN, YN * ROWS, value.shape[-1])


def terms_of(q, pair, far, up, tokens):
    whole = lambda *shape: pl.BlockSpec(shape, lambda n, quarter: (0,) * len(shape))
    return pl.pallas_call(
        terms_kernel,
        out_shape=jax.ShapeDtypeStruct((PLANE, 40, RANK), BF16),
        grid_spec=pltpu.PrefetchScalarGridSpec(
            num_scalar_prefetch=1,
            grid=(1,),
            in_specs=[whole(4 * TOK, RANK), whole(4 * TOK, RANK), whole(SLICE, RANK), whole(PLANE * PADDED, SLICE)]
            + [pl.BlockSpec((1, SLICE, TOK), lambda n, quarter: (quarter[0], 0, 0))] * 4,
            out_specs=whole(PLANE, 40, RANK),
        ),
        compiler_params=pltpu.CompilerParams(vmem_limit_bytes=24 * 2**20),
        cost_estimate=pl.CostEstimate(flops=2 * 512 * 768 * 128, bytes_accessed=3 * 10**6, transcendentals=0),
    )(q.astype(jnp.int32)[None], pair, far, up, jnp.asarray(SPREAD, BF16), *tokens)


def backward(places, before, low, down, weights):
    shape = (ZH, XN, YN * ROWS, 2 * TOK)
    return call(
        backward_kernel, [(shape, BF16), (shape, BF16)], 2 * 512 * 2432 * 736,
        before, low, by_x(down), *weights, places=places,
    )


def per_device(
    attn,
    hidden,
    noisy,
    target,
    quantized_weight_codes,
    weight_exponents,
    adapter_down_map,
    adapter_up_transposed,
    gates,
    group_prompt,
    step_index,
):
    b = lax.axis_index("branch")
    s = lax.axis_index("seq")
    q = 2 * b + s
    level = noise_level(step_index)
    is_first = b == 0
    mine = own_columns(quantized_weight_codes, weight_exponents, q)
    plane = to_all(mine, Z_GROUPS).reshape(ZH * ROWS, SLICE)
    plane, hidden = lax.optimization_barrier((plane, hidden))
    lined = to_all(plane, Y_GROUPS)

    own = attn[0].T
    from_seq = swap(own, "seq")
    from_branch = swap(own, "branch")
    x = (lax.axis_index("dp") // YN) % XN
    places = jnp.stack([(x + k) % XN for k in (0, XN - 1, 1, 2)]).astype(jnp.int32)
    ranks = [((XN, 2 * TOK, SLICE), BF16), ((2 * TOK, RANK), BF16)]
    rows, low_rank = call(features, ranks, 0, by_x(own), by_x(from_branch), by_x(adapter_down_map), places=places)

    selector = (jnp.arange(gates.shape[1], dtype=jnp.int32) == group_prompt[0]).astype(F32)
    gate_row = jnp.sum(selector[:, None] * gates[0], axis=0)
    gate_other = swap(gate_row, "branch")
    hid_other = swap(lax.dynamic_slice_in_dim(hidden[0], (1 - b) * 2 * SLICE, 2 * SLICE, 1), "branch")
    lined, from_seq, rows, low_rank, gate_other, hid_other = lax.optimization_barrier(
        (lined, from_seq, rows, low_rank, gate_other, hid_other)
    )

    square = lined.reshape(YN, ZH, ROWS, SLICE).transpose(1, 0, 2, 3).reshape(SLICE, SLICE)
    square = lax.optimization_barrier(square)
    here = [square[:SLICE // 2], square[SLICE // 2:]]
    here[0], here[1], from_seq, hid_other = lax.optimization_barrier((here[0], here[1], from_seq, hid_other))
    left = [along_x(here[0], 1), along_x(here[1], 1)]
    right = [along_x(here[0], -1), along_x(here[1], -1)]

    c_own = jnp.where(is_first, F32(GUIDE), F32(1.0 - GUIDE))
    c_other = jnp.where(is_first, F32(1.0 - GUIDE), F32(GUIDE))
    half = lambda v, i: lax.dynamic_slice_in_dim(v, i * 2 * SLICE, 2 * SLICE, 1).astype(F32)
    lift = half(target, b) - half(noisy, b) + level * (c_own * half(hidden[0], b) + c_other * hid_other.astype(F32))
    lift = jnp.stack([lift[:, :SLICE], lift[:, SLICE:]])
    take = lambda i: lax.dynamic_index_in_dim(lift, i, 0, keepdims=False)
    lift_near = take(s)
    lift_far = take(1 - s)

    cut = lambda v: lax.dynamic_slice_in_dim(v, q * SLICE, SLICE, 0)
    a_own = (-level * c_own * cut(gate_row))[None]
    a_other = (-level * c_other * cut(gate_other))[None]
    up_slice = cut(adapter_up_transposed)
    lift_far = swap(lift_far, "seq")
    from_both = swap(from_seq, "branch")
    opposite = [along_x(left[0], 1), along_x(right[1], -1)]
    near_weights = here + left + right
    far_rows, far_low_rank, base, far_base = call(
        far_kernel,
        ranks + [((TOK, SLICE), F32)] * 2,
        2 * 256 * 128 * 3600,
        by_x(from_seq), by_x(from_both), by_x(adapter_down_map), low_rank, up_slice, lift_near, lift_far, a_own, a_other,
        places=places,
    )
    product = call(
        near_kernel, [((4 * TOK, SLICE), F32)], 2 * 512 * 1824 * 608, rows, far_rows, *near_weights,
    )[0]
    before, low_part = call(
        forward_kernel,
        [((4 * TOK, SLICE), BF16), ((4 * TOK, RANK), F32)],
        2 * 512 * 608 * 736,
        product, rows, far_rows, *opposite, base, far_base, a_own, a_other, up_slice,
    )

    blocks = lambda v, *which: jnp.concatenate([v[i * TOK:(i + 1) * TOK] for i in which], 0)
    from_core = swap(low_part.astype(BF16), "branch").astype(F32)
    pair = low_part + blocks(from_core, 1, 0, 3, 2)
    from_chip = swap(pair.astype(BF16), "seq")
    term_up = (ADAPTER_STRENGTH * dot_tn(before, jnp.concatenate([low_rank, far_low_rank], 0))).astype(BF16)
    tokens = [v.reshape(ZH, SLICE, TOK) for v in (own, from_branch, from_seq, from_both)]
    terms = terms_of(q, pair, from_chip, term_up, tokens)
    keep, send = backward(places, before, low_part, adapter_down_map, near_weights + opposite)
    terms, send, keep = lax.optimization_barrier((terms, send, keep))
    spread = lax.all_to_all(terms, "dp", 0, 0, axis_index_groups=XY_GROUPS)
    plane_sum = jnp.sum(spread.astype(F32), axis=0)
    total = z_transposed(plane_sum, 0) + z_transposed(plane_sum, 1)
    total = total + swap(total, "branch")

    shape = (ZH, XN, YN * ROWS, TOK)
    home, cross = call(join_kernel, [(shape, F32), (shape, BF16)], 2 * 2432 * 256, keep, swap(send, "branch"))
    grad = call(finish_kernel, [((TOK, MODEL_WIDTH), BF16)], 2432 * 128, home, swap(cross, "seq"))[0]
    return (grad[None], total[:ROWS], total[ROWS:2 * ROWS])


def solution(mesh):
    return jax.shard_map(
        per_device,
        mesh=mesh,
        in_specs=(
            P("branch", ("dp", "seq"), None),
            P("branch", ("dp", "seq"), None),
            P(("dp", "seq"), None),
            P(("dp", "seq"), None),
            P("dp", None),
            P("dp", None),
            P(),
            P(),
            P("branch", None, None),
            P("dp"),
            P(),
        ),
        out_specs=(P("branch", ("dp", "seq"), None), P("dp", None), P("dp", None)),
        check_vma=False,
    )
```

time: 188 us -> 155 us (0.82)
  Pallas kernels: 0 us -> 17.9 us
  matrix products: 15.1 us -> 0.38 us
  between operations: 16 us -> 2.66 us
  waiting for transfers between devices: 26 us -> 14.6 us
  starting transfers between devices: 84.7 us -> 75.5 us
  local copies, waits for them, and re-layouts: 13.5 us -> 19.9 us
  other arithmetic: 9.08 us -> 3.88 us
  blocking collectives: 22.8 us -> 18.1 us
    all_gather x1 -> x0, blocking collectives: 22.8 us -> none  [gathered_weight(): lined = lax.all_gather(ordered, 'dp', axis=0, axis_index_groups=Y_GROUPS)]
    all_to_all x0 -> x1, blocking collectives: none -> 18.1 us  [to_all(): return lax.all_to_all(copies, 'dp', 0, 0, axis_index_groups=groups)]
    pallas_call x0 -> x8, Pallas kernels: none -> 17.9 us  [the longest x7 16.2 us: call(): pl.pallas_call(kernel, out_shape=[jax.ShapeDtypeStruct(shape, kind) for s...]
    dot_general x6 -> x0, matrix products: 14.4 us -> none  [the longest x3 7.71 us: dot_nn(): lax.dot_general(left, right, (((1,), (0,)), ((), ())), preferred_element_...]
    ppermute x4 -> x2, starting transfers between devices: 23.7 us -> 9.35 us  [z_transposed(): return lax.ppermute(value, EVERY, pairs)]
    all_gather x1 -> x0, waiting for transfers between devices: 14 us -> none  [gathered_weight(): whole = lax.all_gather(square, 'dp', axis=0, axis_index_groups=X_GROUPS)]
    ppermute x9 -> x11, starting transfers between devices: 23.8 us -> 32.6 us  [swap(): return lax.ppermute(value, axis, [(0, 1), (1, 0)])]
    convert_element_type x7 -> x2, other arithmetic: 4.69 us -> 0.08 us  [the longest x1 0.07 us: per_device(): from_chip = swap(pair.astype(BF16), 'seq')]
  transfers between devices with their start and end apart: 19 -> 21, of which waited for: 6 -> 5; matrix products, arithmetic and copies ran while one was open for 11% -> 7% of each run, Pallas kernels for 0% -> 8%
where the time goes in v3:
time: 155 us; the launch traced here: 153 us
  starting transfers between devices  75.5 us (49%)
  local copies, waits for them, and re-layouts  19.9 us (13%)
  blocking collectives  18.1 us (12%)
  Pallas kernels  17.9 us (12%)
  waiting for transfers between devices  14.6 us (9%)
  other arithmetic  3.88 us (3%)
  between operations  2.66 us (2%)
    ppermute x11, starting transfers between devices, swap(): return lax.ppermute(value, axis, [(0, 1), (1, 0)])  32.6 us
    ppermute x6, starting transfers between devices, along_x(): return lax.ppermute(value, 'dp', pairs)  19.6 us
    all_to_all x1, blocking collectives, to_all(): return lax.all_to_all(copies, 'dp', 0, 0, axis_index_groups=groups)  18.1 us
    pallas_call x7, Pallas kernels, call(): pl.pallas_call(kernel, out_shape=[jax.ShapeDtypeStruct(shape, kind) for s...  16.2 us
    ppermute x2, starting transfers between devices, z_transposed(): return lax.ppermute(value, EVERY, pairs)  9.35 us
    all_to_all x1, starting transfers between devices, per_device(): spread = lax.all_to_all(terms, 'dp', 0, 0, axis_index_groups=XY_GROUPS)  7 us
    all_to_all x1, starting transfers between devices, to_all(): return lax.all_to_all(copies, 'dp', 0, 0, axis_index_groups=groups)  6.95 us
    unnamed x41, local copies, waits for them, and re-layouts  6.9 us
  transfers between devices with their start and end apart: 21, of which 5 were waited for; matrix products, arithmetic and copies ran while one was open for 7% of the time, Pallas kernels for 8%

profile of v3, /device:TPU:1, one launch (start us, length us, event | category | flops | bytes accessed | tf_op | source)
XLA Modules:
  0.0 153.0 jit_solution(13929383736055593198)
XLA Ops:
  2.0 18.1 %all_to_all.15 = bf16[4,19,608]{2,1,0:T(8,128)(2,1)S(1)} all-to-all(bf16[4,19,608]{2,1,0:T(8,128)(2,1)S(1)} %broadcast_in_dim.21), channel_id=1, replica_groups={{0,64,128,192},{2,66,130,194},{4,68,132,196},{6,70,134,198},{8,72,136,2..., dimensions={0} | all-to-all | bytes 184832 | tf_op jit(solution)/shard_map/all_to_all | solution.py:73
  20.2 1.0 broadcast_in_dim.22
  21.2 7.0 %all-to-all-start.1 = ((bf16[8,76,608]{2,1,0:T(8,128)(2,1)}), bf16[8,76,608]{2,1,0:T(8,128)(2,1)S(1)}, u32[]{:S(2)}, u32[]{:S(2)}) async-start(bf16[8,76,608]{2,1,0:T(8,128)(2,1)} %broadcast_in_dim.22), calls=%async_computation.1 | async-start | bytes 1638400 | tf_op jit(solution)/shard_map/all_to_all | solution.py:73
  28.2 4.8 %collective-permute-start.1 = (bf16[2432,128]{0,1:T(8,128)(2,1)}, bf16[2432,128]{0,1:T(8,128)(2,1)}, u32[]{:S(2)}, u32[]{:S(2)}) collective-permute-start(bf16[2432,128]{0,1:T(8,128)(2,1)} %bitcast.2), channel_id=1, source_target_pairs={{0,256},{256,0},{1,257},{257,1},{2,258},{258,2},{3,259},{259,3},{4... | collective-permute-start | bytes 1867784 | tf_op jit(solution)/shard_map/ppermute | solution.py:32
  32.9 2.3 %collective-permute-start = (bf16[2432,128]{0,1:T(8,128)(2,1)}, bf16[2432,128]{0,1:T(8,128)(2,1)}, u32[]{:S(2)}, u32[]{:S(2)}) collective-permute-start(bf16[2432,128]{0,1:T(8,128)(2,1)} %bitcast.2), channel_id=1, source_target_pairs={{0,1},{1,0},{2,3},{3,2},{4,5},{5,4},{6,7},{7,6},{8,9},{9,8},{10,11... | collective-permute-start | bytes 1867784 | tf_op jit(solution)/shard_map/ppermute | solution.py:32
  36.8 2.2 %collective-permute-start.3 = (bf16[128,1216]{1,0:T(8,128)(2,1)}, bf16[128,1216]{1,0:T(8,128)(2,1)}, u32[]{:S(2)}, u32[]{:S(2)}) collective-permute-start(bf16[128,1216]{1,0:T(8,128)(2,1)} %dynamic-slice_bitcast_fusion), channel_id=1, source_target_pairs={{0,256},{256,0},{1,257},{257,1},{2,258},{258,2},{3,259},{259,3},{4... | collective-permute-start | bytes 933896 | tf_op jit(solution)/shard_map/ppermute | solution.py:32
  39.1 2.1 %collective-permute-start.2 = (f32[2432]{0:T(1024)S(1)}, f32[2432]{0:T(1024)S(1)}, u32[]{:S(2)}, u32[]{:S(2)}) collective-permute-start(f32[2432]{0:T(1024)S(1)} %fusion.10), channel_id=1, source_target_pairs={{0,256},{256,0},{1,257},{257,1},{2,258},{258,2},{3,259},{259,3},{4... | collective-permute-start | bytes 29192 | tf_op jit(solution)/shard_map/ppermute | solution.py:32
  41.4 1.5 copy.41
  43.6 1.4 copy.42
  45.0 1.1 shard_map.139
  46.1 1.1 copy-done.1
  47.8 3.0 %collective-permute-done = bf16[2432,128]{0,1:T(8,128)(2,1)} collective-permute-done((bf16[2432,128]{0,1:T(8,128)(2,1)}, bf16[2432,128]{0,1:T(8,128)(2,1)}, u32[]{:S(2)}, u32[]{:S(2)}) %collective-permute-start) | collective-permute-done | bytes 622624 | tf_op jit(solution)/shard_map/ppermute | solution.py:32
  51.1 1.3 reshape.75
  52.4 2.0 %fusion.13 = (bf16[304,608]{1,0:T(8,128)(2,1)S(1)}, bf16[304,608]{1,0:T(8,128)(2,1)}) fusion(bf16[608,608]{1,0:T(8,128)(2,1)} %reshape.75), kind=kLoop, calls=%fused_computation.34 | loop fusion | bytes 1478656 | tf_op jit(solution)/shard_map/slice | solution.py:276
  54.4 4.4 %collective-permute-start.8 = (bf16[304,608]{1,0:T(8,128)(2,1)}, bf16[304,608]{1,0:T(8,128)(2,1)}, u32[]{:S(2)}, u32[]{:S(2)}) collective-permute-start(bf16[304,608]{1,0:T(8,128)(2,1)} %get-tuple-element.43.refs_0_), channel_id=1, source_target_pairs={{0,48},{2,50},{4,52},{6,54},{8,56},{10,58},{12,60},{14,62},{16,0},... | collective-permute-start | bytes 1109000 | tf_op jit(solution)/shard_map/ppermute | solution.py:82
  58.8 1.9 %collective-permute-start.6 = (bf16[304,608]{1,0:T(8,128)(2,1)}, bf16[304,608]{1,0:T(8,128)(2,1)}, u32[]{:S(2)}, u32[]{:S(2)}) collective-permute-start(bf16[304,608]{1,0:T(8,128)(2,1)} %get-tuple-element.43.refs_0_), channel_id=1, source_target_pairs={{0,16},{2,18},{4,20},{6,22},{8,24},{10,26},{12,28},{14,30},{16,32}... | collective-permute-start | bytes 1109000 | tf_op jit(solution)/shard_map/ppermute | solution.py:82
  60.7 4.6 %collective-permute-start.9 = (bf16[304,608]{1,0:T(8,128)(2,1)S(1)}, bf16[304,608]{1,0:T(8,128)(2,1)}, u32[]{:S(2)}, u32[]{:S(2)}) collective-permute-start(bf16[304,608]{1,0:T(8,128)(2,1)S(1)} %get-tuple-element.44.refs_1_), channel_id=1, source_target_pairs={{0,48},{2,50},{4,52},{6,54},{8,56},{10,58},{12,60},{14,62},{16,0},... | collective-permute-start | bytes 1109000 | tf_op jit(solution)/shard_map/ppermute | solution.py:82
  65.3 1.9 %collective-permute-start.7 = (bf16[304,608]{1,0:T(8,128)(2,1)S(1)}, bf16[304,608]{1,0:T(8,128)(2,1)}, u32[]{:S(2)}, u32[]{:S(2)}) collective-permute-start(bf16[304,608]{1,0:T(8,128)(2,1)S(1)} %get-tuple-element.44.refs_1_), channel_id=1, source_target_pairs={{0,16},{2,18},{4,20},{6,22},{8,24},{10,26},{12,28},{14,30},{16,32}... | collective-permute-start | bytes 1109000 | tf_op jit(solution)/shard_map/ppermute | solution.py:82
  67.2 4.9 %collective-permute-start.4 = (bf16[2432,128]{0,1:T(8,128)(2,1)}, bf16[2432,128]{0,1:T(8,128)(2,1)}, u32[]{:S(2)}, u32[]{:S(2)}) collective-permute-start(bf16[2432,128]{0,1:T(8,128)(2,1)} %collective-permute-done), channel_id=1, source_target_pairs={{0,256},{256,0},{1,257},{257,1},{2,258},{258,2},{3,259},{259,3},{4... | collective-permute-start | bytes 1867784 | tf_op jit(solution)/shard_map/ppermute | solution.py:32
  72.2 1.6 %fusion.2 = f32[128,1216]{1,0:T(8,128)S(1)} fusion(bf16[128,1216]{1,0:T(8,128)(2,1)} %collective-permute-done.3, f32[]{:T(128)S(6)} %select_n.69, bf16[1,128,2432]{2,1,0:T(8,128)(2,1)S(1)} %copy-done.15, s32[]{:T(128)S(6)} %select_n.67, f32[]{:T(128)S(6)} %select_n.68, f32[]{:T(128)} %bitcast.18, bf16[128,2432]{1,0:T(8,128)(2,1)S(1)} %copy-done.16, ...), kind=kLoop, calls=%fused_computation.8 | loop fusion | flops 1556480 | bytes 1867792 | tf_op jit(solution)/shard_map/add | solution.py:284
  73.9 1.0 fusion.4
  74.9 3.0 %collective-permute-start.5 = (f32[128,608]{1,0:T(8,128)}, f32[128,608]{1,0:T(8,128)}, u32[]{:S(2)}, u32[]{:S(2)}) collective-permute-start(f32[128,608]{1,0:T(8,128)} %get-tuple-element.61), channel_id=1, source_target_pairs={{0,1},{1,0},{2,3},{3,2},{4,5},{5,4},{6,7},{7,6},{8,9},{9,8},{10,11... | collective-permute-start | bytes 933896 | tf_op jit(solution)/shard_map/ppermute | solution.py:32
  77.9 1.9 %collective-permute-start.10 = (bf16[304,608]{1,0:T(8,128)(2,1)}, bf16[304,608]{1,0:T(8,128)(2,1)}, u32[]{:S(2)}, u32[]{:S(2)}) collective-permute-start(bf16[304,608]{1,0:T(8,128)(2,1)} %collective-permute-done.6.refs_2_), channel_id=1, source_target_pairs={{0,16},{2,18},{4,20},{6,22},{8,24},{10,26},{12,28},{14,30},{16,32}... | collective-permute-start | bytes 1109000 | tf_op jit(solution)/shard_map/ppermute | solution.py:82
  79.9 4.9 %collective-permute-start.11 = (bf16[304,608]{1,0:T(8,128)(2,1)}, bf16[304,608]{1,0:T(8,128)(2,1)}, u32[]{:S(2)}, u32[]{:S(2)}) collective-permute-start(bf16[304,608]{1,0:T(8,128)(2,1)} %collective-permute-done.9.refs_5_), channel_id=1, source_target_pairs={{0,48},{2,50},{4,52},{6,54},{8,56},{10,58},{12,60},{14,62},{16,0},... | collective-permute-start | bytes 1109000 | tf_op jit(solution)/shard_map/ppermute | solution.py:82
  85.5 1.4 copy.45
  87.0 1.4 copy.46
  88.4 1.1 copy-done.4
  89.5 0.9 copy-done.6
  90.4 1.0 copy-done.8
  92.2 1.8 %shard_map.140 = (bf16[4,256,608]{2,1,0:T(8,128)(2,1)S(1)}, bf16[256,128]{1,0:T(8,128)(2,1)S(1)}, f32[128,608]{1,0:T(8,128)S(1)}, f32[128,608]{1,0:T(8,128)S(1)}) custom-call(s32[4]{0:T(128)S(1)} %pad_add_fusion.places, bf16[4,4,152,128]{3,2,1,0:T(8,128)(2,1)S(1)} %bitcast.55, bf16[4,4,152,128]{3,2,1,0:T(8,128)(2,1)S(1)} %bitcast.57, ...), custom_call_target="tpu_custom_call" | custom-call | flops 235929600 | bytes 4649744 | tf_op jit(solution)/shard_map/pallas_call | solution.py:121
  94.1 3.4 %shard_map.141.product = f32[512,608]{1,0:T(8,128)S(1)} custom-call(bf16[4,256,608]{2,1,0:T(8,128)(2,1)S(1)} %copy-done.2, bf16[4,256,608]{2,1,0:T(8,128)(2,1)S(1)} %get-tuple-element.42.far_rows, bf16[304,608]{1,0:T(8,128)(2,1)} %get-tuple-element.43.refs_0_, bf16[304,608]{1,0:T(8,128)(2,1)S(1)} %get-tuple-element.44.refs_1_, ...), custom_call_target="tpu_custom_call" | custom-call | flops 1135607808 | bytes 5953536 | tf_op jit(solution)/shard_map/pallas_call | solution.py:121
  97.5 2.2 %shard_map.142 = (bf16[512,608]{1,0:T(8,128)(2,1)S(1)}, f32[512,128]{1,0:T(8,128)S(1)}) custom-call(f32[512,608]{1,0:T(8,128)S(1)} %shard_map.141.product, bf16[4,256,608]{2,1,0:T(8,128)(2,1)S(1)} %copy-done.2, bf16[4,256,608]{2,1,0:T(8,128)(2,1)S(1)} %get-tuple-element.42.far_rows, bf16[304,608]{1,0:T(8,128)(2,1)} %collective-permute-done.10.upper.refs_6_, ...), custom_call_target="tpu_custom_call" | custom-call | flops 458227712 | bytes 6142720 | tf_op jit(solution)/shard_map/pallas_call | solution.py:121
  99.8 3.4 %collective-permute-start.12 = (bf16[512,128]{1,0:T(8,128)(2,1)S(1)}, bf16[512,128]{1,0:T(8,128)(2,1)S(1)}, u32[]{:S(2)}, u32[]{:S(2)}) collective-permute-start(bf16[512,128]{1,0:T(8,128)(2,1)S(1)} %convert_element_type.57), channel_id=1, source_target_pairs={{0,256},{256,0},{1,257},{257,1},{2,258},{258,2},{3,259},{259,3},{4... | collective-permute-start | bytes 393224 | tf_op jit(solution)/shard_map/ppermute | solution.py:32
  104.2 2.5 %collective-permute-start.13 = (bf16[512,128]{1,0:T(8,128)(2,1)S(1)}, bf16[512,128]{1,0:T(8,128)(2,1)S(1)}, u32[]{:S(2)}, u32[]{:S(2)}) collective-permute-start(bf16[512,128]{1,0:T(8,128)(2,1)S(1)} %get-tuple-element.57), channel_id=1, source_target_pairs={{0,1},{1,0},{2,3},{3,2},{4,5},{5,4},{6,7},{7,6},{8,9},{9,8},{10,11... | collective-permute-start | bytes 393224 | tf_op jit(solution)/shard_map/ppermute | solution.py:32
  106.7 5.6 %shard_map.144 = (bf16[4,4,152,256]{3,2,1,0:T(8,128)(2,1)S(1)}, bf16[4,4,152,256]{3,2,1,0:T(8,128)(2,1)}) custom-call(s32[4]{0:T(128)S(1)} %pad_add_fusion.places, bf16[512,608]{1,0:T(8,128)(2,1)S(1)} %get-tuple-element.48.before, f32[512,128]{1,0:T(8,128)S(1)} %get-tuple-element.47.low, bf16[4,4,152,128]{3,2,1,0:T(8,128)(2,1)S(1)} %bitcast.61, ...), custom_call_target="tpu_custom_call" | custom-call | flops 1832910848 | bytes 6955024 | tf_op jit(solution)/shard_map/pallas_call | solution.py:121
  112.3 1.7 %shard_map.143 = bf16[32,40,128]{2,1,0:T(8,128)(2,1)} custom-call(s32[1]{0:T(128)} %bitcast.quarter, f32[512,128]{1,0:T(8,128)S(1)} %get-tuple-element.58.pair, bf16[512,128]{1,0:T(8,128)(2,1)S(1)} %collective-permute-done.13.far, bf16[608,128]{1,0:T(8,128)(2,1)S(1)} %fusion.up, bf16[768,608]{1,0:T(8,128)(2,1)S(1)} %copy-done.11, ...), custom_call_target="tpu_custom_call" | custom-call | flops 100663296 | bytes 3000000 | tf_op jit(solution)/shard_map/pallas_call | solution.py:212
  114.1 2.5 %collective-permute-start.14 = (bf16[4,4,152,256]{3,2,1,0:T(8,128)(2,1)}, bf16[4,4,152,256]{3,2,1,0:T(8,128)(2,1)S(1)}, u32[]{:S(2)}, u32[]{:S(2)}) collective-permute-start(bf16[4,4,152,256]{3,2,1,0:T(8,128)(2,1)} %get-tuple-element.53), channel_id=1, source_target_pairs={{0,256},{256,0},{1,257},{257,1},{2,258},{258,2},{3,259},{259,3},{4... | collective-permute-start | bytes 3735560 | tf_op jit(solution)/shard_map/ppermute | solution.py:32
  116.6 7.0 %all-to-all-start.2 = ((bf16[32,40,128]{2,1,0:T(8,128)(2,1)}), bf16[32,40,128]{2,1,0:T(8,128)(2,1)S(1)}, u32[]{:S(2)}, u32[]{:S(2)}) async-start(bf16[32,40,128]{2,1,0:T(8,128)(2,1)} %shard_map.143), calls=%async_computation.2 | async-start | bytes 655360 | tf_op jit(solution)/shard_map/all_to_all | solution.py:324
  123.6 1.3 copy-done.10
  124.9 1.0 shard_map.145
  125.9 3.0 %collective-permute-start.15 = (bf16[4,4,152,128]{3,2,1,0:T(8,128)(2,1)}, bf16[4,4,152,128]{3,2,1,0:T(8,128)(2,1)S(1)}, u32[]{:S(2)}, u32[]{:S(2)}) collective-permute-start(bf16[4,4,152,128]{3,2,1,0:T(8,128)(2,1)} %get-tuple-element.55), channel_id=1, source_target_pairs={{0,1},{1,0},{2,3},{3,2},{4,5},{5,4},{6,7},{7,6},{8,9},{9,8},{10,11... | collective-permute-start | bytes 1867784 | tf_op jit(solution)/shard_map/ppermute | solution.py:32
  128.9 6.0 %all-to-all-done.2 = bf16[32,40,128]{2,1,0:T(8,128)(2,1)S(1)} async-done(((bf16[32,40,128]{2,1,0:T(8,128)(2,1)}), bf16[32,40,128]{2,1,0:T(8,128)(2,1)S(1)}, u32[]{:S(2)}, u32[]{:S(2)}) %all-to-all-start.2) | async-done | bytes 327712 | tf_op jit(solution)/shard_map/all_to_all | solution.py:324
  135.0 4.2 %collective-permute-start.17 = (f32[40,128]{1,0:T(8,128)S(1)}, f32[40,128]{1,0:T(8,128)S(1)}, u32[]{:S(2)}, u32[]{:S(2)}) collective-permute-start(f32[40,128]{1,0:T(8,128)S(1)} %convert_reduce_fusion), channel_id=1, source_target_pairs={{0,1},{1,65},{256,129},{257,193},{2,3},{3,67},{258,131},{259,195},... | collective-permute-start | bytes 61448 | tf_op jit(solution)/shard_map/ppermute | solution.py:96
  139.2 5.1 %collective-permute-start.16 = (f32[40,128]{1,0:T(8,128)S(1)}, f32[40,128]{1,0:T(8,128)S(1)}, u32[]{:S(2)}, u32[]{:S(2)}) collective-permute-start(f32[40,128]{1,0:T(8,128)S(1)} %convert_reduce_fusion), channel_id=1, source_target_pairs={{0,0},{1,64},{256,128},{257,192},{2,2},{3,66},{258,130},{259,194},... | collective-permute-start | bytes 61448 | tf_op jit(solution)/shard_map/ppermute | solution.py:96
  144.4 3.9 %collective-permute-done.16 = f32[40,128]{1,0:T(8,128)S(1)} collective-permute-done((f32[40,128]{1,0:T(8,128)S(1)}, f32[40,128]{1,0:T(8,128)S(1)}, u32[]{:S(2)}, u32[]{:S(2)}) %collective-permute-start.16) | collective-permute-done | bytes 20512 | tf_op jit(solution)/shard_map/ppermute | solution.py:96
  148.2 1.9 %collective-permute-start.18 = (f32[40,128]{1,0:T(8,128)S(1)}, f32[40,128]{1,0:T(8,128)S(1)}, u32[]{:S(2)}, u32[]{:S(2)}) collective-permute-start(f32[40,128]{1,0:T(8,128)S(1)} %add.87), channel_id=1, source_target_pairs={{0,256},{256,0},{1,257},{257,1},{2,258},{258,2},{3,259},{259,3},{4... | collective-permute-start | bytes 61448 | tf_op jit(solution)/shard_map/ppermute | solution.py:32
  150.2 1.2 collective-permute-done.18
  151.9 1.1 shard_map.146
  (80 shorter events, 7.0 us)
Async XLA Ops:
  0.6 84.2 %copy-start = (bf16[2432,128]{1,0:T(8,128)(2,1)S(1)}, bf16[2432,128]{1,0:T(8,128)(2,1)}, u32[]{:S(2)}) copy-start(bf16[2432,128]{1,0:T(8,128)(2,1)} %param.19) | copy-start | bytes 1867780
  0.6 1.0 copy-start.17
  20.2 15.7 %copy-start.14 = (bf16[1,128,2432]{2,1,0:T(8,128)(2,1)S(1)}, bf16[1,128,2432]{2,1,0:T(8,128)(2,1)}, u32[]{:S(2)}) copy-start(bf16[1,128,2432]{2,1,0:T(8,128)(2,1)} %param.13) | copy-start | bytes 1867780
  21.2 17.8 %copy-start.18 = (f32[1,8,2432]{2,1,0:T(8,128)S(1)}, f32[1,8,2432]{2,1,0:T(8,128)}, u32[]{:S(2)}) copy-start(f32[1,8,2432]{2,1,0:T(8,128)} %param.20) | copy-start | bytes 233476
  21.2 29.6 %all-to-all-start.1 = ((bf16[8,76,608]{2,1,0:T(8,128)(2,1)}), bf16[8,76,608]{2,1,0:T(8,128)(2,1)S(1)}, u32[]{:S(2)}, u32[]{:S(2)}) async-start(bf16[8,76,608]{2,1,0:T(8,128)(2,1)} %broadcast_in_dim.22), calls=%async_computation.1 | async-start | bytes 1638400 | tf_op jit(solution)/shard_map/all_to_all | solution.py:73
  28.2 15.4 %collective-permute-start.1 = (bf16[2432,128]{0,1:T(8,128)(2,1)}, bf16[2432,128]{0,1:T(8,128)(2,1)}, u32[]{:S(2)}, u32[]{:S(2)}) collective-permute-start(bf16[2432,128]{0,1:T(8,128)(2,1)} %bitcast.2), channel_id=1, source_target_pairs={{0,256},{256,0},{1,257},{257,1},{2,258},{258,2},{3,259},{259,3},{4... | collective-permute-start | bytes 1867784 | tf_op jit(solution)/shard_map/ppermute | solution.py:32
  32.9 17.9 %collective-permute-start = (bf16[2432,128]{0,1:T(8,128)(2,1)}, bf16[2432,128]{0,1:T(8,128)(2,1)}, u32[]{:S(2)}, u32[]{:S(2)}) collective-permute-start(bf16[2432,128]{0,1:T(8,128)(2,1)} %bitcast.2), channel_id=1, source_target_pairs={{0,1},{1,0},{2,3},{3,2},{4,5},{5,4},{6,7},{7,6},{8,9},{9,8},{10,11... | collective-permute-start | bytes 1867784 | tf_op jit(solution)/shard_map/ppermute | solution.py:32
  36.8 11.0 %collective-permute-start.3 = (bf16[128,1216]{1,0:T(8,128)(2,1)}, bf16[128,1216]{1,0:T(8,128)(2,1)}, u32[]{:S(2)}, u32[]{:S(2)}) collective-permute-start(bf16[128,1216]{1,0:T(8,128)(2,1)} %dynamic-slice_bitcast_fusion), channel_id=1, source_target_pairs={{0,256},{256,0},{1,257},{257,1},{2,258},{258,2},{3,259},{259,3},{4... | collective-permute-start | bytes 933896 | tf_op jit(solution)/shard_map/ppermute | solution.py:32
  39.1 8.7 %collective-permute-start.2 = (f32[2432]{0:T(1024)S(1)}, f32[2432]{0:T(1024)S(1)}, u32[]{:S(2)}, u32[]{:S(2)}) collective-permute-start(f32[2432]{0:T(1024)S(1)} %fusion.10), channel_id=1, source_target_pairs={{0,256},{256,0},{1,257},{257,1},{2,258},{258,2},{3,259},{259,3},{4... | collective-permute-start | bytes 29192 | tf_op jit(solution)/shard_map/ppermute | solution.py:32
  41.4 3.6 %copy-start.3 = (bf16[2432,128]{1,0:T(8,128)(2,1)S(1)}, bf16[2432,128]{1,0:T(8,128)(2,1)}, u32[]{:S(2)}) copy-start(bf16[2432,128]{1,0:T(8,128)(2,1)} %param.18) | copy-start | bytes 1867780
  46.1 1.1 copy-start.1
  47.2 0.6 copy-start.12
  52.4 19.8 %copy-start.15 = (bf16[1,128,2432]{2,1,0:T(8,128)(2,1)S(1)}, bf16[1,128,2432]{2,1,0:T(8,128)(2,1)}, u32[]{:S(2)}) copy-start(bf16[1,128,2432]{2,1,0:T(8,128)(2,1)} %param.13) | copy-start | bytes 1867780
  52.4 19.8 %copy-start.16 = (bf16[128,2432]{1,0:T(8,128)(2,1)S(1)}, bf16[128,2432]{1,0:T(8,128)(2,1)}, u32[]{:S(2)}) copy-start(bf16[128,2432]{1,0:T(8,128)(2,1)} %param.14) | copy-start | bytes 1867780
  54.4 39.6 %collective-permute-start.8 = (bf16[304,608]{1,0:T(8,128)(2,1)}, bf16[304,608]{1,0:T(8,128)(2,1)}, u32[]{:S(2)}, u32[]{:S(2)}) collective-permute-start(bf16[304,608]{1,0:T(8,128)(2,1)} %get-tuple-element.43.refs_0_), channel_id=1, source_target_pairs={{0,48},{2,50},{4,52},{6,54},{8,56},{10,58},{12,60},{14,62},{16,0},... | collective-permute-start | bytes 1109000 | tf_op jit(solution)/shard_map/ppermute | solution.py:82
  58.8 16.1 %collective-permute-start.6 = (bf16[304,608]{1,0:T(8,128)(2,1)}, bf16[304,608]{1,0:T(8,128)(2,1)}, u32[]{:S(2)}, u32[]{:S(2)}) collective-permute-start(bf16[304,608]{1,0:T(8,128)(2,1)} %get-tuple-element.43.refs_0_), channel_id=1, source_target_pairs={{0,16},{2,18},{4,20},{6,22},{8,24},{10,26},{12,28},{14,30},{16,32}... | collective-permute-start | bytes 1109000 | tf_op jit(solution)/shard_map/ppermute | solution.py:82
  60.7 17.2 %collective-permute-start.9 = (bf16[304,608]{1,0:T(8,128)(2,1)S(1)}, bf16[304,608]{1,0:T(8,128)(2,1)}, u32[]{:S(2)}, u32[]{:S(2)}) collective-permute-start(bf16[304,608]{1,0:T(8,128)(2,1)S(1)} %get-tuple-element.44.refs_1_), channel_id=1, source_target_pairs={{0,48},{2,50},{4,52},{6,54},{8,56},{10,58},{12,60},{14,62},{16,0},... | collective-permute-start | bytes 1109000 | tf_op jit(solution)/shard_map/ppermute | solution.py:82
  65.3 28.8 %collective-permute-start.7 = (bf16[304,608]{1,0:T(8,128)(2,1)S(1)}, bf16[304,608]{1,0:T(8,128)(2,1)}, u32[]{:S(2)}, u32[]{:S(2)}) collective-permute-start(bf16[304,608]{1,0:T(8,128)(2,1)S(1)} %get-tuple-element.44.refs_1_), channel_id=1, source_target_pairs={{0,16},{2,18},{4,20},{6,22},{8,24},{10,26},{12,28},{14,30},{16,32}... | collective-permute-start | bytes 1109000 | tf_op jit(solution)/shard_map/ppermute | solution.py:82
  67.2 12.6 %collective-permute-start.4 = (bf16[2432,128]{0,1:T(8,128)(2,1)}, bf16[2432,128]{0,1:T(8,128)(2,1)}, u32[]{:S(2)}, u32[]{:S(2)}) collective-permute-start(bf16[2432,128]{0,1:T(8,128)(2,1)} %collective-permute-done), channel_id=1, source_target_pairs={{0,256},{256,0},{1,257},{257,1},{2,258},{258,2},{3,259},{259,3},{4... | collective-permute-start | bytes 1867784 | tf_op jit(solution)/shard_map/ppermute | solution.py:32
  74.9 13.5 %collective-permute-start.5 = (f32[128,608]{1,0:T(8,128)}, f32[128,608]{1,0:T(8,128)}, u32[]{:S(2)}, u32[]{:S(2)}) collective-permute-start(f32[128,608]{1,0:T(8,128)} %get-tuple-element.61), channel_id=1, source_target_pairs={{0,1},{1,0},{2,3},{3,2},{4,5},{5,4},{6,7},{7,6},{8,9},{9,8},{10,11... | collective-permute-start | bytes 933896 | tf_op jit(solution)/shard_map/ppermute | solution.py:32
  77.9 19.6 %collective-permute-start.10 = (bf16[304,608]{1,0:T(8,128)(2,1)}, bf16[304,608]{1,0:T(8,128)(2,1)}, u32[]{:S(2)}, u32[]{:S(2)}) collective-permute-start(bf16[304,608]{1,0:T(8,128)(2,1)} %collective-permute-done.6.refs_2_), channel_id=1, source_target_pairs={{0,16},{2,18},{4,20},{6,22},{8,24},{10,26},{12,28},{14,30},{16,32}... | collective-permute-start | bytes 1109000 | tf_op jit(solution)/shard_map/ppermute | solution.py:82
  79.9 17.6 %collective-permute-start.11 = (bf16[304,608]{1,0:T(8,128)(2,1)}, bf16[304,608]{1,0:T(8,128)(2,1)}, u32[]{:S(2)}, u32[]{:S(2)}) collective-permute-start(bf16[304,608]{1,0:T(8,128)(2,1)} %collective-permute-done.9.refs_5_), channel_id=1, source_target_pairs={{0,48},{2,50},{4,52},{6,54},{8,56},{10,58},{12,60},{14,62},{16,0},... | collective-permute-start | bytes 1109000 | tf_op jit(solution)/shard_map/ppermute | solution.py:82
  88.4 1.1 copy-start.4
  89.5 0.9 copy-start.6
  90.4 1.0 copy-start.8
  91.4 0.8 copy-start.13
  92.2 1.9 %copy-start.2 = (bf16[4,256,608]{2,1,0:T(8,128)(2,1)S(1)}, bf16[4,256,608]{2,1,0:T(8,128)(2,1)}, u32[]{:S(2)}) copy-start(bf16[4,256,608]{2,1,0:T(8,128)(2,1)} %copy-done.1) | copy-start | bytes 3735556
  94.1 3.5 %copy-start.7 = (bf16[608,128]{1,0:T(8,128)(2,1)S(1)}, bf16[608,128]{1,0:T(8,128)(2,1)}, u32[]{:S(2)}) copy-start(bf16[608,128]{1,0:T(8,128)(2,1)} %constant_dynamic-slice_fusion.up) | copy-start | bytes 466948
  99.7 7.0 %copy-start.5 = (bf16[2432,128]{1,0:T(8,128)(2,1)S(1)}, bf16[2432,128]{1,0:T(8,128)(2,1)}, u32[]{:S(2)}) copy-start(bf16[2432,128]{1,0:T(8,128)(2,1)} %param.18) | copy-start | bytes 1867780
  99.8 4.3 %collective-permute-start.12 = (bf16[512,128]{1,0:T(8,128)(2,1)S(1)}, bf16[512,128]{1,0:T(8,128)(2,1)S(1)}, u32[]{:S(2)}, u32[]{:S(2)}) collective-permute-start(bf16[512,128]{1,0:T(8,128)(2,1)S(1)} %convert_element_type.57), channel_id=1, source_target_pairs={{0,256},{256,0},{1,257},{257,1},{2,258},{258,2},{3,259},{259,3},{4... | collective-permute-start | bytes 393224 | tf_op jit(solution)/shard_map/ppermute | solution.py:32
  104.2 8.1 %copy-start.11 = (bf16[768,608]{1,0:T(8,128)(2,1)S(1)}, bf16[768,608]{1,0:T(8,128)(2,1)}, u32[]{:S(2)}) copy-start(bf16[768,608]{1,0:T(8,128)(2,1)} %constant.105.clone.spread) | copy-start | bytes 2801668
  104.2 8.1 %collective-permute-start.13 = (bf16[512,128]{1,0:T(8,128)(2,1)S(1)}, bf16[512,128]{1,0:T(8,128)(2,1)S(1)}, u32[]{:S(2)}, u32[]{:S(2)}) collective-permute-start(bf16[512,128]{1,0:T(8,128)(2,1)S(1)} %get-tuple-element.57), channel_id=1, source_target_pairs={{0,1},{1,0},{2,3},{3,2},{4,5},{5,4},{6,7},{7,6},{8,9},{9,8},{10,11... | collective-permute-start | bytes 393224 | tf_op jit(solution)/shard_map/ppermute | solution.py:32
  112.3 1.7 %copy-start.9 = (bf16[4,4,152,256]{3,2,1,0:T(8,128)(2,1)}, bf16[4,4,152,256]{3,2,1,0:T(8,128)(2,1)S(1)}, u32[]{:S(2)}) copy-start(bf16[4,4,152,256]{3,2,1,0:T(8,128)(2,1)S(1)} %get-tuple-element.52.keep) | copy-start | bytes 3735556
  114.1 9.6 %collective-permute-start.14 = (bf16[4,4,152,256]{3,2,1,0:T(8,128)(2,1)}, bf16[4,4,152,256]{3,2,1,0:T(8,128)(2,1)S(1)}, u32[]{:S(2)}, u32[]{:S(2)}) collective-permute-start(bf16[4,4,152,256]{3,2,1,0:T(8,128)(2,1)} %get-tuple-element.53), channel_id=1, source_target_pairs={{0,256},{256,0},{1,257},{257,1},{2,258},{258,2},{3,259},{259,3},{4... | collective-permute-start | bytes 3735560 | tf_op jit(solution)/shard_map/ppermute | solution.py:32
  116.6 18.3 %all-to-all-start.2 = ((bf16[32,40,128]{2,1,0:T(8,128)(2,1)}), bf16[32,40,128]{2,1,0:T(8,128)(2,1)S(1)}, u32[]{:S(2)}, u32[]{:S(2)}) async-start(bf16[32,40,128]{2,1,0:T(8,128)(2,1)} %shard_map.143), calls=%async_computation.2 | async-start | bytes 655360 | tf_op jit(solution)/shard_map/all_to_all | solution.py:324
  123.6 1.3 copy-start.10
  125.9 26.0 %collective-permute-start.15 = (bf16[4,4,152,128]{3,2,1,0:T(8,128)(2,1)}, bf16[4,4,152,128]{3,2,1,0:T(8,128)(2,1)S(1)}, u32[]{:S(2)}, u32[]{:S(2)}) collective-permute-start(bf16[4,4,152,128]{3,2,1,0:T(8,128)(2,1)} %get-tuple-element.55), channel_id=1, source_target_pairs={{0,1},{1,0},{2,3},{3,2},{4,5},{5,4},{6,7},{7,6},{8,9},{9,8},{10,11... | collective-permute-start | bytes 1867784 | tf_op jit(solution)/shard_map/ppermute | solution.py:32
  135.0 9.4 %collective-permute-start.17 = (f32[40,128]{1,0:T(8,128)S(1)}, f32[40,128]{1,0:T(8,128)S(1)}, u32[]{:S(2)}, u32[]{:S(2)}) collective-permute-start(f32[40,128]{1,0:T(8,128)S(1)} %convert_reduce_fusion), channel_id=1, source_target_pairs={{0,1},{1,65},{256,129},{257,193},{2,3},{3,67},{258,131},{259,195},... | collective-permute-start | bytes 61448 | tf_op jit(solution)/shard_map/ppermute | solution.py:96
  139.2 9.0 %collective-permute-start.16 = (f32[40,128]{1,0:T(8,128)S(1)}, f32[40,128]{1,0:T(8,128)S(1)}, u32[]{:S(2)}, u32[]{:S(2)}) collective-permute-start(f32[40,128]{1,0:T(8,128)S(1)} %convert_reduce_fusion), channel_id=1, source_target_pairs={{0,0},{1,64},{256,128},{257,192},{2,2},{3,66},{258,130},{259,194},... | collective-permute-start | bytes 61448 | tf_op jit(solution)/shard_map/ppermute | solution.py:96
  148.2 3.1 %collective-permute-start.18 = (f32[40,128]{1,0:T(8,128)S(1)}, f32[40,128]{1,0:T(8,128)S(1)}, u32[]{:S(2)}, u32[]{:S(2)}) collective-permute-start(f32[40,128]{1,0:T(8,128)S(1)} %add.87), channel_id=1, source_target_pairs={{0,256},{256,0},{1,257},{257,1},{2,258},{258,2},{3,259},{259,3},{4... | collective-permute-start | bytes 61448 | tf_op jit(solution)/shard_map/ppermute | solution.py:32

commit v4 on v3

--- a/solution.py
+++ b/solution.py
@@ -101,6 +101,10 @@
     return lax.dynamic_index_in_dim(local, q, 1, keepdims=False)
 
 
+def lanes(refs):
+    return jnp.concatenate([ref[...] for ref in refs], 1)
+
+
 SPREAD = np.zeros((PLANE * PADDED, SLICE), np.float32)
 for _i in range(PLANE):
     for _j in range(ROWS):
@@ -111,11 +115,10 @@
     return ref[:, x].astype(F32).reshape(SLICE, ref.shape[-1]).astype(BF16)
 
 
-def call(kernel, outs, flops, *args, places=None, **more):
+def call(kernel, outs, flops, *args, places=None, scratch=()):
     specs = [pl.BlockSpec(memory_space=pltpu.VMEM)] * len(args)
     if places is not None:
         args, specs = (places,) + args, [pl.BlockSpec(memory_space=pltpu.SMEM)] + specs
-    more = more or dict(in_specs=specs)
     moved = sum(a.size * a.dtype.itemsize for a in args)
     moved += sum(math.prod(shape) * jnp.dtype(kind).itemsize for shape, kind in outs)
     return pl.pallas_call(
@@ -123,24 +126,36 @@
         out_shape=[jax.ShapeDtypeStruct(shape, kind) for shape, kind in outs],
         compiler_params=pltpu.CompilerParams(vmem_limit_bytes=24 * 2**20),
         cost_estimate=pl.CostEstimate(flops=flops, bytes_accessed=moved, transcendentals=0),
-        **more,
+        in_specs=specs,
+        scratch_shapes=scratch,
     )(*args)
 
 
-def features(places, own, other, down, rows, low_rank):
+def features(slots, own, other, down, rows, low_rank, columns):
     low = jnp.zeros((2 * TOK, RANK), F32)
-    for c in range(XN):
-        part = jnp.concatenate([x_block(ref, places[c]).T for ref in (own, other)], 0)
-        rows[c] = part
-        low = low + dot_nn(part, x_block(down, places[c]))
+    for x in range(XN):
+        for z in range(ZH):
+            start = z * SLICE + x * YN * ROWS
+            for i, ref in enumerate((own, other)):
+                part = ref[:, start:start + YN * ROWS]
+                rows[slots[x], i * TOK:(i + 1) * TOK, z * YN * ROWS:(z + 1) * YN * ROWS] = part
+        low = low + dot_nn(rows[slots[x]], x_block(down, x))
     low_rank[...] = low.astype(BF16)
-
-
-def far_kernel(places, own, other, down, near_rank, up, lift, far_lift, a_own, a_other, rows, low_rank, base, far_base):
-    features(places, own, other, down, rows, low_rank)
-    for rank, source, out in ((near_rank, lift, base), (low_rank, far_lift, far_base)):
-        adapted = ADAPTER_STRENGTH * dot_nt(rank[...], up[...])
-        out[...] = source[...] - a_own[...] * adapted[:TOK] - a_other[...] * adapted[TOK:]
+    for k in range(ZH):
+        @pl.when(slots[XN] == k)
+        def _():
+            both = jnp.concatenate([ref[:, k * SLICE:(k + 1) * SLICE] for ref in (own, other)], 0)
+            columns[...] = both.T
+
+
+def arrange_kernel(lined, upper, lower, whole):
+    for y in range(YN):
+        block = lined[y].astype(F32)
+        for z in range(ZH):
+            start = (z * YN + y) * ROWS
+            whole[start:start + ROWS] = block[z * ROWS:(z + 1) * ROWS]
+    upper[...] = whole[:SLICE // 2].astype(BF16)
+    lower[...] = whole[SLICE // 2:].astype(BF16)
 
 
 def piece(upper, lower):
@@ -156,13 +171,15 @@
         product[2 * TOK * i:2 * TOK * (i + 1)] = total
 
 
-def forward_kernel(product, rows, far_rows, upper, lower, base, far_base, a_own, a_other, up, before, low):
+def forward_kernel(
+    product, rows, far_rows, upper, lower, rank, far_rank, lift, far_lift, a_own, a_other, up, before, low
+):
     weight = piece(upper, lower)
     first, second = a_own[...], a_other[...]
-    for i, (ref, lift) in enumerate(((rows, base), (far_rows, far_base))):
+    for i, (ref, ranks, lifts) in enumerate(((rows, rank, lift), (far_rows, far_rank, far_lift))):
         part = slice(2 * TOK * i, 2 * TOK * (i + 1))
-        whole = product[part] + dot_nn(ref[XN - 1], weight)
-        reward_grad = REWARD * (lift[...] - first * whole[:TOK] - second * whole[TOK:])
+        whole = product[part] + dot_nn(ref[XN - 1], weight) + ADAPTER_STRENGTH * dot_nt(ranks[...], up[...])
+        reward_grad = REWARD * (lifts[...] - first * whole[:TOK] - second * whole[TOK:])
         grad = jnp.concatenate([first * reward_grad, second * reward_grad], 0).astype(BF16)
         before[part] = grad
         low[part] = dot_nn(grad, up[...])
@@ -190,12 +207,10 @@
     grad[...] = (home[...].reshape(MODEL_WIDTH, TOK) + across[...].astype(F32).reshape(MODEL_WIDTH, TOK)).T.astype(BF16)
 
 
-def terms_kernel(quarter, pair, far, up, spread, *refs):
-    tokens, terms = refs[:-1], refs[-1]
+def terms_kernel(pair, far, up, spread, columns, far_columns, terms):
     far = far[...].astype(F32)
     low = (pair[...] + jnp.concatenate([far[2 * TOK:], far[:2 * TOK]], 0)).astype(BF16)
-    columns = jnp.concatenate([ref[0] for ref in tokens], 1)
-    down = (ADAPTER_STRENGTH * dot_nn(columns, low)).astype(BF16)
+    down = (ADAPTER_STRENGTH * dot_nn(lanes((columns, far_columns)), low)).astype(BF16)
     both = dot_nn(spread[...], jnp.concatenate([down, up[...]], 1))
     first = both[:, :RANK].reshape(PLANE, PADDED, RANK)
     second = pltpu.roll(both[:, RANK:], ROWS - 16, 0).reshape(PLANE, PADDED, RANK)
@@ -205,23 +220,6 @@
 
 def by_x(value):
     return value.reshape(ZH, XN, YN * ROWS, value.shape[-1])
-
-
-def terms_of(q, pair, far, up, tokens):
-    whole = lambda *shape: pl.BlockSpec(shape, lambda n, quarter: (0,) * len(shape))
-    return pl.pallas_call(
-        terms_kernel,
-        out_shape=jax.ShapeDtypeStruct((PLANE, 40, RANK), BF16),
-        grid_spec=pltpu.PrefetchScalarGridSpec(
-            num_scalar_prefetch=1,
-            grid=(1,),
-            in_specs=[whole(4 * TOK, RANK), whole(4 * TOK, RANK), whole(SLICE, RANK), whole(PLANE * PADDED, SLICE)]
-            + [pl.BlockSpec((1, SLICE, TOK), lambda n, quarter: (quarter[0], 0, 0))] * 4,
-            out_specs=whole(PLANE, 40, RANK),
-        ),
-        compiler_params=pltpu.CompilerParams(vmem_limit_bytes=24 * 2**20),
-        cost_estimate=pl.CostEstimate(flops=2 * 512 * 768 * 128, bytes_accessed=3 * 10**6, transcendentals=0),
-    )(q.astype(jnp.int32)[None], pair, far, up, jnp.asarray(SPREAD, BF16), *tokens)
 
 
 def backward(places, before, low, down, weights):
@@ -255,38 +253,39 @@
     plane, hidden = lax.optimization_barrier((plane, hidden))
     lined = to_all(plane, Y_GROUPS)
 
-    own = attn[0].T
+    own = attn[0]
     from_seq = swap(own, "seq")
     from_branch = swap(own, "branch")
     x = (lax.axis_index("dp") // YN) % XN
     places = jnp.stack([(x + k) % XN for k in (0, XN - 1, 1, 2)]).astype(jnp.int32)
-    ranks = [((XN, 2 * TOK, SLICE), BF16), ((2 * TOK, RANK), BF16)]
-    rows, low_rank = call(features, ranks, 0, by_x(own), by_x(from_branch), by_x(adapter_down_map), places=places)
+    slots = jnp.array([0, 2, 3, 1], jnp.int32)[(jnp.arange(XN) - x) % XN]
+    slots = jnp.concatenate([slots, q.astype(jnp.int32)[None]])
+    kinds = [((XN, 2 * TOK, SLICE), BF16), ((2 * TOK, RANK), BF16), ((SLICE, 2 * TOK), BF16)]
+    rows, low_rank, columns = call(features, kinds, 0, own, from_branch, by_x(adapter_down_map), places=slots)
 
     selector = (jnp.arange(gates.shape[1], dtype=jnp.int32) == group_prompt[0]).astype(F32)
     gate_row = jnp.sum(selector[:, None] * gates[0], axis=0)
     gate_other = swap(gate_row, "branch")
-    hid_other = swap(lax.dynamic_slice_in_dim(hidden[0], (1 - b) * 2 * SLICE, 2 * SLICE, 1), "branch")
-    lined, from_seq, rows, low_rank, gate_other, hid_other = lax.optimization_barrier(
-        (lined, from_seq, rows, low_rank, gate_other, hid_other)
-    )
-
-    square = lined.reshape(YN, ZH, ROWS, SLICE).transpose(1, 0, 2, 3).reshape(SLICE, SLICE)
-    square = lax.optimization_barrier(square)
-    here = [square[:SLICE // 2], square[SLICE // 2:]]
-    here[0], here[1], from_seq, hid_other = lax.optimization_barrier((here[0], here[1], from_seq, hid_other))
+    half = lambda v, i: lax.dynamic_slice_in_dim(v, i * 2 * SLICE, 2 * SLICE, 1)
+    hid_other = swap(half(hidden[0], 1 - b), "branch")
+
+    here = call(
+        arrange_kernel, [((SLICE // 2, SLICE), BF16)] * 2, 0, lined, scratch=[pltpu.VMEM((SLICE, SLICE), F32)],
+    )
+    *here, from_seq, rows, low_rank, columns, gate_other, hid_other = lax.optimization_barrier(
+        (*here, from_seq, rows, low_rank, columns, gate_other, hid_other)
+    )
     left = [along_x(here[0], 1), along_x(here[1], 1)]
     right = [along_x(here[0], -1), along_x(here[1], -1)]
 
     c_own = jnp.where(is_first, F32(GUIDE), F32(1.0 - GUIDE))
     c_other = jnp.where(is_first, F32(1.0 - GUIDE), F32(GUIDE))
-    half = lambda v, i: lax.dynamic_slice_in_dim(v, i * 2 * SLICE, 2 * SLICE, 1).astype(F32)
-    lift = half(target, b) - half(noisy, b) + level * (c_own * half(hidden[0], b) + c_other * hid_other.astype(F32))
+    lift = half(target, b).astype(F32) - half(noisy, b).astype(F32)
+    lift = lift + level * (c_own * half(hidden[0], b).astype(F32) + c_other * hid_other.astype(F32))
     lift = jnp.stack([lift[:, :SLICE], lift[:, SLICE:]])
     take = lambda i: lax.dynamic_index_in_dim(lift, i, 0, keepdims=False)
     lift_near = take(s)
     lift_far = take(1 - s)
-
     cut = lambda v: lax.dynamic_slice_in_dim(v, q * SLICE, SLICE, 0)
     a_own = (-level * c_own * cut(gate_row))[None]
     a_other = (-level * c_other * cut(gate_other))[None]
@@ -295,12 +294,8 @@
     from_both = swap(from_seq, "branch")
     opposite = [along_x(left[0], 1), along_x(right[1], -1)]
     near_weights = here + left + right
-    far_rows, far_low_rank, base, far_base = call(
-        far_kernel,
-        ranks + [((TOK, SLICE), F32)] * 2,
-        2 * 256 * 128 * 3600,
-        by_x(from_seq), by_x(from_both), by_x(adapter_down_map), low_rank, up_slice, lift_near, lift_far, a_own, a_other,
-        places=places,
+    far_rows, far_low_rank, far_columns = call(
+        features, kinds, 2 * 256 * 128 * 2432, from_seq, from_both, by_x(adapter_down_map), places=slots,
     )
     product = call(
         near_kernel, [((4 * TOK, SLICE), F32)], 2 * 512 * 1824 * 608, rows, far_rows, *near_weights,
@@ -309,7 +304,7 @@
         forward_kernel,
         [((4 * TOK, SLICE), BF16), ((4 * TOK, RANK), F32)],
         2 * 512 * 608 * 736,
-        product, rows, far_rows, *opposite, base, far_base, a_own, a_other, up_slice,
+        product, rows, far_rows, *opposite, low_rank, far_low_rank, lift_near, lift_far, a_own, a_other, up_slice,
     )
 
     blocks = lambda v, *which: jnp.concatenate([v[i * TOK:(i + 1) * TOK] for i in which], 0)
@@ -317,18 +312,21 @@
     pair = low_part + blocks(from_core, 1, 0, 3, 2)
     from_chip = swap(pair.astype(BF16), "seq")
     term_up = (ADAPTER_STRENGTH * dot_tn(before, jnp.concatenate([low_rank, far_low_rank], 0))).astype(BF16)
-    tokens = [v.reshape(ZH, SLICE, TOK) for v in (own, from_branch, from_seq, from_both)]
-    terms = terms_of(q, pair, from_chip, term_up, tokens)
+    terms = call(
+        terms_kernel, [((PLANE, 40, RANK), BF16)], 2 * 512 * 768 * 128,
+        pair, from_chip, term_up, jnp.asarray(SPREAD, BF16), columns, far_columns,
+    )[0]
     keep, send = backward(places, before, low_part, adapter_down_map, near_weights + opposite)
     terms, send, keep = lax.optimization_barrier((terms, send, keep))
     spread = lax.all_to_all(terms, "dp", 0, 0, axis_index_groups=XY_GROUPS)
     plane_sum = jnp.sum(spread.astype(F32), axis=0)
     total = z_transposed(plane_sum, 0) + z_transposed(plane_sum, 1)
-    total = total + swap(total, "branch")
 
     shape = (ZH, XN, YN * ROWS, TOK)
     home, cross = call(join_kernel, [(shape, F32), (shape, BF16)], 2 * 2432 * 256, keep, swap(send, "branch"))
     grad = call(finish_kernel, [((TOK, MODEL_WIDTH), BF16)], 2432 * 128, home, swap(cross, "seq"))[0]
+    total, grad = lax.optimization_barrier((total, grad))
+    total = total + swap(total, "branch")
     return (grad[None], total[:ROWS], total[ROWS:2 * ROWS])
 
 

time: 155 us -> 144 us (0.929)
  local copies, waits for them, and re-layouts: 19.9 us -> 9.44 us
    ppermute x2 -> x0, local copies, waits for them, and re-layouts: 2.78 us -> none  [swap(): return lax.ppermute(value, axis, [(0, 1), (1, 0)])]
    slice x1 -> x0, local copies, waits for them, and re-layouts: 2.02 us -> none  [per_device(): here = [square[:SLICE // 2], square[SLICE // 2:]]]
    pallas_call x1 -> x0, Pallas kernels: 1.72 us -> none  [terms_of(): pl.pallas_call(terms_kernel, out_shape=jax.ShapeDtypeStruct((PLANE, 40, R...]
    transpose x2 -> x0, local copies, waits for them, and re-layouts: 1.58 us -> none  [the longest x1 1.46 us: per_device(): own = attn[0].T]
    unnamed x41 -> x33, local copies, waits for them, and re-layouts: 6.9 us -> 5.72 us
    pallas_call x7 -> x9, Pallas kernels: 16.2 us -> 16.6 us  [call(): pl.pallas_call(kernel, out_shape=[jax.ShapeDtypeStruct(shape, kind) for s...]
  transfers between devices with their start and end apart: 21 -> 21, of which waited for: 5 -> 8; matrix products, arithmetic and copies ran while one was open for 7% -> 4% of each run, Pallas kernels for 8% -> 9%
where the time goes in v4:
time: 144 us; the launch traced here: 142 us
  starting transfers between devices  76.2 us (53%)
  blocking collectives  18.1 us (13%)
  Pallas kernels  16.6 us (12%)
  waiting for transfers between devices  15 us (10%)
  local copies, waits for them, and re-layouts  9.44 us (7%)
  other arithmetic  4.01 us (3%)
  between operations  2.61 us (2%)
    ppermute x11, starting transfers between devices, swap(): return lax.ppermute(value, axis, [(0, 1), (1, 0)])  34.1 us
    ppermute x6, starting transfers between devices, along_x(): return lax.ppermute(value, 'dp', pairs)  19.6 us
    all_to_all x1, blocking collectives, to_all(): return lax.all_to_all(copies, 'dp', 0, 0, axis_index_groups=groups)  18.1 us
    pallas_call x9, Pallas kernels, call(): pl.pallas_call(kernel, out_shape=[jax.ShapeDtypeStruct(shape, kind) for s...  16.6 us
    ppermute x2, starting transfers between devices, z_transposed(): return lax.ppermute(value, EVERY, pairs)  9.09 us
    all_to_all x1, starting transfers between devices, to_all(): return lax.all_to_all(copies, 'dp', 0, 0, axis_index_groups=groups)  6.95 us
    all_to_all x1, starting transfers between devices, per_device(): spread = lax.all_to_all(terms, 'dp', 0, 0, axis_index_groups=XY_GROUPS)  6.49 us
    unnamed x33, local copies, waits for them, and re-layouts  5.72 us
  transfers between devices with their start and end apart: 21, of which 8 were waited for; matrix products, arithmetic and copies ran while one was open for 4% of the time, Pallas kernels for 9%

profile of v4, /device:TPU:1, one launch (start us, length us, event | category | flops | bytes accessed | tf_op | source)
XLA Modules:
  0.0 142.3 jit_solution(6300822846163218776)
XLA Ops:
  0.7 0.8 multiply_exponential_fusion
  2.0 18.1 %all_to_all.15 = bf16[4,19,608]{2,1,0:T(8,128)(2,1)S(1)} all-to-all(bf16[4,19,608]{2,1,0:T(8,128)(2,1)S(1)} %broadcast_in_dim.21), channel_id=1, replica_groups={{0,64,128,192},{2,66,130,194},{4,68,132,196},{6,70,134,198},{8,72,136,2..., dimensions={0} | all-to-all | bytes 184832 | tf_op jit(solution)/shard_map/all_to_all | solution.py:73
  20.2 1.0 broadcast_in_dim.22
  21.2 7.0 %all-to-all-start.1 = ((bf16[8,76,608]{2,1,0:T(8,128)(2,1)}), bf16[8,76,608]{2,1,0:T(8,128)(2,1)S(1)}, u32[]{:S(2)}, u32[]{:S(2)}) async-start(bf16[8,76,608]{2,1,0:T(8,128)(2,1)} %broadcast_in_dim.22), calls=%async_computation.1 | async-start | bytes 1638400 | tf_op jit(solution)/shard_map/all_to_all | solution.py:73
  28.2 4.9 %collective-permute-start.1 = (bf16[128,2432]{1,0:T(8,128)(2,1)}, bf16[128,2432]{1,0:T(8,128)(2,1)S(1)}, u32[]{:S(2)}, u32[]{:S(2)}) collective-permute-start(bf16[128,2432]{1,0:T(8,128)(2,1)} %bitcast.own), channel_id=1, source_target_pairs={{0,256},{256,0},{1,257},{257,1},{2,258},{258,2},{3,259},{259,3},{4... | collective-permute-start | bytes 1867784 | tf_op jit(solution)/shard_map/ppermute | solution.py:32
  33.1 2.3 %collective-permute-start = (bf16[128,2432]{1,0:T(8,128)(2,1)}, bf16[128,2432]{1,0:T(8,128)(2,1)}, u32[]{:S(2)}, u32[]{:S(2)}) collective-permute-start(bf16[128,2432]{1,0:T(8,128)(2,1)} %bitcast.own), channel_id=1, source_target_pairs={{0,1},{1,0},{2,3},{3,2},{4,5},{5,4},{6,7},{7,6},{8,9},{9,8},{10,11... | collective-permute-start | bytes 1867784 | tf_op jit(solution)/shard_map/ppermute | solution.py:32
  36.2 2.2 %collective-permute-start.2 = (f32[2432]{0:T(1024)S(1)}, f32[2432]{0:T(1024)}, u32[]{:S(2)}, u32[]{:S(2)}) collective-permute-start(f32[2432]{0:T(1024)S(1)} %fusion.10), channel_id=1, source_target_pairs={{0,256},{256,0},{1,257},{257,1},{2,258},{258,2},{3,259},{259,3},{4... | collective-permute-start | bytes 29192 | tf_op jit(solution)/shard_map/ppermute | solution.py:32
  39.2 0.6 gather_fusion
  39.8 0.9 dynamic-slice_bitcast_fusion
  40.7 2.1 %collective-permute-start.3 = (bf16[128,1216]{1,0:T(8,128)(2,1)}, bf16[128,1216]{1,0:T(8,128)(2,1)}, u32[]{:S(2)}, u32[]{:S(2)}) collective-permute-start(bf16[128,1216]{1,0:T(8,128)(2,1)} %dynamic-slice_bitcast_fusion), channel_id=1, source_target_pairs={{0,256},{256,0},{1,257},{257,1},{2,258},{258,2},{3,259},{259,3},{4... | collective-permute-start | bytes 933896 | tf_op jit(solution)/shard_map/ppermute | solution.py:32
  43.1 0.8 copy-done.5
  43.9 1.1 copy-done.6
  45.0 2.3 %shard_map.149 = (bf16[4,256,608]{2,1,0:T(8,128)(2,1)S(1)}, bf16[256,128]{1,0:T(8,128)(2,1)S(1)}, bf16[608,256]{1,0:T(8,128)(2,1)S(1)}) custom-call(s32[5]{0:T(128)S(1)} %pad_add_fusion.slots, bf16[128,2432]{1,0:T(8,128)(2,1)} %bitcast.own, bf16[128,2432]{1,0:T(8,128)(2,1)S(1)} %copy-done.6, bf16[4,4,152,128]{3,2,1,0:T(8,128)(2,1)S(1)} %bitcast.40), custom_call_target="tpu_custom_call" | custom-call | bytes 3489812 | tf_op jit(solution)/shard_map/pallas_call | solution.py:124
  47.3 0.7 copy-done.7
  48.0 0.6 copy-done.9
  48.7 1.1 all-to-all-done.1.lined
  50.0 0.9 collective-permute-done.own
  50.9 4.4 %collective-permute-start.7 = (bf16[304,608]{1,0:T(8,128)(2,1)S(1)}, bf16[304,608]{1,0:T(8,128)(2,1)S(1)}, u32[]{:S(2)}, u32[]{:S(2)}) collective-permute-start(bf16[304,608]{1,0:T(8,128)(2,1)S(1)} %get-tuple-element.42.refs_0_), channel_id=1, source_target_pairs={{0,48},{2,50},{4,52},{6,54},{8,56},{10,58},{12,60},{14,62},{16,0},... | collective-permute-start | bytes 1109000 | tf_op jit(solution)/shard_map/ppermute | solution.py:82
  55.3 1.9 %collective-permute-start.5 = (bf16[304,608]{1,0:T(8,128)(2,1)S(1)}, bf16[304,608]{1,0:T(8,128)(2,1)S(1)}, u32[]{:S(2)}, u32[]{:S(2)}) collective-permute-start(bf16[304,608]{1,0:T(8,128)(2,1)S(1)} %get-tuple-element.42.refs_0_), channel_id=1, source_target_pairs={{0,16},{2,18},{4,20},{6,22},{8,24},{10,26},{12,28},{14,30},{16,32}... | collective-permute-start | bytes 1109000 | tf_op jit(solution)/shard_map/ppermute | solution.py:82
  57.3 4.6 %collective-permute-start.8 = (bf16[304,608]{1,0:T(8,128)(2,1)S(1)}, bf16[304,608]{1,0:T(8,128)(2,1)S(1)}, u32[]{:S(2)}, u32[]{:S(2)}) collective-permute-start(bf16[304,608]{1,0:T(8,128)(2,1)S(1)} %get-tuple-element.43.refs_1_), channel_id=1, source_target_pairs={{0,48},{2,50},{4,52},{6,54},{8,56},{10,58},{12,60},{14,62},{16,0},... | collective-permute-start | bytes 1109000 | tf_op jit(solution)/shard_map/ppermute | solution.py:82
  61.8 1.9 %collective-permute-start.6 = (bf16[304,608]{1,0:T(8,128)(2,1)S(1)}, bf16[304,608]{1,0:T(8,128)(2,1)S(1)}, u32[]{:S(2)}, u32[]{:S(2)}) collective-permute-start(bf16[304,608]{1,0:T(8,128)(2,1)S(1)} %get-tuple-element.43.refs_1_), channel_id=1, source_target_pairs={{0,16},{2,18},{4,20},{6,22},{8,24},{10,26},{12,28},{14,30},{16,32}... | collective-permute-start | bytes 1109000 | tf_op jit(solution)/shard_map/ppermute | solution.py:82
  63.8 5.1 %collective-permute-start.4 = (bf16[128,2432]{1,0:T(8,128)(2,1)}, bf16[128,2432]{1,0:T(8,128)(2,1)S(1)}, u32[]{:S(2)}, u32[]{:S(2)}) collective-permute-start(bf16[128,2432]{1,0:T(8,128)(2,1)} %collective-permute-done.own), channel_id=1, source_target_pairs={{0,256},{256,0},{1,257},{257,1},{2,258},{258,2},{3,259},{259,3},{4... | collective-permute-start | bytes 1867784 | tf_op jit(solution)/shard_map/ppermute | solution.py:32
  68.8 1.8 %fusion.2 = f32[128,1216]{1,0:T(8,128)S(1)} fusion(bf16[128,1216]{1,0:T(8,128)(2,1)} %collective-permute-done.3, f32[]{:T(128)S(6)} %select_n.89, bf16[1,128,2432]{2,1,0:T(8,128)(2,1)} %param.14, s32[]{:T(128)S(6)} %select_n.87, f32[]{:T(128)S(6)} %select_n.88, f32[]{:T(128)} %bitcast.7, bf16[128,2432]{1,0:T(8,128)(2,1)} %param.15, bf16[128,2432]{1,0:T(8,128)(2,1)} %param.16), kind=kLoop, calls=%fused_computation.9 | loop fusion | flops 1556480 | bytes 1867792 | tf_op jit(solution)/shard_map/add | solution.py:284
  70.8 1.9 %collective-permute-start.9 = (bf16[304,608]{1,0:T(8,128)(2,1)S(1)}, bf16[304,608]{1,0:T(8,128)(2,1)S(1)}, u32[]{:S(2)}, u32[]{:S(2)}) collective-permute-start(bf16[304,608]{1,0:T(8,128)(2,1)S(1)} %collective-permute-done.5.refs_2_), channel_id=1, source_target_pairs={{0,16},{2,18},{4,20},{6,22},{8,24},{10,26},{12,28},{14,30},{16,32}... | collective-permute-start | bytes 1109000 | tf_op jit(solution)/shard_map/ppermute | solution.py:82
  72.7 4.9 %collective-permute-start.10 = (bf16[304,608]{1,0:T(8,128)(2,1)S(1)}, bf16[304,608]{1,0:T(8,128)(2,1)S(1)}, u32[]{:S(2)}, u32[]{:S(2)}) collective-permute-start(bf16[304,608]{1,0:T(8,128)(2,1)S(1)} %collective-permute-done.8.refs_5_), channel_id=1, source_target_pairs={{0,48},{2,50},{4,52},{6,54},{8,56},{10,58},{12,60},{14,62},{16,0},... | collective-permute-start | bytes 1109000 | tf_op jit(solution)/shard_map/ppermute | solution.py:82
  77.8 3.0 %collective-permute-start.11 = (f32[128,608]{1,0:T(8,128)S(1)}, f32[128,608]{1,0:T(8,128)S(1)}, u32[]{:S(2)}, u32[]{:S(2)}) collective-permute-start(f32[128,608]{1,0:T(8,128)S(1)} %get-tuple-element.63), channel_id=1, source_target_pairs={{0,1},{1,0},{2,3},{3,2},{4,5},{5,4},{6,7},{7,6},{8,9},{9,8},{10,11... | collective-permute-start | bytes 933896 | tf_op jit(solution)/shard_map/ppermute | solution.py:32
  80.9 0.8 dynamic-slice_multiply_fusion
  81.7 2.3 %shard_map.150 = (bf16[4,256,608]{2,1,0:T(8,128)(2,1)S(1)}, bf16[256,128]{1,0:T(8,128)(2,1)S(1)}, bf16[608,256]{1,0:T(8,128)(2,1)S(1)}) custom-call(s32[5]{0:T(128)S(1)} %pad_add_fusion.slots, bf16[128,2432]{1,0:T(8,128)(2,1)} %collective-permute-done.own, bf16[128,2432]{1,0:T(8,128)(2,1)S(1)} %collective-permute-done.4.other, ...), custom_call_target="tpu_custom_call" | custom-call | flops 159383552 | bytes 3489812 | tf_op jit(solution)/shard_map/pallas_call | solution.py:124
  84.0 1.9 %shard_map.151.product = f32[512,608]{1,0:T(8,128)S(1)} custom-call(bf16[4,256,608]{2,1,0:T(8,128)(2,1)S(1)} %get-tuple-element.39.rows, bf16[4,256,608]{2,1,0:T(8,128)(2,1)S(1)} %get-tuple-element.41.far_rows, bf16[304,608]{1,0:T(8,128)(2,1)S(1)} %get-tuple-element.42.refs_0_, bf16[304,608]{1,0:T(8,128)(2,1)S(1)} %get-tuple-element.43.refs_1_, ...), custom_call_target="tpu_custom_call" | custom-call | flops 1135607808 | bytes 5953536 | tf_op jit(solution)/shard_map/pallas_call | solution.py:124
  86.0 1.8 %collective-permute-done.11.far_lift = f32[128,608]{1,0:T(8,128)S(1)} collective-permute-done((f32[128,608]{1,0:T(8,128)S(1)}, f32[128,608]{1,0:T(8,128)S(1)}, u32[]{:S(2)}, u32[]{:S(2)}) %collective-permute-start.11) | collective-permute-done | bytes 311328 | tf_op jit(solution)/shard_map/ppermute | solution.py:32
  87.8 1.5 %shard_map.152 = (bf16[512,608]{1,0:T(8,128)(2,1)S(1)}, f32[512,128]{1,0:T(8,128)S(1)}) custom-call(f32[512,608]{1,0:T(8,128)S(1)} %shard_map.151.product, bf16[4,256,608]{2,1,0:T(8,128)(2,1)S(1)} %get-tuple-element.39.rows, bf16[4,256,608]{2,1,0:T(8,128)(2,1)S(1)} %get-tuple-element.41.far_rows, bf16[304,608]{1,0:T(8,128)(2,1)S(1)} %collective-permute-done.9.upper.refs_6_, ...), custom_call_target="tpu_custom_call" | custom-call | flops 458227712 | bytes 6273792 | tf_op jit(solution)/shard_map/pallas_call | solution.py:124
  89.2 3.9 %collective-permute-start.12 = (bf16[512,128]{1,0:T(8,128)(2,1)S(1)}, bf16[512,128]{1,0:T(8,128)(2,1)S(1)}, u32[]{:S(2)}, u32[]{:S(2)}) collective-permute-start(bf16[512,128]{1,0:T(8,128)(2,1)S(1)} %convert_element_type.57), channel_id=1, source_target_pairs={{0,256},{256,0},{1,257},{257,1},{2,258},{258,2},{3,259},{259,3},{4... | collective-permute-start | bytes 393224 | tf_op jit(solution)/shard_map/ppermute | solution.py:32
  94.3 3.3 %collective-permute-start.13 = (bf16[512,128]{1,0:T(8,128)(2,1)S(1)}, bf16[512,128]{1,0:T(8,128)(2,1)S(1)}, u32[]{:S(2)}, u32[]{:S(2)}) collective-permute-start(bf16[512,128]{1,0:T(8,128)(2,1)S(1)} %get-tuple-element.61), channel_id=1, source_target_pairs={{0,1},{1,0},{2,3},{3,2},{4,5},{5,4},{6,7},{7,6},{8,9},{9,8},{10,11... | collective-permute-start | bytes 393224 | tf_op jit(solution)/shard_map/ppermute | solution.py:32
  97.6 4.4 %shard_map.154 = (bf16[4,4,152,256]{3,2,1,0:T(8,128)(2,1)S(1)}, bf16[4,4,152,256]{3,2,1,0:T(8,128)(2,1)}) custom-call(s32[4]{0:T(128)S(1)} %pad_add_fusion.1.places, bf16[512,608]{1,0:T(8,128)(2,1)S(1)} %get-tuple-element.49.before, f32[512,128]{1,0:T(8,128)S(1)} %get-tuple-element.48.low, bf16[4,4,152,128]{3,2,1,0:T(8,128)(2,1)S(1)} %bitcast.42, ...), custom_call_target="tpu_custom_call" | custom-call | flops 1832910848 | bytes 6955024 | tf_op jit(solution)/shard_map/pallas_call | solution.py:124
  102.0 1.7 %shard_map.153 = bf16[32,40,128]{2,1,0:T(8,128)(2,1)} custom-call(f32[512,128]{1,0:T(8,128)S(1)} %get-tuple-element.62.pair, bf16[512,128]{1,0:T(8,128)(2,1)S(1)} %collective-permute-done.13.far, bf16[608,128]{1,0:T(8,128)(2,1)S(1)} %fusion.up, bf16[768,608]{1,0:T(8,128)(2,1)S(1)} %copy-done.4, bf16[608,256]{1,0:T(8,128)(2,1)S(1)} %copy-done.8, ...), custom_call_target="tpu_custom_call" | custom-call | flops 100663296 | bytes 2433024 | tf_op jit(solution)/shard_map/pallas_call | solution.py:124
  103.7 2.5 %collective-permute-start.16 = (bf16[4,4,152,256]{3,2,1,0:T(8,128)(2,1)}, bf16[4,4,152,256]{3,2,1,0:T(8,128)(2,1)S(1)}, u32[]{:S(2)}, u32[]{:S(2)}) collective-permute-start(bf16[4,4,152,256]{3,2,1,0:T(8,128)(2,1)} %get-tuple-element.56), channel_id=1, source_target_pairs={{0,256},{256,0},{1,257},{257,1},{2,258},{258,2},{3,259},{259,3},{4... | collective-permute-start | bytes 3735560 | tf_op jit(solution)/shard_map/ppermute | solution.py:32
  106.3 6.5 %all-to-all-start.2 = ((bf16[32,40,128]{2,1,0:T(8,128)(2,1)}), bf16[32,40,128]{2,1,0:T(8,128)(2,1)S(1)}, u32[]{:S(2)}, u32[]{:S(2)}) async-start(bf16[32,40,128]{2,1,0:T(8,128)(2,1)} %shard_map.153), calls=%async_computation.2 | async-start | bytes 655360 | tf_op jit(solution)/shard_map/all_to_all | solution.py:321
  112.8 1.1 copy-done.2
  113.9 1.3 copy-done.3
  115.2 1.0 shard_map.155
  116.2 2.7 %collective-permute-start.17 = (bf16[4,4,152,128]{3,2,1,0:T(8,128)(2,1)}, bf16[4,4,152,128]{3,2,1,0:T(8,128)(2,1)S(1)}, u32[]{:S(2)}, u32[]{:S(2)}) collective-permute-start(bf16[4,4,152,128]{3,2,1,0:T(8,128)(2,1)} %get-tuple-element.58), channel_id=1, source_target_pairs={{0,1},{1,0},{2,3},{3,2},{4,5},{5,4},{6,7},{7,6},{8,9},{9,8},{10,11... | collective-permute-start | bytes 1867784 | tf_op jit(solution)/shard_map/ppermute | solution.py:32
  118.9 5.2 %all-to-all-done.2 = bf16[32,40,128]{2,1,0:T(8,128)(2,1)S(1)} async-done(((bf16[32,40,128]{2,1,0:T(8,128)(2,1)}), bf16[32,40,128]{2,1,0:T(8,128)(2,1)S(1)}, u32[]{:S(2)}, u32[]{:S(2)}) %all-to-all-start.2) | async-done | bytes 327712 | tf_op jit(solution)/shard_map/all_to_all | solution.py:321
  124.2 4.3 %collective-permute-start.15 = (f32[40,128]{1,0:T(8,128)S(1)}, f32[40,128]{1,0:T(8,128)S(1)}, u32[]{:S(2)}, u32[]{:S(2)}) collective-permute-start(f32[40,128]{1,0:T(8,128)S(1)} %convert_reduce_fusion), channel_id=1, source_target_pairs={{0,1},{1,65},{256,129},{257,193},{2,3},{3,67},{258,131},{259,195},... | collective-permute-start | bytes 61448 | tf_op jit(solution)/shard_map/ppermute | solution.py:96
  128.5 4.8 %collective-permute-start.14 = (f32[40,128]{1,0:T(8,128)S(1)}, f32[40,128]{1,0:T(8,128)S(1)}, u32[]{:S(2)}, u32[]{:S(2)}) collective-permute-start(f32[40,128]{1,0:T(8,128)S(1)} %convert_reduce_fusion), channel_id=1, source_target_pairs={{0,0},{1,64},{256,128},{257,192},{2,2},{3,66},{258,130},{259,194},... | collective-permute-start | bytes 61448 | tf_op jit(solution)/shard_map/ppermute | solution.py:96
  133.8 3.6 %collective-permute-done.14 = f32[40,128]{1,0:T(8,128)S(1)} collective-permute-done((f32[40,128]{1,0:T(8,128)S(1)}, f32[40,128]{1,0:T(8,128)S(1)}, u32[]{:S(2)}, u32[]{:S(2)}) %collective-permute-start.14) | collective-permute-done | bytes 20512 | tf_op jit(solution)/shard_map/ppermute | solution.py:96
  137.5 1.1 shard_map.156
  138.6 1.9 %collective-permute-start.18 = (f32[40,128]{1,0:T(8,128)S(1)}, f32[40,128]{1,0:T(8,128)S(1)}, u32[]{:S(2)}, u32[]{:S(2)}) collective-permute-start(f32[40,128]{1,0:T(8,128)S(1)} %add.112), channel_id=1, source_target_pairs={{0,256},{256,0},{1,257},{257,1},{2,258},{258,2},{3,259},{259,3},{4... | collective-permute-start | bytes 61448 | tf_op jit(solution)/shard_map/ppermute | solution.py:32
  140.5 1.2 collective-permute-done.18
  (69 shorter events, 3.8 us)
Async XLA Ops:
  0.6 42.3 %copy-start = (bf16[2432,128]{1,0:T(8,128)(2,1)S(1)}, bf16[2432,128]{1,0:T(8,128)(2,1)}, u32[]{:S(2)}) copy-start(bf16[2432,128]{1,0:T(8,128)(2,1)} %param.20) | copy-start | bytes 1867780
  0.6 1.0 copy-start.13
  20.2 15.9 %copy-start.14 = (f32[1,8,2432]{2,1,0:T(8,128)S(1)}, f32[1,8,2432]{2,1,0:T(8,128)}, u32[]{:S(2)}) copy-start(f32[1,8,2432]{2,1,0:T(8,128)} %param.21) | copy-start | bytes 233476
  20.2 18.9 %copy-start.11 = (s32[4]{0:T(128)S(1)}, s32[4]{0:T(128)}, u32[]{:S(2)}) copy-start(s32[4]{0:T(128)} %constant.117.clone) | copy-start | bytes 52
  21.2 18.6 %copy-start.12 = (bf16[1,128,2432]{2,1,0:T(8,128)(2,1)S(1)}, bf16[1,128,2432]{2,1,0:T(8,128)(2,1)}, u32[]{:S(2)}) copy-start(bf16[1,128,2432]{2,1,0:T(8,128)(2,1)} %param.14) | copy-start | bytes 1867780
  21.2 28.5 %all-to-all-start.1 = ((bf16[8,76,608]{2,1,0:T(8,128)(2,1)}), bf16[8,76,608]{2,1,0:T(8,128)(2,1)S(1)}, u32[]{:S(2)}, u32[]{:S(2)}) async-start(bf16[8,76,608]{2,1,0:T(8,128)(2,1)} %broadcast_in_dim.22), calls=%async_computation.1 | async-start | bytes 1638400 | tf_op jit(solution)/shard_map/all_to_all | solution.py:73
  28.2 15.7 %copy-start.1 = (bf16[2432,128]{1,0:T(8,128)(2,1)S(1)}, bf16[2432,128]{1,0:T(8,128)(2,1)}, u32[]{:S(2)}) copy-start(bf16[2432,128]{1,0:T(8,128)(2,1)} %param.19) | copy-start | bytes 1867780
  28.2 14.9 %collective-permute-start.1 = (bf16[128,2432]{1,0:T(8,128)(2,1)}, bf16[128,2432]{1,0:T(8,128)(2,1)S(1)}, u32[]{:S(2)}, u32[]{:S(2)}) collective-permute-start(bf16[128,2432]{1,0:T(8,128)(2,1)} %bitcast.own), channel_id=1, source_target_pairs={{0,256},{256,0},{1,257},{257,1},{2,258},{258,2},{3,259},{259,3},{4... | collective-permute-start | bytes 1867784 | tf_op jit(solution)/shard_map/ppermute | solution.py:32
  33.1 17.9 %collective-permute-start = (bf16[128,2432]{1,0:T(8,128)(2,1)}, bf16[128,2432]{1,0:T(8,128)(2,1)}, u32[]{:S(2)}, u32[]{:S(2)}) collective-permute-start(bf16[128,2432]{1,0:T(8,128)(2,1)} %bitcast.own), channel_id=1, source_target_pairs={{0,1},{1,0},{2,3},{3,2},{4,5},{5,4},{6,7},{7,6},{8,9},{9,8},{10,11... | collective-permute-start | bytes 1867784 | tf_op jit(solution)/shard_map/ppermute | solution.py:32
  36.2 13.8 %collective-permute-start.2 = (f32[2432]{0:T(1024)S(1)}, f32[2432]{0:T(1024)}, u32[]{:S(2)}, u32[]{:S(2)}) collective-permute-start(f32[2432]{0:T(1024)S(1)} %fusion.10), channel_id=1, source_target_pairs={{0,256},{256,0},{1,257},{257,1},{2,258},{258,2},{3,259},{259,3},{4... | collective-permute-start | bytes 29192 | tf_op jit(solution)/shard_map/ppermute | solution.py:32
  40.7 9.3 %collective-permute-start.3 = (bf16[128,1216]{1,0:T(8,128)(2,1)}, bf16[128,1216]{1,0:T(8,128)(2,1)}, u32[]{:S(2)}, u32[]{:S(2)}) collective-permute-start(bf16[128,1216]{1,0:T(8,128)(2,1)} %dynamic-slice_bitcast_fusion), channel_id=1, source_target_pairs={{0,256},{256,0},{1,257},{257,1},{2,258},{258,2},{3,259},{259,3},{4... | collective-permute-start | bytes 933896 | tf_op jit(solution)/shard_map/ppermute | solution.py:32
  43.1 0.8 copy-start.5
  43.9 1.1 copy-start.6
  47.3 0.7 copy-start.7
  48.0 0.6 copy-start.9
  50.9 33.1 %collective-permute-start.7 = (bf16[304,608]{1,0:T(8,128)(2,1)S(1)}, bf16[304,608]{1,0:T(8,128)(2,1)S(1)}, u32[]{:S(2)}, u32[]{:S(2)}) collective-permute-start(bf16[304,608]{1,0:T(8,128)(2,1)S(1)} %get-tuple-element.42.refs_0_), channel_id=1, source_target_pairs={{0,48},{2,50},{4,52},{6,54},{8,56},{10,58},{12,60},{14,62},{16,0},... | collective-permute-start | bytes 1109000 | tf_op jit(solution)/shard_map/ppermute | solution.py:82
  55.3 15.5 %collective-permute-start.5 = (bf16[304,608]{1,0:T(8,128)(2,1)S(1)}, bf16[304,608]{1,0:T(8,128)(2,1)S(1)}, u32[]{:S(2)}, u32[]{:S(2)}) collective-permute-start(bf16[304,608]{1,0:T(8,128)(2,1)S(1)} %get-tuple-element.42.refs_0_), channel_id=1, source_target_pairs={{0,16},{2,18},{4,20},{6,22},{8,24},{10,26},{12,28},{14,30},{16,32}... | collective-permute-start | bytes 1109000 | tf_op jit(solution)/shard_map/ppermute | solution.py:82
  57.3 15.5 %collective-permute-start.8 = (bf16[304,608]{1,0:T(8,128)(2,1)S(1)}, bf16[304,608]{1,0:T(8,128)(2,1)S(1)}, u32[]{:S(2)}, u32[]{:S(2)}) collective-permute-start(bf16[304,608]{1,0:T(8,128)(2,1)S(1)} %get-tuple-element.43.refs_1_), channel_id=1, source_target_pairs={{0,48},{2,50},{4,52},{6,54},{8,56},{10,58},{12,60},{14,62},{16,0},... | collective-permute-start | bytes 1109000 | tf_op jit(solution)/shard_map/ppermute | solution.py:82
  61.8 22.2 %collective-permute-start.6 = (bf16[304,608]{1,0:T(8,128)(2,1)S(1)}, bf16[304,608]{1,0:T(8,128)(2,1)S(1)}, u32[]{:S(2)}, u32[]{:S(2)}) collective-permute-start(bf16[304,608]{1,0:T(8,128)(2,1)S(1)} %get-tuple-element.43.refs_1_), channel_id=1, source_target_pairs={{0,16},{2,18},{4,20},{6,22},{8,24},{10,26},{12,28},{14,30},{16,32}... | collective-permute-start | bytes 1109000 | tf_op jit(solution)/shard_map/ppermute | solution.py:82
  63.8 14.0 %collective-permute-start.4 = (bf16[128,2432]{1,0:T(8,128)(2,1)}, bf16[128,2432]{1,0:T(8,128)(2,1)S(1)}, u32[]{:S(2)}, u32[]{:S(2)}) collective-permute-start(bf16[128,2432]{1,0:T(8,128)(2,1)} %collective-permute-done.own), channel_id=1, source_target_pairs={{0,256},{256,0},{1,257},{257,1},{2,258},{258,2},{3,259},{259,3},{4... | collective-permute-start | bytes 1867784 | tf_op jit(solution)/shard_map/ppermute | solution.py:32
  70.8 16.9 %collective-permute-start.9 = (bf16[304,608]{1,0:T(8,128)(2,1)S(1)}, bf16[304,608]{1,0:T(8,128)(2,1)S(1)}, u32[]{:S(2)}, u32[]{:S(2)}) collective-permute-start(bf16[304,608]{1,0:T(8,128)(2,1)S(1)} %collective-permute-done.5.refs_2_), channel_id=1, source_target_pairs={{0,16},{2,18},{4,20},{6,22},{8,24},{10,26},{12,28},{14,30},{16,32}... | collective-permute-start | bytes 1109000 | tf_op jit(solution)/shard_map/ppermute | solution.py:82
  72.7 15.0 %collective-permute-start.10 = (bf16[304,608]{1,0:T(8,128)(2,1)S(1)}, bf16[304,608]{1,0:T(8,128)(2,1)S(1)}, u32[]{:S(2)}, u32[]{:S(2)}) collective-permute-start(bf16[304,608]{1,0:T(8,128)(2,1)S(1)} %collective-permute-done.8.refs_5_), channel_id=1, source_target_pairs={{0,48},{2,50},{4,52},{6,54},{8,56},{10,58},{12,60},{14,62},{16,0},... | collective-permute-start | bytes 1109000 | tf_op jit(solution)/shard_map/ppermute | solution.py:82
  77.8 10.0 %collective-permute-start.11 = (f32[128,608]{1,0:T(8,128)S(1)}, f32[128,608]{1,0:T(8,128)S(1)}, u32[]{:S(2)}, u32[]{:S(2)}) collective-permute-start(f32[128,608]{1,0:T(8,128)S(1)} %get-tuple-element.63), channel_id=1, source_target_pairs={{0,1},{1,0},{2,3},{3,2},{4,5},{5,4},{6,7},{7,6},{8,9},{9,8},{10,11... | collective-permute-start | bytes 933896 | tf_op jit(solution)/shard_map/ppermute | solution.py:32
  84.0 3.7 %copy-start.10 = (bf16[256,128]{1,0:T(8,128)(2,1)S(1)}, bf16[256,128]{1,0:T(8,128)(2,1)}, u32[]{:S(2)}) copy-start(bf16[256,128]{1,0:T(8,128)(2,1)} %copy-done.9) | copy-start | bytes 196612
  89.2 4.9 %collective-permute-start.12 = (bf16[512,128]{1,0:T(8,128)(2,1)S(1)}, bf16[512,128]{1,0:T(8,128)(2,1)S(1)}, u32[]{:S(2)}, u32[]{:S(2)}) collective-permute-start(bf16[512,128]{1,0:T(8,128)(2,1)S(1)} %convert_element_type.57), channel_id=1, source_target_pairs={{0,256},{256,0},{1,257},{257,1},{2,258},{258,2},{3,259},{259,3},{4... | collective-permute-start | bytes 393224 | tf_op jit(solution)/shard_map/ppermute | solution.py:32
  94.2 7.8 %copy-start.4 = (bf16[768,608]{1,0:T(8,128)(2,1)S(1)}, bf16[768,608]{1,0:T(8,128)(2,1)}, u32[]{:S(2)}) copy-start(bf16[768,608]{1,0:T(8,128)(2,1)} %constant.118.clone.spread) | copy-start | bytes 2801668
  94.2 7.8 %copy-start.8 = (bf16[608,256]{1,0:T(8,128)(2,1)S(1)}, bf16[608,256]{1,0:T(8,128)(2,1)}, u32[]{:S(2)}) copy-start(bf16[608,256]{1,0:T(8,128)(2,1)} %copy-done.7) | copy-start | bytes 933892
  94.3 7.8 %collective-permute-start.13 = (bf16[512,128]{1,0:T(8,128)(2,1)S(1)}, bf16[512,128]{1,0:T(8,128)(2,1)S(1)}, u32[]{:S(2)}, u32[]{:S(2)}) collective-permute-start(bf16[512,128]{1,0:T(8,128)(2,1)S(1)} %get-tuple-element.61), channel_id=1, source_target_pairs={{0,1},{1,0},{2,3},{3,2},{4,5},{5,4},{6,7},{7,6},{8,9},{9,8},{10,11... | collective-permute-start | bytes 393224 | tf_op jit(solution)/shard_map/ppermute | solution.py:32
  103.7 9.0 %collective-permute-start.16 = (bf16[4,4,152,256]{3,2,1,0:T(8,128)(2,1)}, bf16[4,4,152,256]{3,2,1,0:T(8,128)(2,1)S(1)}, u32[]{:S(2)}, u32[]{:S(2)}) collective-permute-start(bf16[4,4,152,256]{3,2,1,0:T(8,128)(2,1)} %get-tuple-element.56), channel_id=1, source_target_pairs={{0,256},{256,0},{1,257},{257,1},{2,258},{258,2},{3,259},{259,3},{4... | collective-permute-start | bytes 3735560 | tf_op jit(solution)/shard_map/ppermute | solution.py:32
  106.3 17.8 %all-to-all-start.2 = ((bf16[32,40,128]{2,1,0:T(8,128)(2,1)}), bf16[32,40,128]{2,1,0:T(8,128)(2,1)S(1)}, u32[]{:S(2)}, u32[]{:S(2)}) async-start(bf16[32,40,128]{2,1,0:T(8,128)(2,1)} %shard_map.153), calls=%async_computation.2 | async-start | bytes 655360 | tf_op jit(solution)/shard_map/all_to_all | solution.py:321
  112.8 1.1 copy-start.2
  113.9 1.3 copy-start.3
  116.2 21.3 %collective-permute-start.17 = (bf16[4,4,152,128]{3,2,1,0:T(8,128)(2,1)}, bf16[4,4,152,128]{3,2,1,0:T(8,128)(2,1)S(1)}, u32[]{:S(2)}, u32[]{:S(2)}) collective-permute-start(bf16[4,4,152,128]{3,2,1,0:T(8,128)(2,1)} %get-tuple-element.58), channel_id=1, source_target_pairs={{0,1},{1,0},{2,3},{3,2},{4,5},{5,4},{6,7},{7,6},{8,9},{9,8},{10,11... | collective-permute-start | bytes 1867784 | tf_op jit(solution)/shard_map/ppermute | solution.py:32
  124.2 9.7 %collective-permute-start.15 = (f32[40,128]{1,0:T(8,128)S(1)}, f32[40,128]{1,0:T(8,128)S(1)}, u32[]{:S(2)}, u32[]{:S(2)}) collective-permute-start(f32[40,128]{1,0:T(8,128)S(1)} %convert_reduce_fusion), channel_id=1, source_target_pairs={{0,1},{1,65},{256,129},{257,193},{2,3},{3,67},{258,131},{259,195},... | collective-permute-start | bytes 61448 | tf_op jit(solution)/shard_map/ppermute | solution.py:96
  128.5 9.0 %collective-permute-start.14 = (f32[40,128]{1,0:T(8,128)S(1)}, f32[40,128]{1,0:T(8,128)S(1)}, u32[]{:S(2)}, u32[]{:S(2)}) collective-permute-start(f32[40,128]{1,0:T(8,128)S(1)} %convert_reduce_fusion), channel_id=1, source_target_pairs={{0,0},{1,64},{256,128},{257,192},{2,2},{3,66},{258,130},{259,194},... | collective-permute-start | bytes 61448 | tf_op jit(solution)/shard_map/ppermute | solution.py:96
  138.6 3.1 %collective-permute-start.18 = (f32[40,128]{1,0:T(8,128)S(1)}, f32[40,128]{1,0:T(8,128)S(1)}, u32[]{:S(2)}, u32[]{:S(2)}) collective-permute-start(f32[40,128]{1,0:T(8,128)S(1)} %add.112), channel_id=1, source_target_pairs={{0,256},{256,0},{1,257},{257,1},{2,258},{258,2},{3,259},{259,3},{4... | collective-permute-start | bytes 61448 | tf_op jit(solution)/shard_map/ppermute | solution.py:32

commit v5 on v4

--- a/solution.py
+++ b/solution.py
@@ -179,7 +179,7 @@
     for i, (ref, ranks, lifts) in enumerate(((rows, rank, lift), (far_rows, far_rank, far_lift))):
         part = slice(2 * TOK * i, 2 * TOK * (i + 1))
         whole = product[part] + dot_nn(ref[XN - 1], weight) + ADAPTER_STRENGTH * dot_nt(ranks[...], up[...])
-        reward_grad = REWARD * (lifts[...] - first * whole[:TOK] - second * whole[TOK:])
+        reward_grad = REWARD * (lifts[...].astype(F32) - first * whole[:TOK] - second * whole[TOK:])
         grad = jnp.concatenate([first * reward_grad, second * reward_grad], 0).astype(BF16)
         before[part] = grad
         low[part] = dot_nn(grad, up[...])
@@ -261,7 +261,7 @@
     slots = jnp.array([0, 2, 3, 1], jnp.int32)[(jnp.arange(XN) - x) % XN]
     slots = jnp.concatenate([slots, q.astype(jnp.int32)[None]])
     kinds = [((XN, 2 * TOK, SLICE), BF16), ((2 * TOK, RANK), BF16), ((SLICE, 2 * TOK), BF16)]
-    rows, low_rank, columns = call(features, kinds, 0, own, from_branch, by_x(adapter_down_map), places=slots)
+    rows, low_rank, columns = call(features, kinds, 2 * 256 * 128 * 2432, own, from_branch, by_x(adapter_down_map), places=slots)
 
     selector = (jnp.arange(gates.shape[1], dtype=jnp.int32) == group_prompt[0]).astype(F32)
     gate_row = jnp.sum(selector[:, None] * gates[0], axis=0)
@@ -270,7 +270,7 @@
     hid_other = swap(half(hidden[0], 1 - b), "branch")
 
     here = call(
-        arrange_kernel, [((SLICE // 2, SLICE), BF16)] * 2, 0, lined, scratch=[pltpu.VMEM((SLICE, SLICE), F32)],
+        arrange_kernel, [((SLICE // 2, SLICE), BF16)] * 2, 1, lined, scratch=[pltpu.VMEM((SLICE, SLICE), F32)],
     )
     *here, from_seq, rows, low_rank, columns, gate_other, hid_other = lax.optimization_barrier(
         (*here, from_seq, rows, low_rank, columns, gate_other, hid_other)
@@ -290,7 +290,7 @@
     a_own = (-level * c_own * cut(gate_row))[None]
     a_other = (-level * c_other * cut(gate_other))[None]
     up_slice = cut(adapter_up_transposed)
-    lift_far = swap(lift_far, "seq")
+    lift_far = swap(lift_far.astype(BF16), "seq")
     from_both = swap(from_seq, "branch")
     opposite = [along_x(left[0], 1), along_x(right[1], -1)]
     near_weights = here + left + right
@@ -324,9 +324,10 @@
 
     shape = (ZH, XN, YN * ROWS, TOK)
     home, cross = call(join_kernel, [(shape, F32), (shape, BF16)], 2 * 2432 * 256, keep, swap(send, "branch"))
-    grad = call(finish_kernel, [((TOK, MODEL_WIDTH), BF16)], 2432 * 128, home, swap(cross, "seq"))[0]
-    total, grad = lax.optimization_barrier((total, grad))
+    across = swap(cross, "seq")
+    total, across = lax.optimization_barrier((total, across))
     total = total + swap(total, "branch")
+    grad = call(finish_kernel, [((TOK, MODEL_WIDTH), BF16)], 2432 * 128, home, across)[0]
     return (grad[None], total[:ROWS], total[ROWS:2 * ROWS])
 
 

time: 144 us -> 142 us (0.986)
  waiting for transfers between devices: 15 us -> 12.1 us
    ppermute x11, waiting for transfers between devices: 4.43 us -> 1.6 us  [swap(): return lax.ppermute(value, axis, [(0, 1), (1, 0)])]
    all_to_all x1, starting transfers between devices: 6.49 us -> 8.75 us  [per_device(): spread = lax.all_to_all(terms, 'dp', 0, 0, axis_index_groups=XY_GROUPS)]
  transfers between devices with their start and end apart: 21 -> 21, of which waited for: 8 -> 7; matrix products, arithmetic and copies ran while one was open for 4% -> 4% of each run, Pallas kernels for 9% -> 9%
where the time goes in v5:
time: 142 us; the launch traced here: 141 us
  starting transfers between devices  77.4 us (55%)
  blocking collectives  18.1 us (13%)
  Pallas kernels  16.5 us (12%)
  waiting for transfers between devices  12.1 us (9%)
  local copies, waits for them, and re-layouts  9.43 us (7%)
  other arithmetic  4.01 us (3%)
  between operations  2.65 us (2%)
    ppermute x11, starting transfers between devices, swap(): return lax.ppermute(value, axis, [(0, 1), (1, 0)])  33 us
    ppermute x6, starting transfers between devices, along_x(): return lax.ppermute(value, 'dp', pairs)  19.6 us
    all_to_all x1, blocking collectives, to_all(): return lax.all_to_all(copies, 'dp', 0, 0, axis_index_groups=groups)  18.1 us
    pallas_call x9, Pallas kernels, call(): pl.pallas_call(kernel, out_shape=[jax.ShapeDtypeStruct(shape, kind) for s...  16.5 us
    ppermute x2, starting transfers between devices, z_transposed(): return lax.ppermute(value, EVERY, pairs)  9.07 us
    all_to_all x1, starting transfers between devices, per_device(): spread = lax.all_to_all(terms, 'dp', 0, 0, axis_index_groups=XY_GROUPS)  8.75 us
    all_to_all x1, starting transfers between devices, to_all(): return lax.all_to_all(copies, 'dp', 0, 0, axis_index_groups=groups)  6.95 us
    unnamed x33, local copies, waits for them, and re-layouts  5.71 us
  transfers between devices with their start and end apart: 21, of which 7 were waited for; matrix products, arithmetic and copies ran while one was open for 4% of the time, Pallas kernels for 9%

profile of v5, /device:TPU:1, one launch (start us, length us, event | category | flops | bytes accessed | tf_op | source)
XLA Modules:
  0.0 140.6 jit_solution(4754212844650057576)
XLA Ops:
  0.7 0.8 multiply_exponential_fusion
  2.0 18.1 %all_to_all.15 = bf16[4,19,608]{2,1,0:T(8,128)(2,1)S(1)} all-to-all(bf16[4,19,608]{2,1,0:T(8,128)(2,1)S(1)} %broadcast_in_dim.21), channel_id=1, replica_groups={{0,64,128,192},{2,66,130,194},{4,68,132,196},{6,70,134,198},{8,72,136,2..., dimensions={0} | all-to-all | bytes 184832 | tf_op jit(solution)/shard_map/all_to_all | solution.py:73
  20.2 1.0 broadcast_in_dim.22
  21.2 7.0 %all-to-all-start.1 = ((bf16[8,76,608]{2,1,0:T(8,128)(2,1)}), bf16[8,76,608]{2,1,0:T(8,128)(2,1)S(1)}, u32[]{:S(2)}, u32[]{:S(2)}) async-start(bf16[8,76,608]{2,1,0:T(8,128)(2,1)} %broadcast_in_dim.22), calls=%async_computation.1 | async-start | bytes 1638400 | tf_op jit(solution)/shard_map/all_to_all | solution.py:73
  28.2 4.9 %collective-permute-start.1 = (bf16[128,2432]{1,0:T(8,128)(2,1)}, bf16[128,2432]{1,0:T(8,128)(2,1)S(1)}, u32[]{:S(2)}, u32[]{:S(2)}) collective-permute-start(bf16[128,2432]{1,0:T(8,128)(2,1)} %bitcast.own), channel_id=1, source_target_pairs={{0,256},{256,0},{1,257},{257,1},{2,258},{258,2},{3,259},{259,3},{4... | collective-permute-start | bytes 1867784 | tf_op jit(solution)/shard_map/ppermute | solution.py:32
  33.1 2.3 %collective-permute-start = (bf16[128,2432]{1,0:T(8,128)(2,1)}, bf16[128,2432]{1,0:T(8,128)(2,1)}, u32[]{:S(2)}, u32[]{:S(2)}) collective-permute-start(bf16[128,2432]{1,0:T(8,128)(2,1)} %bitcast.own), channel_id=1, source_target_pairs={{0,1},{1,0},{2,3},{3,2},{4,5},{5,4},{6,7},{7,6},{8,9},{9,8},{10,11... | collective-permute-start | bytes 1867784 | tf_op jit(solution)/shard_map/ppermute | solution.py:32
  36.2 2.2 %collective-permute-start.2 = (f32[2432]{0:T(1024)S(1)}, f32[2432]{0:T(1024)}, u32[]{:S(2)}, u32[]{:S(2)}) collective-permute-start(f32[2432]{0:T(1024)S(1)} %fusion.11), channel_id=1, source_target_pairs={{0,256},{256,0},{1,257},{257,1},{2,258},{258,2},{3,259},{259,3},{4... | collective-permute-start | bytes 29192 | tf_op jit(solution)/shard_map/ppermute | solution.py:32
  39.3 0.6 gather_fusion
  39.9 0.9 dynamic-slice_bitcast_fusion
  40.8 2.1 %collective-permute-start.3 = (bf16[128,1216]{1,0:T(8,128)(2,1)}, bf16[128,1216]{1,0:T(8,128)(2,1)}, u32[]{:S(2)}, u32[]{:S(2)}) collective-permute-start(bf16[128,1216]{1,0:T(8,128)(2,1)} %dynamic-slice_bitcast_fusion), channel_id=1, source_target_pairs={{0,256},{256,0},{1,257},{257,1},{2,258},{258,2},{3,259},{259,3},{4... | collective-permute-start | bytes 933896 | tf_op jit(solution)/shard_map/ppermute | solution.py:32
  43.2 0.8 copy-done.5
  44.0 1.1 copy-done.6
  45.0 2.3 %shard_map.149 = (bf16[4,256,608]{2,1,0:T(8,128)(2,1)S(1)}, bf16[256,128]{1,0:T(8,128)(2,1)S(1)}, bf16[608,256]{1,0:T(8,128)(2,1)S(1)}) custom-call(s32[5]{0:T(128)S(1)} %pad_add_fusion.slots, bf16[128,2432]{1,0:T(8,128)(2,1)} %bitcast.own, bf16[128,2432]{1,0:T(8,128)(2,1)S(1)} %copy-done.6, bf16[4,4,152,128]{3,2,1,0:T(8,128)(2,1)S(1)} %bitcast.40), custom_call_target="tpu_custom_call" | custom-call | flops 159383552 | bytes 3489812 | tf_op jit(solution)/shard_map/pallas_call | solution.py:124
  47.4 0.7 copy-done.7
  48.1 0.6 copy-done.9
  48.8 1.0 all-to-all-done.1.lined
  50.0 0.9 collective-permute-done.own
  50.9 4.4 %collective-permute-start.7 = (bf16[304,608]{1,0:T(8,128)(2,1)S(1)}, bf16[304,608]{1,0:T(8,128)(2,1)S(1)}, u32[]{:S(2)}, u32[]{:S(2)}) collective-permute-start(bf16[304,608]{1,0:T(8,128)(2,1)S(1)} %get-tuple-element.42.refs_0_), channel_id=1, source_target_pairs={{0,48},{2,50},{4,52},{6,54},{8,56},{10,58},{12,60},{14,62},{16,0},... | collective-permute-start | bytes 1109000 | tf_op jit(solution)/shard_map/ppermute | solution.py:82
  55.3 1.9 %collective-permute-start.5 = (bf16[304,608]{1,0:T(8,128)(2,1)S(1)}, bf16[304,608]{1,0:T(8,128)(2,1)S(1)}, u32[]{:S(2)}, u32[]{:S(2)}) collective-permute-start(bf16[304,608]{1,0:T(8,128)(2,1)S(1)} %get-tuple-element.42.refs_0_), channel_id=1, source_target_pairs={{0,16},{2,18},{4,20},{6,22},{8,24},{10,26},{12,28},{14,30},{16,32}... | collective-permute-start | bytes 1109000 | tf_op jit(solution)/shard_map/ppermute | solution.py:82
  57.3 4.6 %collective-permute-start.8 = (bf16[304,608]{1,0:T(8,128)(2,1)S(1)}, bf16[304,608]{1,0:T(8,128)(2,1)S(1)}, u32[]{:S(2)}, u32[]{:S(2)}) collective-permute-start(bf16[304,608]{1,0:T(8,128)(2,1)S(1)} %get-tuple-element.43.refs_1_), channel_id=1, source_target_pairs={{0,48},{2,50},{4,52},{6,54},{8,56},{10,58},{12,60},{14,62},{16,0},... | collective-permute-start | bytes 1109000 | tf_op jit(solution)/shard_map/ppermute | solution.py:82
  61.8 1.9 %collective-permute-start.6 = (bf16[304,608]{1,0:T(8,128)(2,1)S(1)}, bf16[304,608]{1,0:T(8,128)(2,1)S(1)}, u32[]{:S(2)}, u32[]{:S(2)}) collective-permute-start(bf16[304,608]{1,0:T(8,128)(2,1)S(1)} %get-tuple-element.43.refs_1_), channel_id=1, source_target_pairs={{0,16},{2,18},{4,20},{6,22},{8,24},{10,26},{12,28},{14,30},{16,32}... | collective-permute-start | bytes 1109000 | tf_op jit(solution)/shard_map/ppermute | solution.py:82
  63.8 5.1 %collective-permute-start.4 = (bf16[128,2432]{1,0:T(8,128)(2,1)}, bf16[128,2432]{1,0:T(8,128)(2,1)S(1)}, u32[]{:S(2)}, u32[]{:S(2)}) collective-permute-start(bf16[128,2432]{1,0:T(8,128)(2,1)} %collective-permute-done.own), channel_id=1, source_target_pairs={{0,256},{256,0},{1,257},{257,1},{2,258},{258,2},{3,259},{259,3},{4... | collective-permute-start | bytes 1867784 | tf_op jit(solution)/shard_map/ppermute | solution.py:32
  68.8 1.8 %fusion.2 = f32[128,1216]{1,0:T(8,128)S(1)} fusion(bf16[128,1216]{1,0:T(8,128)(2,1)} %collective-permute-done.3, f32[]{:T(128)S(6)} %select_n.89, bf16[1,128,2432]{2,1,0:T(8,128)(2,1)} %param.14, s32[]{:T(128)S(6)} %select_n.87, f32[]{:T(128)S(6)} %select_n.88, f32[]{:T(128)} %bitcast.7, bf16[128,2432]{1,0:T(8,128)(2,1)} %param.15, bf16[128,2432]{1,0:T(8,128)(2,1)} %param.16), kind=kLoop, calls=%fused_computation.9 | loop fusion | flops 1556480 | bytes 1867792 | tf_op jit(solution)/shard_map/add | solution.py:284
  70.8 1.9 %collective-permute-start.9 = (bf16[304,608]{1,0:T(8,128)(2,1)S(1)}, bf16[304,608]{1,0:T(8,128)(2,1)S(1)}, u32[]{:S(2)}, u32[]{:S(2)}) collective-permute-start(bf16[304,608]{1,0:T(8,128)(2,1)S(1)} %collective-permute-done.5.refs_2_), channel_id=1, source_target_pairs={{0,16},{2,18},{4,20},{6,22},{8,24},{10,26},{12,28},{14,30},{16,32}... | collective-permute-start | bytes 1109000 | tf_op jit(solution)/shard_map/ppermute | solution.py:82
  72.7 4.9 %collective-permute-start.10 = (bf16[304,608]{1,0:T(8,128)(2,1)S(1)}, bf16[304,608]{1,0:T(8,128)(2,1)S(1)}, u32[]{:S(2)}, u32[]{:S(2)}) collective-permute-start(bf16[304,608]{1,0:T(8,128)(2,1)S(1)} %collective-permute-done.8.refs_5_), channel_id=1, source_target_pairs={{0,48},{2,50},{4,52},{6,54},{8,56},{10,58},{12,60},{14,62},{16,0},... | collective-permute-start | bytes 1109000 | tf_op jit(solution)/shard_map/ppermute | solution.py:82
  77.8 3.0 %collective-permute-start.11 = (bf16[128,608]{1,0:T(8,128)(2,1)S(1)}, bf16[128,608]{1,0:T(8,128)(2,1)S(1)}, u32[]{:S(2)}, u32[]{:S(2)}) collective-permute-start(bf16[128,608]{1,0:T(8,128)(2,1)S(1)} %fusion.7), channel_id=1, source_target_pairs={{0,1},{1,0},{2,3},{3,2},{4,5},{5,4},{6,7},{7,6},{8,9},{9,8},{10,11... | collective-permute-start | bytes 466952 | tf_op jit(solution)/shard_map/ppermute | solution.py:32
  80.8 0.8 dynamic-slice_multiply_fusion
  81.6 2.3 %shard_map.150 = (bf16[4,256,608]{2,1,0:T(8,128)(2,1)S(1)}, bf16[256,128]{1,0:T(8,128)(2,1)S(1)}, bf16[608,256]{1,0:T(8,128)(2,1)S(1)}) custom-call(s32[5]{0:T(128)S(1)} %pad_add_fusion.slots, bf16[128,2432]{1,0:T(8,128)(2,1)} %collective-permute-done.own, bf16[128,2432]{1,0:T(8,128)(2,1)S(1)} %collective-permute-done.4.other, ...), custom_call_target="tpu_custom_call" | custom-call | flops 159383552 | bytes 3489812 | tf_op jit(solution)/shard_map/pallas_call | solution.py:124
  84.0 1.9 %shard_map.151.product = f32[512,608]{1,0:T(8,128)S(1)} custom-call(bf16[4,256,608]{2,1,0:T(8,128)(2,1)S(1)} %get-tuple-element.39.rows, bf16[4,256,608]{2,1,0:T(8,128)(2,1)S(1)} %get-tuple-element.41.far_rows, bf16[304,608]{1,0:T(8,128)(2,1)S(1)} %get-tuple-element.42.refs_0_, bf16[304,608]{1,0:T(8,128)(2,1)S(1)} %get-tuple-element.43.refs_1_, ...), custom_call_target="tpu_custom_call" | custom-call | flops 1135607808 | bytes 5953536 | tf_op jit(solution)/shard_map/pallas_call | solution.py:124
  86.0 1.4 %shard_map.152 = (bf16[512,608]{1,0:T(8,128)(2,1)S(1)}, f32[512,128]{1,0:T(8,128)S(1)}) custom-call(f32[512,608]{1,0:T(8,128)S(1)} %shard_map.151.product, bf16[4,256,608]{2,1,0:T(8,128)(2,1)S(1)} %get-tuple-element.39.rows, bf16[4,256,608]{2,1,0:T(8,128)(2,1)S(1)} %get-tuple-element.41.far_rows, bf16[304,608]{1,0:T(8,128)(2,1)S(1)} %collective-permute-done.9.upper.refs_6_, ...), custom_call_target="tpu_custom_call" | custom-call | flops 458227712 | bytes 6118144 | tf_op jit(solution)/shard_map/pallas_call | solution.py:124
  87.4 3.4 %collective-permute-start.12 = (bf16[512,128]{1,0:T(8,128)(2,1)S(1)}, bf16[512,128]{1,0:T(8,128)(2,1)S(1)}, u32[]{:S(2)}, u32[]{:S(2)}) collective-permute-start(bf16[512,128]{1,0:T(8,128)(2,1)S(1)} %convert_element_type.65), channel_id=1, source_target_pairs={{0,256},{256,0},{1,257},{257,1},{2,258},{258,2},{3,259},{259,3},{4... | collective-permute-start | bytes 393224 | tf_op jit(solution)/shard_map/ppermute | solution.py:32
  91.2 0.6 collective-permute-done.12
  91.9 2.7 %collective-permute-start.13 = (bf16[512,128]{1,0:T(8,128)(2,1)S(1)}, bf16[512,128]{1,0:T(8,128)(2,1)S(1)}, u32[]{:S(2)}, u32[]{:S(2)}) collective-permute-start(bf16[512,128]{1,0:T(8,128)(2,1)S(1)} %get-tuple-element.61), channel_id=1, source_target_pairs={{0,1},{1,0},{2,3},{3,2},{4,5},{5,4},{6,7},{7,6},{8,9},{9,8},{10,11... | collective-permute-start | bytes 393224 | tf_op jit(solution)/shard_map/ppermute | solution.py:32
  94.6 4.4 %shard_map.154 = (bf16[4,4,152,256]{3,2,1,0:T(8,128)(2,1)S(1)}, bf16[4,4,152,256]{3,2,1,0:T(8,128)(2,1)}) custom-call(s32[4]{0:T(128)S(1)} %pad_add_fusion.1.places, bf16[512,608]{1,0:T(8,128)(2,1)S(1)} %get-tuple-element.49.before, f32[512,128]{1,0:T(8,128)S(1)} %get-tuple-element.48.low, bf16[4,4,152,128]{3,2,1,0:T(8,128)(2,1)S(1)} %bitcast.42, ...), custom_call_target="tpu_custom_call" | custom-call | flops 1832910848 | bytes 6955024 | tf_op jit(solution)/shard_map/pallas_call | solution.py:124
  99.0 1.7 %shard_map.153 = bf16[32,40,128]{2,1,0:T(8,128)(2,1)} custom-call(f32[512,128]{1,0:T(8,128)S(1)} %get-tuple-element.62.pair, bf16[512,128]{1,0:T(8,128)(2,1)S(1)} %collective-permute-done.13.far, bf16[608,128]{1,0:T(8,128)(2,1)S(1)} %fusion.up, bf16[768,608]{1,0:T(8,128)(2,1)S(1)} %copy-done.4, bf16[608,256]{1,0:T(8,128)(2,1)S(1)} %copy-done.8, ...), custom_call_target="tpu_custom_call" | custom-call | flops 100663296 | bytes 2433024 | tf_op jit(solution)/shard_map/pallas_call | solution.py:124
  100.7 2.7 %collective-permute-start.14 = (bf16[4,4,152,256]{3,2,1,0:T(8,128)(2,1)}, bf16[4,4,152,256]{3,2,1,0:T(8,128)(2,1)S(1)}, u32[]{:S(2)}, u32[]{:S(2)}) collective-permute-start(bf16[4,4,152,256]{3,2,1,0:T(8,128)(2,1)} %get-tuple-element.55), channel_id=1, source_target_pairs={{0,256},{256,0},{1,257},{257,1},{2,258},{258,2},{3,259},{259,3},{4... | collective-permute-start | bytes 3735560 | tf_op jit(solution)/shard_map/ppermute | solution.py:32
  103.5 8.7 %all-to-all-start.2 = ((bf16[32,40,128]{2,1,0:T(8,128)(2,1)}), bf16[32,40,128]{2,1,0:T(8,128)(2,1)S(1)}, u32[]{:S(2)}, u32[]{:S(2)}) async-start(bf16[32,40,128]{2,1,0:T(8,128)(2,1)} %shard_map.153), calls=%async_computation.2 | async-start | bytes 655360 | tf_op jit(solution)/shard_map/all_to_all | solution.py:321
  112.2 1.0 copy-done.2
  113.3 1.3 copy-done.3
  114.6 1.0 shard_map.155
  115.6 2.7 %collective-permute-start.17 = (bf16[4,4,152,128]{3,2,1,0:T(8,128)(2,1)}, bf16[4,4,152,128]{3,2,1,0:T(8,128)(2,1)S(1)}, u32[]{:S(2)}, u32[]{:S(2)}) collective-permute-start(bf16[4,4,152,128]{3,2,1,0:T(8,128)(2,1)} %get-tuple-element.58), channel_id=1, source_target_pairs={{0,1},{1,0},{2,3},{3,2},{4,5},{5,4},{6,7},{7,6},{8,9},{9,8},{10,11... | collective-permute-start | bytes 1867784 | tf_op jit(solution)/shard_map/ppermute | solution.py:32
  118.3 5.2 %all-to-all-done.2 = bf16[32,40,128]{2,1,0:T(8,128)(2,1)S(1)} async-done(((bf16[32,40,128]{2,1,0:T(8,128)(2,1)}), bf16[32,40,128]{2,1,0:T(8,128)(2,1)S(1)}, u32[]{:S(2)}, u32[]{:S(2)}) %all-to-all-start.2) | async-done | bytes 327712 | tf_op jit(solution)/shard_map/all_to_all | solution.py:321
  123.6 4.3 %collective-permute-start.16 = (f32[40,128]{1,0:T(8,128)S(1)}, f32[40,128]{1,0:T(8,128)S(1)}, u32[]{:S(2)}, u32[]{:S(2)}) collective-permute-start(f32[40,128]{1,0:T(8,128)S(1)} %convert_reduce_fusion), channel_id=1, source_target_pairs={{0,1},{1,65},{256,129},{257,193},{2,3},{3,67},{258,131},{259,195},... | collective-permute-start | bytes 61448 | tf_op jit(solution)/shard_map/ppermute | solution.py:96
  127.9 4.8 %collective-permute-start.15 = (f32[40,128]{1,0:T(8,128)S(1)}, f32[40,128]{1,0:T(8,128)S(1)}, u32[]{:S(2)}, u32[]{:S(2)}) collective-permute-start(f32[40,128]{1,0:T(8,128)S(1)} %convert_reduce_fusion), channel_id=1, source_target_pairs={{0,0},{1,64},{256,128},{257,192},{2,2},{3,66},{258,130},{259,194},... | collective-permute-start | bytes 61448 | tf_op jit(solution)/shard_map/ppermute | solution.py:96
  133.2 3.7 %collective-permute-done.15 = f32[40,128]{1,0:T(8,128)S(1)} collective-permute-done((f32[40,128]{1,0:T(8,128)S(1)}, f32[40,128]{1,0:T(8,128)S(1)}, u32[]{:S(2)}, u32[]{:S(2)}) %collective-permute-start.15) | collective-permute-done | bytes 20512 | tf_op jit(solution)/shard_map/ppermute | solution.py:96
  136.9 1.9 %collective-permute-start.18 = (f32[40,128]{1,0:T(8,128)S(1)}, f32[40,128]{1,0:T(8,128)S(1)}, u32[]{:S(2)}, u32[]{:S(2)}) collective-permute-start(f32[40,128]{1,0:T(8,128)S(1)} %add.112), channel_id=1, source_target_pairs={{0,256},{256,0},{1,257},{257,1},{2,258},{258,2},{3,259},{259,3},{4... | collective-permute-start | bytes 61448 | tf_op jit(solution)/shard_map/ppermute | solution.py:32
  138.8 1.1 shard_map.156
  140.0 0.6 fusion.17
  (70 shorter events, 2.7 us)
Async XLA Ops:
  0.6 42.5 %copy-start = (bf16[2432,128]{1,0:T(8,128)(2,1)S(1)}, bf16[2432,128]{1,0:T(8,128)(2,1)}, u32[]{:S(2)}) copy-start(bf16[2432,128]{1,0:T(8,128)(2,1)} %param.20) | copy-start | bytes 1867780
  0.6 1.0 copy-start.13
  20.2 15.9 %copy-start.14 = (f32[1,8,2432]{2,1,0:T(8,128)S(1)}, f32[1,8,2432]{2,1,0:T(8,128)}, u32[]{:S(2)}) copy-start(f32[1,8,2432]{2,1,0:T(8,128)} %param.21) | copy-start | bytes 233476
  20.2 19.1 %copy-start.11 = (s32[4]{0:T(128)S(1)}, s32[4]{0:T(128)}, u32[]{:S(2)}) copy-start(s32[4]{0:T(128)} %constant.117.clone) | copy-start | bytes 52
  21.2 18.7 %copy-start.12 = (bf16[1,128,2432]{2,1,0:T(8,128)(2,1)S(1)}, bf16[1,128,2432]{2,1,0:T(8,128)(2,1)}, u32[]{:S(2)}) copy-start(bf16[1,128,2432]{2,1,0:T(8,128)(2,1)} %param.14) | copy-start | bytes 1867780
  21.2 28.5 %all-to-all-start.1 = ((bf16[8,76,608]{2,1,0:T(8,128)(2,1)}), bf16[8,76,608]{2,1,0:T(8,128)(2,1)S(1)}, u32[]{:S(2)}, u32[]{:S(2)}) async-start(bf16[8,76,608]{2,1,0:T(8,128)(2,1)} %broadcast_in_dim.22), calls=%async_computation.1 | async-start | bytes 1638400 | tf_op jit(solution)/shard_map/all_to_all | solution.py:73
  28.2 15.8 %copy-start.1 = (bf16[2432,128]{1,0:T(8,128)(2,1)S(1)}, bf16[2432,128]{1,0:T(8,128)(2,1)}, u32[]{:S(2)}) copy-start(bf16[2432,128]{1,0:T(8,128)(2,1)} %param.19) | copy-start | bytes 1867780
  28.2 15.0 %collective-permute-start.1 = (bf16[128,2432]{1,0:T(8,128)(2,1)}, bf16[128,2432]{1,0:T(8,128)(2,1)S(1)}, u32[]{:S(2)}, u32[]{:S(2)}) collective-permute-start(bf16[128,2432]{1,0:T(8,128)(2,1)} %bitcast.own), channel_id=1, source_target_pairs={{0,256},{256,0},{1,257},{257,1},{2,258},{258,2},{3,259},{259,3},{4... | collective-permute-start | bytes 1867784 | tf_op jit(solution)/shard_map/ppermute | solution.py:32
  33.1 17.9 %collective-permute-start = (bf16[128,2432]{1,0:T(8,128)(2,1)}, bf16[128,2432]{1,0:T(8,128)(2,1)}, u32[]{:S(2)}, u32[]{:S(2)}) collective-permute-start(bf16[128,2432]{1,0:T(8,128)(2,1)} %bitcast.own), channel_id=1, source_target_pairs={{0,1},{1,0},{2,3},{3,2},{4,5},{5,4},{6,7},{7,6},{8,9},{9,8},{10,11... | collective-permute-start | bytes 1867784 | tf_op jit(solution)/shard_map/ppermute | solution.py:32
  36.2 13.8 %collective-permute-start.2 = (f32[2432]{0:T(1024)S(1)}, f32[2432]{0:T(1024)}, u32[]{:S(2)}, u32[]{:S(2)}) collective-permute-start(f32[2432]{0:T(1024)S(1)} %fusion.11), channel_id=1, source_target_pairs={{0,256},{256,0},{1,257},{257,1},{2,258},{258,2},{3,259},{259,3},{4... | collective-permute-start | bytes 29192 | tf_op jit(solution)/shard_map/ppermute | solution.py:32
  40.8 9.2 %collective-permute-start.3 = (bf16[128,1216]{1,0:T(8,128)(2,1)}, bf16[128,1216]{1,0:T(8,128)(2,1)}, u32[]{:S(2)}, u32[]{:S(2)}) collective-permute-start(bf16[128,1216]{1,0:T(8,128)(2,1)} %dynamic-slice_bitcast_fusion), channel_id=1, source_target_pairs={{0,256},{256,0},{1,257},{257,1},{2,258},{258,2},{3,259},{259,3},{4... | collective-permute-start | bytes 933896 | tf_op jit(solution)/shard_map/ppermute | solution.py:32
  43.1 0.8 copy-start.5
  44.0 1.1 copy-start.6
  47.4 0.7 copy-start.7
  48.1 0.6 copy-start.9
  50.9 33.0 %collective-permute-start.7 = (bf16[304,608]{1,0:T(8,128)(2,1)S(1)}, bf16[304,608]{1,0:T(8,128)(2,1)S(1)}, u32[]{:S(2)}, u32[]{:S(2)}) collective-permute-start(bf16[304,608]{1,0:T(8,128)(2,1)S(1)} %get-tuple-element.42.refs_0_), channel_id=1, source_target_pairs={{0,48},{2,50},{4,52},{6,54},{8,56},{10,58},{12,60},{14,62},{16,0},... | collective-permute-start | bytes 1109000 | tf_op jit(solution)/shard_map/ppermute | solution.py:82
  55.3 15.5 %collective-permute-start.5 = (bf16[304,608]{1,0:T(8,128)(2,1)S(1)}, bf16[304,608]{1,0:T(8,128)(2,1)S(1)}, u32[]{:S(2)}, u32[]{:S(2)}) collective-permute-start(bf16[304,608]{1,0:T(8,128)(2,1)S(1)} %get-tuple-element.42.refs_0_), channel_id=1, source_target_pairs={{0,16},{2,18},{4,20},{6,22},{8,24},{10,26},{12,28},{14,30},{16,32}... | collective-permute-start | bytes 1109000 | tf_op jit(solution)/shard_map/ppermute | solution.py:82
  57.3 15.5 %collective-permute-start.8 = (bf16[304,608]{1,0:T(8,128)(2,1)S(1)}, bf16[304,608]{1,0:T(8,128)(2,1)S(1)}, u32[]{:S(2)}, u32[]{:S(2)}) collective-permute-start(bf16[304,608]{1,0:T(8,128)(2,1)S(1)} %get-tuple-element.43.refs_1_), channel_id=1, source_target_pairs={{0,48},{2,50},{4,52},{6,54},{8,56},{10,58},{12,60},{14,62},{16,0},... | collective-permute-start | bytes 1109000 | tf_op jit(solution)/shard_map/ppermute | solution.py:82
  61.8 22.1 %collective-permute-start.6 = (bf16[304,608]{1,0:T(8,128)(2,1)S(1)}, bf16[304,608]{1,0:T(8,128)(2,1)S(1)}, u32[]{:S(2)}, u32[]{:S(2)}) collective-permute-start(bf16[304,608]{1,0:T(8,128)(2,1)S(1)} %get-tuple-element.43.refs_1_), channel_id=1, source_target_pairs={{0,16},{2,18},{4,20},{6,22},{8,24},{10,26},{12,28},{14,30},{16,32}... | collective-permute-start | bytes 1109000 | tf_op jit(solution)/shard_map/ppermute | solution.py:82
  63.8 14.0 %collective-permute-start.4 = (bf16[128,2432]{1,0:T(8,128)(2,1)}, bf16[128,2432]{1,0:T(8,128)(2,1)S(1)}, u32[]{:S(2)}, u32[]{:S(2)}) collective-permute-start(bf16[128,2432]{1,0:T(8,128)(2,1)} %collective-permute-done.own), channel_id=1, source_target_pairs={{0,256},{256,0},{1,257},{257,1},{2,258},{258,2},{3,259},{259,3},{4... | collective-permute-start | bytes 1867784 | tf_op jit(solution)/shard_map/ppermute | solution.py:32
  70.8 15.1 %collective-permute-start.9 = (bf16[304,608]{1,0:T(8,128)(2,1)S(1)}, bf16[304,608]{1,0:T(8,128)(2,1)S(1)}, u32[]{:S(2)}, u32[]{:S(2)}) collective-permute-start(bf16[304,608]{1,0:T(8,128)(2,1)S(1)} %collective-permute-done.5.refs_2_), channel_id=1, source_target_pairs={{0,16},{2,18},{4,20},{6,22},{8,24},{10,26},{12,28},{14,30},{16,32}... | collective-permute-start | bytes 1109000 | tf_op jit(solution)/shard_map/ppermute | solution.py:82
  72.7 13.2 %collective-permute-start.10 = (bf16[304,608]{1,0:T(8,128)(2,1)S(1)}, bf16[304,608]{1,0:T(8,128)(2,1)S(1)}, u32[]{:S(2)}, u32[]{:S(2)}) collective-permute-start(bf16[304,608]{1,0:T(8,128)(2,1)S(1)} %collective-permute-done.8.refs_5_), channel_id=1, source_target_pairs={{0,48},{2,50},{4,52},{6,54},{8,56},{10,58},{12,60},{14,62},{16,0},... | collective-permute-start | bytes 1109000 | tf_op jit(solution)/shard_map/ppermute | solution.py:82
  77.8 8.2 %collective-permute-start.11 = (bf16[128,608]{1,0:T(8,128)(2,1)S(1)}, bf16[128,608]{1,0:T(8,128)(2,1)S(1)}, u32[]{:S(2)}, u32[]{:S(2)}) collective-permute-start(bf16[128,608]{1,0:T(8,128)(2,1)S(1)} %fusion.7), channel_id=1, source_target_pairs={{0,1},{1,0},{2,3},{3,2},{4,5},{5,4},{6,7},{7,6},{8,9},{9,8},{10,11... | collective-permute-start | bytes 466952 | tf_op jit(solution)/shard_map/ppermute | solution.py:32
  84.0 2.0 %copy-start.10 = (bf16[256,128]{1,0:T(8,128)(2,1)S(1)}, bf16[256,128]{1,0:T(8,128)(2,1)}, u32[]{:S(2)}) copy-start(bf16[256,128]{1,0:T(8,128)(2,1)} %copy-done.9) | copy-start | bytes 196612
  87.4 4.3 %collective-permute-start.12 = (bf16[512,128]{1,0:T(8,128)(2,1)S(1)}, bf16[512,128]{1,0:T(8,128)(2,1)S(1)}, u32[]{:S(2)}, u32[]{:S(2)}) collective-permute-start(bf16[512,128]{1,0:T(8,128)(2,1)S(1)} %convert_element_type.65), channel_id=1, source_target_pairs={{0,256},{256,0},{1,257},{257,1},{2,258},{258,2},{3,259},{259,3},{4... | collective-permute-start | bytes 393224 | tf_op jit(solution)/shard_map/ppermute | solution.py:32
  91.9 7.2 %copy-start.4 = (bf16[768,608]{1,0:T(8,128)(2,1)S(1)}, bf16[768,608]{1,0:T(8,128)(2,1)}, u32[]{:S(2)}) copy-start(bf16[768,608]{1,0:T(8,128)(2,1)} %constant.118.clone.spread) | copy-start | bytes 2801668
  91.9 7.1 %copy-start.8 = (bf16[608,256]{1,0:T(8,128)(2,1)S(1)}, bf16[608,256]{1,0:T(8,128)(2,1)}, u32[]{:S(2)}) copy-start(bf16[608,256]{1,0:T(8,128)(2,1)} %copy-done.7) | copy-start | bytes 933892
  91.9 7.1 %collective-permute-start.13 = (bf16[512,128]{1,0:T(8,128)(2,1)S(1)}, bf16[512,128]{1,0:T(8,128)(2,1)S(1)}, u32[]{:S(2)}, u32[]{:S(2)}) collective-permute-start(bf16[512,128]{1,0:T(8,128)(2,1)S(1)} %get-tuple-element.61), channel_id=1, source_target_pairs={{0,1},{1,0},{2,3},{3,2},{4,5},{5,4},{6,7},{7,6},{8,9},{9,8},{10,11... | collective-permute-start | bytes 393224 | tf_op jit(solution)/shard_map/ppermute | solution.py:32
  100.7 11.5 %collective-permute-start.14 = (bf16[4,4,152,256]{3,2,1,0:T(8,128)(2,1)}, bf16[4,4,152,256]{3,2,1,0:T(8,128)(2,1)S(1)}, u32[]{:S(2)}, u32[]{:S(2)}) collective-permute-start(bf16[4,4,152,256]{3,2,1,0:T(8,128)(2,1)} %get-tuple-element.55), channel_id=1, source_target_pairs={{0,256},{256,0},{1,257},{257,1},{2,258},{258,2},{3,259},{259,3},{4... | collective-permute-start | bytes 3735560 | tf_op jit(solution)/shard_map/ppermute | solution.py:32
  103.5 20.1 %all-to-all-start.2 = ((bf16[32,40,128]{2,1,0:T(8,128)(2,1)}), bf16[32,40,128]{2,1,0:T(8,128)(2,1)S(1)}, u32[]{:S(2)}, u32[]{:S(2)}) async-start(bf16[32,40,128]{2,1,0:T(8,128)(2,1)} %shard_map.153), calls=%async_computation.2 | async-start | bytes 655360 | tf_op jit(solution)/shard_map/all_to_all | solution.py:321
  112.2 1.1 copy-start.2
  113.3 1.3 copy-start.3
  115.6 21.3 %collective-permute-start.17 = (bf16[4,4,152,128]{3,2,1,0:T(8,128)(2,1)}, bf16[4,4,152,128]{3,2,1,0:T(8,128)(2,1)S(1)}, u32[]{:S(2)}, u32[]{:S(2)}) collective-permute-start(bf16[4,4,152,128]{3,2,1,0:T(8,128)(2,1)} %get-tuple-element.58), channel_id=1, source_target_pairs={{0,1},{1,0},{2,3},{3,2},{4,5},{5,4},{6,7},{7,6},{8,9},{9,8},{10,11... | collective-permute-start | bytes 1867784 | tf_op jit(solution)/shard_map/ppermute | solution.py:32
  123.6 9.7 %collective-permute-start.16 = (f32[40,128]{1,0:T(8,128)S(1)}, f32[40,128]{1,0:T(8,128)S(1)}, u32[]{:S(2)}, u32[]{:S(2)}) collective-permute-start(f32[40,128]{1,0:T(8,128)S(1)} %convert_reduce_fusion), channel_id=1, source_target_pairs={{0,1},{1,65},{256,129},{257,193},{2,3},{3,67},{258,131},{259,195},... | collective-permute-start | bytes 61448 | tf_op jit(solution)/shard_map/ppermute | solution.py:96
  127.9 9.0 %collective-permute-start.15 = (f32[40,128]{1,0:T(8,128)S(1)}, f32[40,128]{1,0:T(8,128)S(1)}, u32[]{:S(2)}, u32[]{:S(2)}) collective-permute-start(f32[40,128]{1,0:T(8,128)S(1)} %convert_reduce_fusion), channel_id=1, source_target_pairs={{0,0},{1,64},{256,128},{257,192},{2,2},{3,66},{258,130},{259,194},... | collective-permute-start | bytes 61448 | tf_op jit(solution)/shard_map/ppermute | solution.py:96
  136.9 3.1 %collective-permute-start.18 = (f32[40,128]{1,0:T(8,128)S(1)}, f32[40,128]{1,0:T(8,128)S(1)}, u32[]{:S(2)}, u32[]{:S(2)}) collective-permute-start(f32[40,128]{1,0:T(8,128)S(1)} %add.112), channel_id=1, source_target_pairs={{0,256},{256,0},{1,257},{257,1},{2,258},{258,2},{3,259},{259,3},{4... | collective-permute-start | bytes 61448 | tf_op jit(solution)/shard_map/ppermute | solution.py:32

commit v6 on v5

--- a/solution.py
+++ b/solution.py
@@ -115,8 +115,8 @@
     return ref[:, x].astype(F32).reshape(SLICE, ref.shape[-1]).astype(BF16)
 
 
-def call(kernel, outs, flops, *args, places=None, scratch=()):
-    specs = [pl.BlockSpec(memory_space=pltpu.VMEM)] * len(args)
+def call(kernel, outs, flops, *args, places=None, scratch=(), space=pltpu.VMEM):
+    specs = [pl.BlockSpec(memory_space=space)] * len(args)
     if places is not None:
         args, specs = (places,) + args, [pl.BlockSpec(memory_space=pltpu.SMEM)] + specs
     moved = sum(a.size * a.dtype.itemsize for a in args)
@@ -197,14 +197,31 @@
             out[:, places[c]] = both.reshape(ZH, YN * ROWS, 2 * TOK).astype(BF16)
 
 
-def join_kernel(keep, got, home, cross):
-    both = keep[...].astype(F32) + got[...].astype(F32)
-    home[...] = both[..., :TOK]
-    cross[...] = both[..., TOK:].astype(BF16)
+def join_kernel(keep, got, home, cross, kept, gotten, arrived):
+    copies = [
+        pltpu.make_async_copy(source, target, arrived.at[i])
+        for i, (source, target) in enumerate(((keep, kept), (got, gotten)))
+    ]
+    for copy in copies:
+        copy.start()
+    for copy in copies:
+        copy.wait()
+    both = kept[...].astype(F32) + gotten[...].astype(F32)
+    home[...] = both[:, :TOK]
+    cross[...] = both[:, TOK:].astype(BF16)
+
+
+def join(keep, got):
+    shape, wide = (MODEL_WIDTH, TOK), (MODEL_WIDTH, 2 * TOK)
+    return call(
+        join_kernel, [(shape, F32), (shape, BF16)], 2 * 2432 * 256, keep.reshape(wide), got.reshape(wide),
+        scratch=[pltpu.VMEM(wide, BF16), pltpu.VMEM(wide, BF16), pltpu.SemaphoreType.DMA((2,))],
+        space=pl.ANY,
+    )
 
 
 def finish_kernel(home, across, grad):
-    grad[...] = (home[...].reshape(MODEL_WIDTH, TOK) + across[...].astype(F32).reshape(MODEL_WIDTH, TOK)).T.astype(BF16)
+    grad[...] = (home[...] + across[...].astype(F32)).T.astype(BF16)
 
 
 def terms_kernel(pair, far, up, spread, columns, far_columns, terms):
@@ -322,8 +339,7 @@
     plane_sum = jnp.sum(spread.astype(F32), axis=0)
     total = z_transposed(plane_sum, 0) + z_transposed(plane_sum, 1)
 
-    shape = (ZH, XN, YN * ROWS, TOK)
-    home, cross = call(join_kernel, [(shape, F32), (shape, BF16)], 2 * 2432 * 256, keep, swap(send, "branch"))
+    home, cross = join(keep, swap(send, "branch"))
     across = swap(cross, "seq")
     total, across = lax.optimization_barrier((total, across))
     total = total + swap(total, "branch")

time: 142 us -> 142 us (level)
  transfers between devices with their start and end apart: 21 -> 21, of which waited for: 7 -> 7; matrix products, arithmetic and copies ran while one was open for 4% -> 4% of each run, Pallas kernels for 9% -> 10%
where the time goes in v6:
time: 142 us; the launch traced here: 141 us
  starting transfers between devices  77.4 us (55%)
  blocking collectives  18.1 us (13%)
  Pallas kernels  17.2 us (12%)
  waiting for transfers between devices  11.6 us (8%)
  local copies, waits for them, and re-layouts  9.43 us (7%)
  other arithmetic  4.01 us (3%)
  between operations  2.65 us (2%)
    ppermute x11, starting transfers between devices, swap(): return lax.ppermute(value, axis, [(0, 1), (1, 0)])  33.1 us
    ppermute x6, starting transfers between devices, along_x(): return lax.ppermute(value, 'dp', pairs)  19.6 us
    all_to_all x1, blocking collectives, to_all(): return lax.all_to_all(copies, 'dp', 0, 0, axis_index_groups=groups)  18.1 us
    pallas_call x9, Pallas kernels, call(): pl.pallas_call(kernel, out_shape=[jax.ShapeDtypeStruct(shape, kind) for s...  17.2 us
    ppermute x2, starting transfers between devices, z_transposed(): return lax.ppermute(value, EVERY, pairs)  9.07 us
    all_to_all x1, starting transfers between devices, per_device(): spread = lax.all_to_all(terms, 'dp', 0, 0, axis_index_groups=XY_GROUPS)  8.75 us
    all_to_all x1, starting transfers between devices, to_all(): return lax.all_to_all(copies, 'dp', 0, 0, axis_index_groups=groups)  6.95 us
    unnamed x33, local copies, waits for them, and re-layouts  5.71 us
  transfers between devices with their start and end apart: 21, of which 7 were waited for; matrix products, arithmetic and copies ran while one was open for 4% of the time, Pallas kernels for 10%

profile of v6, /device:TPU:1, one launch (start us, length us, event | category | flops | bytes accessed | tf_op | source)
XLA Modules:
  0.0 140.8 jit_solution(9931505312837944923)
XLA Ops:
  0.7 0.8 multiply_exponential_fusion
  2.0 18.1 %all_to_all.15 = bf16[4,19,608]{2,1,0:T(8,128)(2,1)S(1)} all-to-all(bf16[4,19,608]{2,1,0:T(8,128)(2,1)S(1)} %broadcast_in_dim.21), channel_id=1, replica_groups={{0,64,128,192},{2,66,130,194},{4,68,132,196},{6,70,134,198},{8,72,136,2..., dimensions={0} | all-to-all | bytes 184832 | tf_op jit(solution)/shard_map/all_to_all | solution.py:73
  20.2 1.0 broadcast_in_dim.22
  21.2 7.0 %all-to-all-start.1 = ((bf16[8,76,608]{2,1,0:T(8,128)(2,1)}), bf16[8,76,608]{2,1,0:T(8,128)(2,1)S(1)}, u32[]{:S(2)}, u32[]{:S(2)}) async-start(bf16[8,76,608]{2,1,0:T(8,128)(2,1)} %broadcast_in_dim.22), calls=%async_computation.1 | async-start | bytes 1638400 | tf_op jit(solution)/shard_map/all_to_all | solution.py:73
  28.2 4.9 %collective-permute-start.1 = (bf16[128,2432]{1,0:T(8,128)(2,1)}, bf16[128,2432]{1,0:T(8,128)(2,1)S(1)}, u32[]{:S(2)}, u32[]{:S(2)}) collective-permute-start(bf16[128,2432]{1,0:T(8,128)(2,1)} %bitcast.own), channel_id=1, source_target_pairs={{0,256},{256,0},{1,257},{257,1},{2,258},{258,2},{3,259},{259,3},{4... | collective-permute-start | bytes 1867784 | tf_op jit(solution)/shard_map/ppermute | solution.py:32
  33.1 2.3 %collective-permute-start = (bf16[128,2432]{1,0:T(8,128)(2,1)}, bf16[128,2432]{1,0:T(8,128)(2,1)}, u32[]{:S(2)}, u32[]{:S(2)}) collective-permute-start(bf16[128,2432]{1,0:T(8,128)(2,1)} %bitcast.own), channel_id=1, source_target_pairs={{0,1},{1,0},{2,3},{3,2},{4,5},{5,4},{6,7},{7,6},{8,9},{9,8},{10,11... | collective-permute-start | bytes 1867784 | tf_op jit(solution)/shard_map/ppermute | solution.py:32
  36.2 2.2 %collective-permute-start.2 = (f32[2432]{0:T(1024)S(1)}, f32[2432]{0:T(1024)}, u32[]{:S(2)}, u32[]{:S(2)}) collective-permute-start(f32[2432]{0:T(1024)S(1)} %fusion.11), channel_id=1, source_target_pairs={{0,256},{256,0},{1,257},{257,1},{2,258},{258,2},{3,259},{259,3},{4... | collective-permute-start | bytes 29192 | tf_op jit(solution)/shard_map/ppermute | solution.py:32
  39.3 0.6 gather_fusion
  39.9 0.9 dynamic-slice_bitcast_fusion
  40.8 2.1 %collective-permute-start.3 = (bf16[128,1216]{1,0:T(8,128)(2,1)}, bf16[128,1216]{1,0:T(8,128)(2,1)}, u32[]{:S(2)}, u32[]{:S(2)}) collective-permute-start(bf16[128,1216]{1,0:T(8,128)(2,1)} %dynamic-slice_bitcast_fusion), channel_id=1, source_target_pairs={{0,256},{256,0},{1,257},{257,1},{2,258},{258,2},{3,259},{259,3},{4... | collective-permute-start | bytes 933896 | tf_op jit(solution)/shard_map/ppermute | solution.py:32
  43.2 0.8 copy-done.5
  44.0 1.1 copy-done.6
  45.0 2.3 %shard_map.149 = (bf16[4,256,608]{2,1,0:T(8,128)(2,1)S(1)}, bf16[256,128]{1,0:T(8,128)(2,1)S(1)}, bf16[608,256]{1,0:T(8,128)(2,1)S(1)}) custom-call(s32[5]{0:T(128)S(1)} %pad_add_fusion.slots, bf16[128,2432]{1,0:T(8,128)(2,1)} %bitcast.own, bf16[128,2432]{1,0:T(8,128)(2,1)S(1)} %copy-done.6, bf16[4,4,152,128]{3,2,1,0:T(8,128)(2,1)S(1)} %bitcast.42), custom_call_target="tpu_custom_call" | custom-call | flops 159383552 | bytes 3489812 | tf_op jit(solution)/shard_map/pallas_call | solution.py:124
  47.4 0.7 copy-done.7
  48.1 0.6 copy-done.9
  48.8 1.0 all-to-all-done.1.lined
  50.0 0.9 collective-permute-done.own
  50.9 4.4 %collective-permute-start.7 = (bf16[304,608]{1,0:T(8,128)(2,1)S(1)}, bf16[304,608]{1,0:T(8,128)(2,1)S(1)}, u32[]{:S(2)}, u32[]{:S(2)}) collective-permute-start(bf16[304,608]{1,0:T(8,128)(2,1)S(1)} %get-tuple-element.42.refs_0_), channel_id=1, source_target_pairs={{0,48},{2,50},{4,52},{6,54},{8,56},{10,58},{12,60},{14,62},{16,0},... | collective-permute-start | bytes 1109000 | tf_op jit(solution)/shard_map/ppermute | solution.py:82
  55.3 1.9 %collective-permute-start.5 = (bf16[304,608]{1,0:T(8,128)(2,1)S(1)}, bf16[304,608]{1,0:T(8,128)(2,1)S(1)}, u32[]{:S(2)}, u32[]{:S(2)}) collective-permute-start(bf16[304,608]{1,0:T(8,128)(2,1)S(1)} %get-tuple-element.42.refs_0_), channel_id=1, source_target_pairs={{0,16},{2,18},{4,20},{6,22},{8,24},{10,26},{12,28},{14,30},{16,32}... | collective-permute-start | bytes 1109000 | tf_op jit(solution)/shard_map/ppermute | solution.py:82
  57.3 4.6 %collective-permute-start.8 = (bf16[304,608]{1,0:T(8,128)(2,1)S(1)}, bf16[304,608]{1,0:T(8,128)(2,1)S(1)}, u32[]{:S(2)}, u32[]{:S(2)}) collective-permute-start(bf16[304,608]{1,0:T(8,128)(2,1)S(1)} %get-tuple-element.43.refs_1_), channel_id=1, source_target_pairs={{0,48},{2,50},{4,52},{6,54},{8,56},{10,58},{12,60},{14,62},{16,0},... | collective-permute-start | bytes 1109000 | tf_op jit(solution)/shard_map/ppermute | solution.py:82
  61.8 1.9 %collective-permute-start.6 = (bf16[304,608]{1,0:T(8,128)(2,1)S(1)}, bf16[304,608]{1,0:T(8,128)(2,1)S(1)}, u32[]{:S(2)}, u32[]{:S(2)}) collective-permute-start(bf16[304,608]{1,0:T(8,128)(2,1)S(1)} %get-tuple-element.43.refs_1_), channel_id=1, source_target_pairs={{0,16},{2,18},{4,20},{6,22},{8,24},{10,26},{12,28},{14,30},{16,32}... | collective-permute-start | bytes 1109000 | tf_op jit(solution)/shard_map/ppermute | solution.py:82
  63.8 5.1 %collective-permute-start.4 = (bf16[128,2432]{1,0:T(8,128)(2,1)}, bf16[128,2432]{1,0:T(8,128)(2,1)S(1)}, u32[]{:S(2)}, u32[]{:S(2)}) collective-permute-start(bf16[128,2432]{1,0:T(8,128)(2,1)} %collective-permute-done.own), channel_id=1, source_target_pairs={{0,256},{256,0},{1,257},{257,1},{2,258},{258,2},{3,259},{259,3},{4... | collective-permute-start | bytes 1867784 | tf_op jit(solution)/shard_map/ppermute | solution.py:32
  68.8 1.8 %fusion.2 = f32[128,1216]{1,0:T(8,128)S(1)} fusion(bf16[128,1216]{1,0:T(8,128)(2,1)} %collective-permute-done.3, f32[]{:T(128)S(6)} %select_n.89, bf16[1,128,2432]{2,1,0:T(8,128)(2,1)} %param.14, s32[]{:T(128)S(6)} %select_n.87, f32[]{:T(128)S(6)} %select_n.88, f32[]{:T(128)} %bitcast.7, bf16[128,2432]{1,0:T(8,128)(2,1)} %param.15, bf16[128,2432]{1,0:T(8,128)(2,1)} %param.16), kind=kLoop, calls=%fused_computation.9 | loop fusion | flops 1556480 | bytes 1867792 | tf_op jit(solution)/shard_map/add | solution.py:301
  70.8 1.9 %collective-permute-start.9 = (bf16[304,608]{1,0:T(8,128)(2,1)S(1)}, bf16[304,608]{1,0:T(8,128)(2,1)S(1)}, u32[]{:S(2)}, u32[]{:S(2)}) collective-permute-start(bf16[304,608]{1,0:T(8,128)(2,1)S(1)} %collective-permute-done.5.refs_2_), channel_id=1, source_target_pairs={{0,16},{2,18},{4,20},{6,22},{8,24},{10,26},{12,28},{14,30},{16,32}... | collective-permute-start | bytes 1109000 | tf_op jit(solution)/shard_map/ppermute | solution.py:82
  72.7 4.9 %collective-permute-start.10 = (bf16[304,608]{1,0:T(8,128)(2,1)S(1)}, bf16[304,608]{1,0:T(8,128)(2,1)S(1)}, u32[]{:S(2)}, u32[]{:S(2)}) collective-permute-start(bf16[304,608]{1,0:T(8,128)(2,1)S(1)} %collective-permute-done.8.refs_5_), channel_id=1, source_target_pairs={{0,48},{2,50},{4,52},{6,54},{8,56},{10,58},{12,60},{14,62},{16,0},... | collective-permute-start | bytes 1109000 | tf_op jit(solution)/shard_map/ppermute | solution.py:82
  77.8 3.0 %collective-permute-start.11 = (bf16[128,608]{1,0:T(8,128)(2,1)S(1)}, bf16[128,608]{1,0:T(8,128)(2,1)S(1)}, u32[]{:S(2)}, u32[]{:S(2)}) collective-permute-start(bf16[128,608]{1,0:T(8,128)(2,1)S(1)} %fusion.7), channel_id=1, source_target_pairs={{0,1},{1,0},{2,3},{3,2},{4,5},{5,4},{6,7},{7,6},{8,9},{9,8},{10,11... | collective-permute-start | bytes 466952 | tf_op jit(solution)/shard_map/ppermute | solution.py:32
  80.8 0.8 dynamic-slice_multiply_fusion
  81.6 2.3 %shard_map.150 = (bf16[4,256,608]{2,1,0:T(8,128)(2,1)S(1)}, bf16[256,128]{1,0:T(8,128)(2,1)S(1)}, bf16[608,256]{1,0:T(8,128)(2,1)S(1)}) custom-call(s32[5]{0:T(128)S(1)} %pad_add_fusion.slots, bf16[128,2432]{1,0:T(8,128)(2,1)} %collective-permute-done.own, bf16[128,2432]{1,0:T(8,128)(2,1)S(1)} %collective-permute-done.4.other, ...), custom_call_target="tpu_custom_call" | custom-call | flops 159383552 | bytes 3489812 | tf_op jit(solution)/shard_map/pallas_call | solution.py:124
  84.0 1.9 %shard_map.151.product = f32[512,608]{1,0:T(8,128)S(1)} custom-call(bf16[4,256,608]{2,1,0:T(8,128)(2,1)S(1)} %get-tuple-element.39.rows, bf16[4,256,608]{2,1,0:T(8,128)(2,1)S(1)} %get-tuple-element.41.far_rows, bf16[304,608]{1,0:T(8,128)(2,1)S(1)} %get-tuple-element.42.refs_0_, bf16[304,608]{1,0:T(8,128)(2,1)S(1)} %get-tuple-element.43.refs_1_, ...), custom_call_target="tpu_custom_call" | custom-call | flops 1135607808 | bytes 5953536 | tf_op jit(solution)/shard_map/pallas_call | solution.py:124
  86.0 1.4 %shard_map.152 = (bf16[512,608]{1,0:T(8,128)(2,1)S(1)}, f32[512,128]{1,0:T(8,128)S(1)}) custom-call(f32[512,608]{1,0:T(8,128)S(1)} %shard_map.151.product, bf16[4,256,608]{2,1,0:T(8,128)(2,1)S(1)} %get-tuple-element.39.rows, bf16[4,256,608]{2,1,0:T(8,128)(2,1)S(1)} %get-tuple-element.41.far_rows, bf16[304,608]{1,0:T(8,128)(2,1)S(1)} %collective-permute-done.9.upper.refs_6_, ...), custom_call_target="tpu_custom_call" | custom-call | flops 458227712 | bytes 6118144 | tf_op jit(solution)/shard_map/pallas_call | solution.py:124
  87.4 3.4 %collective-permute-start.12 = (bf16[512,128]{1,0:T(8,128)(2,1)S(1)}, bf16[512,128]{1,0:T(8,128)(2,1)S(1)}, u32[]{:S(2)}, u32[]{:S(2)}) collective-permute-start(bf16[512,128]{1,0:T(8,128)(2,1)S(1)} %convert_element_type.65), channel_id=1, source_target_pairs={{0,256},{256,0},{1,257},{257,1},{2,258},{258,2},{3,259},{259,3},{4... | collective-permute-start | bytes 393224 | tf_op jit(solution)/shard_map/ppermute | solution.py:32
  91.9 2.7 %collective-permute-start.13 = (bf16[512,128]{1,0:T(8,128)(2,1)S(1)}, bf16[512,128]{1,0:T(8,128)(2,1)S(1)}, u32[]{:S(2)}, u32[]{:S(2)}) collective-permute-start(bf16[512,128]{1,0:T(8,128)(2,1)S(1)} %get-tuple-element.61), channel_id=1, source_target_pairs={{0,1},{1,0},{2,3},{3,2},{4,5},{5,4},{6,7},{7,6},{8,9},{9,8},{10,11... | collective-permute-start | bytes 393224 | tf_op jit(solution)/shard_map/ppermute | solution.py:32
  94.6 4.4 %shard_map.154 = (bf16[4,4,152,256]{3,2,1,0:T(8,128)(2,1)S(1)}, bf16[4,4,152,256]{3,2,1,0:T(8,128)(2,1)}) custom-call(s32[4]{0:T(128)S(1)} %pad_add_fusion.1.places, bf16[512,608]{1,0:T(8,128)(2,1)S(1)} %get-tuple-element.49.before, f32[512,128]{1,0:T(8,128)S(1)} %get-tuple-element.48.low, bf16[4,4,152,128]{3,2,1,0:T(8,128)(2,1)S(1)} %bitcast.44, ...), custom_call_target="tpu_custom_call" | custom-call | flops 1832910848 | bytes 6955024 | tf_op jit(solution)/shard_map/pallas_call | solution.py:124
  99.0 1.7 %shard_map.153 = bf16[32,40,128]{2,1,0:T(8,128)(2,1)} custom-call(f32[512,128]{1,0:T(8,128)S(1)} %get-tuple-element.62.pair, bf16[512,128]{1,0:T(8,128)(2,1)S(1)} %collective-permute-done.13.far, bf16[608,128]{1,0:T(8,128)(2,1)S(1)} %fusion.up, bf16[768,608]{1,0:T(8,128)(2,1)S(1)} %copy-done.4, bf16[608,256]{1,0:T(8,128)(2,1)S(1)} %copy-done.8, ...), custom_call_target="tpu_custom_call" | custom-call | flops 100663296 | bytes 2433024 | tf_op jit(solution)/shard_map/pallas_call | solution.py:124
  100.7 2.7 %collective-permute-start.14 = (bf16[4,4,152,256]{3,2,1,0:T(8,128)(2,1)}, bf16[4,4,152,256]{3,2,1,0:T(8,128)(2,1)S(1)}, u32[]{:S(2)}, u32[]{:S(2)}) collective-permute-start(bf16[4,4,152,256]{3,2,1,0:T(8,128)(2,1)} %get-tuple-element.55), channel_id=1, source_target_pairs={{0,256},{256,0},{1,257},{257,1},{2,258},{258,2},{3,259},{259,3},{4... | collective-permute-start | bytes 3735560 | tf_op jit(solution)/shard_map/ppermute | solution.py:32
  103.5 8.7 %all-to-all-start.2 = ((bf16[32,40,128]{2,1,0:T(8,128)(2,1)}), bf16[32,40,128]{2,1,0:T(8,128)(2,1)S(1)}, u32[]{:S(2)}, u32[]{:S(2)}) async-start(bf16[32,40,128]{2,1,0:T(8,128)(2,1)} %shard_map.153), calls=%async_computation.2 | async-start | bytes 655360 | tf_op jit(solution)/shard_map/all_to_all | solution.py:338
  112.2 1.0 copy-done.2
  113.3 1.3 copy-done.3
  114.6 1.7 %shard_map.155 = (f32[2432,128]{1,0:T(8,128)S(1)}, bf16[2432,128]{1,0:T(8,128)(2,1)}) custom-call(bf16[2432,256]{1,0:T(8,128)(2,1)S(1)} %bitcast.45, bf16[2432,256]{1,0:T(8,128)(2,1)S(1)} %bitcast.46), custom_call_target="tpu_custom_call" | custom-call | flops 1245184 | bytes 4358144 | tf_op jit(solution)/shard_map/pallas_call | solution.py:124
  116.3 2.7 %collective-permute-start.17 = (bf16[2432,128]{1,0:T(8,128)(2,1)}, bf16[2432,128]{1,0:T(8,128)(2,1)S(1)}, u32[]{:S(2)}, u32[]{:S(2)}) collective-permute-start(bf16[2432,128]{1,0:T(8,128)(2,1)} %get-tuple-element.58), channel_id=1, source_target_pairs={{0,1},{1,0},{2,3},{3,2},{4,5},{5,4},{6,7},{7,6},{8,9},{9,8},{10,11... | collective-permute-start | bytes 1867784 | tf_op jit(solution)/shard_map/ppermute | solution.py:32
  119.0 4.6 %all-to-all-done.2 = bf16[32,40,128]{2,1,0:T(8,128)(2,1)S(1)} async-done(((bf16[32,40,128]{2,1,0:T(8,128)(2,1)}), bf16[32,40,128]{2,1,0:T(8,128)(2,1)S(1)}, u32[]{:S(2)}, u32[]{:S(2)}) %all-to-all-start.2) | async-done | bytes 327712 | tf_op jit(solution)/shard_map/all_to_all | solution.py:338
  123.6 4.3 %collective-permute-start.16 = (f32[40,128]{1,0:T(8,128)S(1)}, f32[40,128]{1,0:T(8,128)S(1)}, u32[]{:S(2)}, u32[]{:S(2)}) collective-permute-start(f32[40,128]{1,0:T(8,128)S(1)} %convert_reduce_fusion), channel_id=1, source_target_pairs={{0,1},{1,65},{256,129},{257,193},{2,3},{3,67},{258,131},{259,195},... | collective-permute-start | bytes 61448 | tf_op jit(solution)/shard_map/ppermute | solution.py:96
  127.9 4.8 %collective-permute-start.15 = (f32[40,128]{1,0:T(8,128)S(1)}, f32[40,128]{1,0:T(8,128)S(1)}, u32[]{:S(2)}, u32[]{:S(2)}) collective-permute-start(f32[40,128]{1,0:T(8,128)S(1)} %convert_reduce_fusion), channel_id=1, source_target_pairs={{0,0},{1,64},{256,128},{257,192},{2,2},{3,66},{258,130},{259,194},... | collective-permute-start | bytes 61448 | tf_op jit(solution)/shard_map/ppermute | solution.py:96
  132.7 1.2 collective-permute-done.16
  133.9 3.2 %collective-permute-done.15 = f32[40,128]{1,0:T(8,128)S(1)} collective-permute-done((f32[40,128]{1,0:T(8,128)S(1)}, f32[40,128]{1,0:T(8,128)S(1)}, u32[]{:S(2)}, u32[]{:S(2)}) %collective-permute-start.15) | collective-permute-done | bytes 20512 | tf_op jit(solution)/shard_map/ppermute | solution.py:96
  137.1 1.9 %collective-permute-start.18 = (f32[40,128]{1,0:T(8,128)S(1)}, f32[40,128]{1,0:T(8,128)S(1)}, u32[]{:S(2)}, u32[]{:S(2)}) collective-permute-start(f32[40,128]{1,0:T(8,128)S(1)} %add.112), channel_id=1, source_target_pairs={{0,256},{256,0},{1,257},{257,1},{2,258},{258,2},{3,259},{259,3},{4... | collective-permute-start | bytes 61448 | tf_op jit(solution)/shard_map/ppermute | solution.py:32
  139.0 1.1 shard_map.156
  140.2 0.6 fusion.17
  (70 shorter events, 2.7 us)
Async XLA Ops:
  0.6 42.5 %copy-start = (bf16[2432,128]{1,0:T(8,128)(2,1)S(1)}, bf16[2432,128]{1,0:T(8,128)(2,1)}, u32[]{:S(2)}) copy-start(bf16[2432,128]{1,0:T(8,128)(2,1)} %param.20) | copy-start | bytes 1867780
  0.6 1.0 copy-start.13
  20.2 15.9 %copy-start.14 = (f32[1,8,2432]{2,1,0:T(8,128)S(1)}, f32[1,8,2432]{2,1,0:T(8,128)}, u32[]{:S(2)}) copy-start(f32[1,8,2432]{2,1,0:T(8,128)} %param.21) | copy-start | bytes 233476
  20.2 19.1 %copy-start.11 = (s32[4]{0:T(128)S(1)}, s32[4]{0:T(128)}, u32[]{:S(2)}) copy-start(s32[4]{0:T(128)} %constant.117.clone) | copy-start | bytes 52
  21.2 18.7 %copy-start.12 = (bf16[1,128,2432]{2,1,0:T(8,128)(2,1)S(1)}, bf16[1,128,2432]{2,1,0:T(8,128)(2,1)}, u32[]{:S(2)}) copy-start(bf16[1,128,2432]{2,1,0:T(8,128)(2,1)} %param.14) | copy-start | bytes 1867780
  21.2 28.5 %all-to-all-start.1 = ((bf16[8,76,608]{2,1,0:T(8,128)(2,1)}), bf16[8,76,608]{2,1,0:T(8,128)(2,1)S(1)}, u32[]{:S(2)}, u32[]{:S(2)}) async-start(bf16[8,76,608]{2,1,0:T(8,128)(2,1)} %broadcast_in_dim.22), calls=%async_computation.1 | async-start | bytes 1638400 | tf_op jit(solution)/shard_map/all_to_all | solution.py:73
  28.2 15.8 %copy-start.1 = (bf16[2432,128]{1,0:T(8,128)(2,1)S(1)}, bf16[2432,128]{1,0:T(8,128)(2,1)}, u32[]{:S(2)}) copy-start(bf16[2432,128]{1,0:T(8,128)(2,1)} %param.19) | copy-start | bytes 1867780
  28.2 15.0 %collective-permute-start.1 = (bf16[128,2432]{1,0:T(8,128)(2,1)}, bf16[128,2432]{1,0:T(8,128)(2,1)S(1)}, u32[]{:S(2)}, u32[]{:S(2)}) collective-permute-start(bf16[128,2432]{1,0:T(8,128)(2,1)} %bitcast.own), channel_id=1, source_target_pairs={{0,256},{256,0},{1,257},{257,1},{2,258},{258,2},{3,259},{259,3},{4... | collective-permute-start | bytes 1867784 | tf_op jit(solution)/shard_map/ppermute | solution.py:32
  33.1 17.9 %collective-permute-start = (bf16[128,2432]{1,0:T(8,128)(2,1)}, bf16[128,2432]{1,0:T(8,128)(2,1)}, u32[]{:S(2)}, u32[]{:S(2)}) collective-permute-start(bf16[128,2432]{1,0:T(8,128)(2,1)} %bitcast.own), channel_id=1, source_target_pairs={{0,1},{1,0},{2,3},{3,2},{4,5},{5,4},{6,7},{7,6},{8,9},{9,8},{10,11... | collective-permute-start | bytes 1867784 | tf_op jit(solution)/shard_map/ppermute | solution.py:32
  36.2 13.8 %collective-permute-start.2 = (f32[2432]{0:T(1024)S(1)}, f32[2432]{0:T(1024)}, u32[]{:S(2)}, u32[]{:S(2)}) collective-permute-start(f32[2432]{0:T(1024)S(1)} %fusion.11), channel_id=1, source_target_pairs={{0,256},{256,0},{1,257},{257,1},{2,258},{258,2},{3,259},{259,3},{4... | collective-permute-start | bytes 29192 | tf_op jit(solution)/shard_map/ppermute | solution.py:32
  40.8 9.2 %collective-permute-start.3 = (bf16[128,1216]{1,0:T(8,128)(2,1)}, bf16[128,1216]{1,0:T(8,128)(2,1)}, u32[]{:S(2)}, u32[]{:S(2)}) collective-permute-start(bf16[128,1216]{1,0:T(8,128)(2,1)} %dynamic-slice_bitcast_fusion), channel_id=1, source_target_pairs={{0,256},{256,0},{1,257},{257,1},{2,258},{258,2},{3,259},{259,3},{4... | collective-permute-start | bytes 933896 | tf_op jit(solution)/shard_map/ppermute | solution.py:32
  43.1 0.8 copy-start.5
  44.0 1.1 copy-start.6
  47.4 0.7 copy-start.7
  48.1 0.6 copy-start.9
  50.9 33.0 %collective-permute-start.7 = (bf16[304,608]{1,0:T(8,128)(2,1)S(1)}, bf16[304,608]{1,0:T(8,128)(2,1)S(1)}, u32[]{:S(2)}, u32[]{:S(2)}) collective-permute-start(bf16[304,608]{1,0:T(8,128)(2,1)S(1)} %get-tuple-element.42.refs_0_), channel_id=1, source_target_pairs={{0,48},{2,50},{4,52},{6,54},{8,56},{10,58},{12,60},{14,62},{16,0},... | collective-permute-start | bytes 1109000 | tf_op jit(solution)/shard_map/ppermute | solution.py:82
  55.3 15.5 %collective-permute-start.5 = (bf16[304,608]{1,0:T(8,128)(2,1)S(1)}, bf16[304,608]{1,0:T(8,128)(2,1)S(1)}, u32[]{:S(2)}, u32[]{:S(2)}) collective-permute-start(bf16[304,608]{1,0:T(8,128)(2,1)S(1)} %get-tuple-element.42.refs_0_), channel_id=1, source_target_pairs={{0,16},{2,18},{4,20},{6,22},{8,24},{10,26},{12,28},{14,30},{16,32}... | collective-permute-start | bytes 1109000 | tf_op jit(solution)/shard_map/ppermute | solution.py:82
  57.3 15.5 %collective-permute-start.8 = (bf16[304,608]{1,0:T(8,128)(2,1)S(1)}, bf16[304,608]{1,0:T(8,128)(2,1)S(1)}, u32[]{:S(2)}, u32[]{:S(2)}) collective-permute-start(bf16[304,608]{1,0:T(8,128)(2,1)S(1)} %get-tuple-element.43.refs_1_), channel_id=1, source_target_pairs={{0,48},{2,50},{4,52},{6,54},{8,56},{10,58},{12,60},{14,62},{16,0},... | collective-permute-start | bytes 1109000 | tf_op jit(solution)/shard_map/ppermute | solution.py:82
  61.8 22.1 %collective-permute-start.6 = (bf16[304,608]{1,0:T(8,128)(2,1)S(1)}, bf16[304,608]{1,0:T(8,128)(2,1)S(1)}, u32[]{:S(2)}, u32[]{:S(2)}) collective-permute-start(bf16[304,608]{1,0:T(8,128)(2,1)S(1)} %get-tuple-element.43.refs_1_), channel_id=1, source_target_pairs={{0,16},{2,18},{4,20},{6,22},{8,24},{10,26},{12,28},{14,30},{16,32}... | collective-permute-start | bytes 1109000 | tf_op jit(solution)/shard_map/ppermute | solution.py:82
  63.8 14.0 %collective-permute-start.4 = (bf16[128,2432]{1,0:T(8,128)(2,1)}, bf16[128,2432]{1,0:T(8,128)(2,1)S(1)}, u32[]{:S(2)}, u32[]{:S(2)}) collective-permute-start(bf16[128,2432]{1,0:T(8,128)(2,1)} %collective-permute-done.own), channel_id=1, source_target_pairs={{0,256},{256,0},{1,257},{257,1},{2,258},{258,2},{3,259},{259,3},{4... | collective-permute-start | bytes 1867784 | tf_op jit(solution)/shard_map/ppermute | solution.py:32
  70.8 15.1 %collective-permute-start.9 = (bf16[304,608]{1,0:T(8,128)(2,1)S(1)}, bf16[304,608]{1,0:T(8,128)(2,1)S(1)}, u32[]{:S(2)}, u32[]{:S(2)}) collective-permute-start(bf16[304,608]{1,0:T(8,128)(2,1)S(1)} %collective-permute-done.5.refs_2_), channel_id=1, source_target_pairs={{0,16},{2,18},{4,20},{6,22},{8,24},{10,26},{12,28},{14,30},{16,32}... | collective-permute-start | bytes 1109000 | tf_op jit(solution)/shard_map/ppermute | solution.py:82
  72.7 13.2 %collective-permute-start.10 = (bf16[304,608]{1,0:T(8,128)(2,1)S(1)}, bf16[304,608]{1,0:T(8,128)(2,1)S(1)}, u32[]{:S(2)}, u32[]{:S(2)}) collective-permute-start(bf16[304,608]{1,0:T(8,128)(2,1)S(1)} %collective-permute-done.8.refs_5_), channel_id=1, source_target_pairs={{0,48},{2,50},{4,52},{6,54},{8,56},{10,58},{12,60},{14,62},{16,0},... | collective-permute-start | bytes 1109000 | tf_op jit(solution)/shard_map/ppermute | solution.py:82
  77.8 8.2 %collective-permute-start.11 = (bf16[128,608]{1,0:T(8,128)(2,1)S(1)}, bf16[128,608]{1,0:T(8,128)(2,1)S(1)}, u32[]{:S(2)}, u32[]{:S(2)}) collective-permute-start(bf16[128,608]{1,0:T(8,128)(2,1)S(1)} %fusion.7), channel_id=1, source_target_pairs={{0,1},{1,0},{2,3},{3,2},{4,5},{5,4},{6,7},{7,6},{8,9},{9,8},{10,11... | collective-permute-start | bytes 466952 | tf_op jit(solution)/shard_map/ppermute | solution.py:32
  84.0 2.0 %copy-start.10 = (bf16[256,128]{1,0:T(8,128)(2,1)S(1)}, bf16[256,128]{1,0:T(8,128)(2,1)}, u32[]{:S(2)}) copy-start(bf16[256,128]{1,0:T(8,128)(2,1)} %copy-done.9) | copy-start | bytes 196612
  87.4 4.3 %collective-permute-start.12 = (bf16[512,128]{1,0:T(8,128)(2,1)S(1)}, bf16[512,128]{1,0:T(8,128)(2,1)S(1)}, u32[]{:S(2)}, u32[]{:S(2)}) collective-permute-start(bf16[512,128]{1,0:T(8,128)(2,1)S(1)} %convert_element_type.65), channel_id=1, source_target_pairs={{0,256},{256,0},{1,257},{257,1},{2,258},{258,2},{3,259},{259,3},{4... | collective-permute-start | bytes 393224 | tf_op jit(solution)/shard_map/ppermute | solution.py:32
  91.9 7.2 %copy-start.4 = (bf16[768,608]{1,0:T(8,128)(2,1)S(1)}, bf16[768,608]{1,0:T(8,128)(2,1)}, u32[]{:S(2)}) copy-start(bf16[768,608]{1,0:T(8,128)(2,1)} %constant.118.clone.spread) | copy-start | bytes 2801668
  91.9 7.1 %copy-start.8 = (bf16[608,256]{1,0:T(8,128)(2,1)S(1)}, bf16[608,256]{1,0:T(8,128)(2,1)}, u32[]{:S(2)}) copy-start(bf16[608,256]{1,0:T(8,128)(2,1)} %copy-done.7) | copy-start | bytes 933892
  91.9 7.1 %collective-permute-start.13 = (bf16[512,128]{1,0:T(8,128)(2,1)S(1)}, bf16[512,128]{1,0:T(8,128)(2,1)S(1)}, u32[]{:S(2)}, u32[]{:S(2)}) collective-permute-start(bf16[512,128]{1,0:T(8,128)(2,1)S(1)} %get-tuple-element.61), channel_id=1, source_target_pairs={{0,1},{1,0},{2,3},{3,2},{4,5},{5,4},{6,7},{7,6},{8,9},{9,8},{10,11... | collective-permute-start | bytes 393224 | tf_op jit(solution)/shard_map/ppermute | solution.py:32
  100.7 11.5 %collective-permute-start.14 = (bf16[4,4,152,256]{3,2,1,0:T(8,128)(2,1)}, bf16[4,4,152,256]{3,2,1,0:T(8,128)(2,1)S(1)}, u32[]{:S(2)}, u32[]{:S(2)}) collective-permute-start(bf16[4,4,152,256]{3,2,1,0:T(8,128)(2,1)} %get-tuple-element.55), channel_id=1, source_target_pairs={{0,256},{256,0},{1,257},{257,1},{2,258},{258,2},{3,259},{259,3},{4... | collective-permute-start | bytes 3735560 | tf_op jit(solution)/shard_map/ppermute | solution.py:32
  103.5 20.1 %all-to-all-start.2 = ((bf16[32,40,128]{2,1,0:T(8,128)(2,1)}), bf16[32,40,128]{2,1,0:T(8,128)(2,1)S(1)}, u32[]{:S(2)}, u32[]{:S(2)}) async-start(bf16[32,40,128]{2,1,0:T(8,128)(2,1)} %shard_map.153), calls=%async_computation.2 | async-start | bytes 655360 | tf_op jit(solution)/shard_map/all_to_all | solution.py:338
  112.2 1.1 copy-start.2
  113.3 1.3 copy-start.3
  116.3 20.8 %collective-permute-start.17 = (bf16[2432,128]{1,0:T(8,128)(2,1)}, bf16[2432,128]{1,0:T(8,128)(2,1)S(1)}, u32[]{:S(2)}, u32[]{:S(2)}) collective-permute-start(bf16[2432,128]{1,0:T(8,128)(2,1)} %get-tuple-element.58), channel_id=1, source_target_pairs={{0,1},{1,0},{2,3},{3,2},{4,5},{5,4},{6,7},{7,6},{8,9},{9,8},{10,11... | collective-permute-start | bytes 1867784 | tf_op jit(solution)/shard_map/ppermute | solution.py:32
  123.6 10.3 %collective-permute-start.16 = (f32[40,128]{1,0:T(8,128)S(1)}, f32[40,128]{1,0:T(8,128)S(1)}, u32[]{:S(2)}, u32[]{:S(2)}) collective-permute-start(f32[40,128]{1,0:T(8,128)S(1)} %convert_reduce_fusion), channel_id=1, source_target_pairs={{0,1},{1,65},{256,129},{257,193},{2,3},{3,67},{258,131},{259,195},... | collective-permute-start | bytes 61448 | tf_op jit(solution)/shard_map/ppermute | solution.py:96
  127.9 9.2 %collective-permute-start.15 = (f32[40,128]{1,0:T(8,128)S(1)}, f32[40,128]{1,0:T(8,128)S(1)}, u32[]{:S(2)}, u32[]{:S(2)}) collective-permute-start(f32[40,128]{1,0:T(8,128)S(1)} %convert_reduce_fusion), channel_id=1, source_target_pairs={{0,0},{1,64},{256,128},{257,192},{2,2},{3,66},{258,130},{259,194},... | collective-permute-start | bytes 61448 | tf_op jit(solution)/shard_map/ppermute | solution.py:96
  137.1 3.1 %collective-permute-start.18 = (f32[40,128]{1,0:T(8,128)S(1)}, f32[40,128]{1,0:T(8,128)S(1)}, u32[]{:S(2)}, u32[]{:S(2)}) collective-permute-start(f32[40,128]{1,0:T(8,128)S(1)} %add.112), channel_id=1, source_target_pairs={{0,256},{256,0},{1,257},{257,1},{2,258},{258,2},{3,259},{259,3},{4... | collective-permute-start | bytes 61448 | tf_op jit(solution)/shard_map/ppermute | solution.py:32
